TPU v7x, 32 devices: a whole 2x2x4 slice. The times are simulated.
32 devices in a mesh: section: 2 (over x), rows: 16 (over z, y, core).
Axes of the slice: x: 2, y: 2, z: 4, core: 2. Of those that a mesh axis runs over, the one named last changes fastest.
Arguments:
- section_input: bfloat16 [2, 2, 2048, 512], P('section', None, 'rows'), may hold values from -6 to 6
- segments: int32 [2, 2, 16, 128], P(None, None, 'rows'), may hold values from 0 to 7, never falling along the last dimension, each value on 1 to 32 neighbouring positions
- cotangent: bfloat16 [2, 2048, 512], P(None, 'rows'), may hold values from -6 to 6
- encoder_inward: bfloat16 [512, 1536], replicated, may hold values from -0.25 to 0.25
- encoder_outward: bfloat16 [512, 512], replicated, may hold values from -0.75 to 0.75
- encoder_widen: bfloat16 [512, 2048], replicated, may hold values from -0.25 to 0.25
- encoder_narrow: bfloat16 [2048, 512], replicated, may hold values from -0.125 to 0.125
- encoder_gain: float32 [2, 512], replicated, may hold values from 0.25 to 1.75
- encoder_shift: float32 [2, 512], replicated, may hold values from -3 to 3
- decoder_inward: bfloat16 [512, 1536], replicated, may hold values from -0.25 to 0.25
- decoder_outward: bfloat16 [512, 512], replicated, may hold values from -0.75 to 0.75
- decoder_cross_query: bfloat16 [512, 512], replicated, may hold values from -0.25 to 0.25
- decoder_cross_memory: bfloat16 [512, 1024], replicated, may hold values from -0.25 to 0.25
- decoder_cross_outward: bfloat16 [512, 512], replicated, may hold values from -0.75 to 0.75
- decoder_widen: bfloat16 [512, 2048], replicated, may hold values from -0.25 to 0.25
- decoder_narrow: bfloat16 [2048, 512], replicated, may hold values from -0.125 to 0.125
- decoder_gain: float32 [3, 512], replicated, may hold values from 0.25 to 1.75
- decoder_shift: float32 [3, 512], replicated, may hold values from -3 to 3
Outputs:
- section_output: bfloat16 [2, 2, 2048, 512], P('section', None, 'rows')
- input_delta: bfloat16 [2, 2, 2048, 512], P('section', None, 'rows')
- encoder_inward_delta: float32 [512, 1536], P('rows', 'section')
- encoder_outward_delta: float32 [512, 512], P('rows', 'section')
- encoder_widen_delta: float32 [512, 2048], P('rows', 'section')
- encoder_narrow_delta: float32 [2048, 512], P('rows', 'section')
- encoder_gain_delta: float32 [2, 512], P(None, 'rows')
- encoder_shift_delta: float32 [2, 512], P(None, 'rows')
- decoder_inward_delta: float32 [512, 1536], P('rows', 'section')
- decoder_outward_delta: float32 [512, 512], P('rows', 'section')
- decoder_cross_query_delta: float32 [512, 512], P('rows', 'section')
- decoder_cross_memory_delta: float32 [512, 1024], P('rows', 'section')
- decoder_cross_outward_delta: float32 [512, 512], P('rows', 'section')
- decoder_widen_delta: float32 [512, 2048], P('rows', 'section')
- decoder_narrow_delta: float32 [2048, 512], P('rows', 'section')
- decoder_gain_delta: float32 [3, 512], P(None, 'rows')
- decoder_shift_delta: float32 [3, 512], P(None, 'rows')
Inputs may be any that keep to these rules, and one draw needn't show every extreme that they name: `segments`: in every row of 128 tokens the ids never fall, each id of 0 to 7 appears, and each covers at most 32 positions, one exactly that many.
All inputs are finite; a program needn't handle non-finite values.
Results may differ from a plain program's by a relative error of at most 0.02.
Values may be sent and summed in bfloat16 or wider, within the bound.
No kernel may reach another device: no remote copies, remote signals or barrier semaphores. Data moves between devices by JAX's collectives and lax.ppermute only.
A program may use at most 320 MiB of HBM per device.

v0:
```python
from functools import partial
import math

import jax
import jax.numpy as jnp
from jax import lax
from jax.sharding import PartitionSpec as P

HEADS = 8
HEAD_DIM = 64


NEG = -1e30
EPS = 1e-05


def from_behind(value, axis, steps):
    count = lax.axis_size(axis)
    initial, last = (max(0, -steps), min(count, count - steps))
    return lax.ppermute(value, axis, [(source, source + steps) for source in range(initial, last)])


def swapped(block, axis, apart):
    count = lax.axis_size(axis)
    route = []
    for low in range(count):
        high = low | 1 << apart
        if high != low and high < count:
            route += [(low, high), (high, low)]
    return lax.ppermute(block, axis, route)


def layer_norm(summed, gain, shift):
    center = jnp.mean(summed, -1, keepdims=True)
    centered = summed - center
    spread = jnp.mean(centered * centered, -1, keepdims=True)
    return centered * lax.rsqrt(spread + EPS) * gain + shift


def smooth(values):
    return jax.nn.gelu(values, approximate=True)


def matmul(left, right):
    return jnp.dot(left, right, preferred_element_type=jnp.float32)


def weight_grad(left, grad):
    return lax.dot_general(left, grad, (((0,), (0,)), ((), ())), preferred_element_type=jnp.float32)


def input_grad(grad, weight):
    return lax.dot_general(
        grad, weight, (((1,), (1,)), ((), ())), preferred_element_type=jnp.float32
    )


def split_heads(array):
    return array.reshape(array.shape[0], HEADS, array.shape[1] // HEADS)


def scores_of(query, keys, allowed):
    factor = 1.0 / math.sqrt(HEAD_DIM)
    raw_scores = jnp.einsum(
        "qhd,khd->hqk", split_heads(query), split_heads(keys), preferred_element_type=jnp.float32
    )
    return jnp.where(allowed[None], raw_scores * factor, NEG)


def attend_forward(query, keys, values, allowed):
    scores = scores_of(query, keys, allowed)
    peak = jnp.max(scores, -1, keepdims=True)
    weights = jnp.exp(scores - peak)
    totals = jnp.sum(weights, -1, keepdims=True)
    chances = (weights / totals).astype(jnp.bfloat16)
    mixed = jnp.einsum(
        "hqk,khd->qhd", chances, split_heads(values), preferred_element_type=jnp.float32
    )
    return (mixed.reshape(query.shape[0], -1).astype(jnp.bfloat16), peak + jnp.log(totals))


def attend_backward(query, keys, values, allowed, log_total, grad_mixed):
    factor = 1.0 / math.sqrt(HEAD_DIM)
    scores = scores_of(query, keys, allowed)
    chances = jnp.exp(scores - log_total)
    grad_heads = split_heads(grad_mixed)
    grad_chances = jnp.einsum(
        "qhd,khd->hqk", grad_heads, split_heads(values), preferred_element_type=jnp.float32
    )
    grad_values = jnp.einsum(
        "hqk,qhd->khd", chances.astype(jnp.bfloat16), grad_heads, preferred_element_type=jnp.float32
    )
    grad_scores = chances * (grad_chances - jnp.sum(chances * grad_chances, -1, keepdims=True))
    grad_scores = grad_scores.astype(jnp.bfloat16)
    grad_query = jnp.einsum(
        "hqk,khd->qhd", grad_scores, split_heads(keys), preferred_element_type=jnp.float32
    )
    grad_keys = jnp.einsum(
        "hqk,qhd->khd", grad_scores, split_heads(query), preferred_element_type=jnp.float32
    )
    rows_here = query.shape[0]
    keys_here = keys.shape[0]
    return (
        grad_query.reshape(rows_here, -1) * factor,
        grad_keys.reshape(keys_here, -1) * factor,
        grad_values.reshape(keys_here, -1),
    )


def self_forward(inputs, allowed, inward, outward):
    width = outward.shape[0]
    projected = matmul(inputs, inward).astype(jnp.bfloat16)
    mixed, log_total = attend_forward(
        projected[:, :width], projected[:, width : 2 * width], projected[:, 2 * width :], allowed
    )
    return (inputs.astype(jnp.float32) + matmul(mixed, outward), (projected, mixed, log_total))


def self_backward(inputs, allowed, inward, outward, kept, grad_sum):
    projected, mixed, log_total = kept
    width = outward.shape[0]
    grad_branch = grad_sum.astype(jnp.bfloat16)
    grad_outward = weight_grad(mixed, grad_branch)
    grad_mixed = input_grad(grad_branch, outward).astype(jnp.bfloat16)
    grad_query, grad_keys, grad_values = attend_backward(
        projected[:, :width],
        projected[:, width : 2 * width],
        projected[:, 2 * width :],
        allowed,
        log_total,
        grad_mixed,
    )
    grad_projected = jnp.concatenate([grad_query, grad_keys, grad_values], 1).astype(jnp.bfloat16)
    grad_inward = weight_grad(inputs, grad_projected)
    return (grad_sum + input_grad(grad_projected, inward), grad_inward, grad_outward)


def feed_forward(normed, widen, narrow):
    normed_low = normed.astype(jnp.bfloat16)
    hidden, smooth_back = jax.vjp(smooth, matmul(normed_low, widen))
    hidden_low = hidden.astype(jnp.bfloat16)
    return (normed + matmul(hidden_low, narrow), (normed_low, hidden_low, smooth_back))


def feed_backward(widen, narrow, kept, grad_sum):
    normed_low, hidden_low, smooth_back = kept
    grad_branch = grad_sum.astype(jnp.bfloat16)
    grad_narrow = weight_grad(hidden_low, grad_branch)
    (grad_before,) = smooth_back(input_grad(grad_branch, narrow))
    grad_before = grad_before.astype(jnp.bfloat16)
    grad_widen = weight_grad(normed_low, grad_before)
    return (grad_sum + input_grad(grad_before, widen), grad_widen, grad_narrow)


def encode(source, source_ids, encoder):
    inward, outward, widen, narrow, gains, shifts = encoder
    allowed = source_ids[:, None] == source_ids[None, :]
    summed, self_kept = self_forward(source, allowed, inward, outward)
    normed, first_back = jax.vjp(layer_norm, summed, gains[0], shifts[0])
    summed, feed_kept = feed_forward(normed, widen, narrow)
    result, second_back = jax.vjp(layer_norm, summed, gains[1], shifts[1])
    return (result.astype(jnp.bfloat16), (allowed, self_kept, first_back, feed_kept, second_back))


def encode_backward(source, source_ids, encoder, grad_memory):
    inward, outward, widen, narrow, gains, shifts = encoder
    unused_memory, kept = encode(source, source_ids, encoder)
    allowed, self_kept, first_back, feed_kept, second_back = kept
    grad_sum, gain_late, shift_late = second_back(grad_memory.astype(jnp.float32))
    grad_normed, grad_widen, grad_narrow = feed_backward(widen, narrow, feed_kept, grad_sum)
    grad_sum, gain_early, shift_early = first_back(grad_normed)
    grad_source, grad_inward, grad_outward = self_backward(
        source, allowed, inward, outward, self_kept, grad_sum
    )
    deltas = (
        grad_inward,
        grad_outward,
        grad_widen,
        grad_narrow,
        jnp.stack([gain_early, gain_late]),
        jnp.stack([shift_early, shift_late]),
    )
    return (grad_source.astype(jnp.bfloat16), deltas)


def decode(target, memory, source_ids, target_ids, decoder):
    inward, outward, cross_query, cross_memory, cross_outward, widen, narrow, gains, shifts = (
        decoder
    )
    places = jnp.arange(target.shape[0])
    causal = (target_ids[:, None] == target_ids[None, :]) & (places[:, None] >= places[None, :])
    across = target_ids[:, None] == source_ids[None, :]
    width = cross_outward.shape[0]
    summed, self_kept = self_forward(target, causal, inward, outward)
    normed, first_back = jax.vjp(layer_norm, summed, gains[0], shifts[0])
    normed_low = normed.astype(jnp.bfloat16)
    query = matmul(normed_low, cross_query).astype(jnp.bfloat16)
    paired = matmul(memory, cross_memory).astype(jnp.bfloat16)
    mixed, log_total = attend_forward(query, paired[:, :width], paired[:, width:], across)
    summed = normed + matmul(mixed, cross_outward)
    normed, second_back = jax.vjp(layer_norm, summed, gains[1], shifts[1])
    summed, feed_kept = feed_forward(normed, widen, narrow)
    result, third_back = jax.vjp(layer_norm, summed, gains[2], shifts[2])
    kept = (
        causal,
        across,
        self_kept,
        first_back,
        normed_low,
        query,
        paired,
        mixed,
        log_total,
        second_back,
        feed_kept,
        third_back,
    )
    return (result, kept)


def decoder_result(target, memory, source_ids, target_ids, decoder):
    return decode(target, memory, source_ids, target_ids, decoder)[0].astype(jnp.bfloat16)


def encoder_result(source, source_ids, encoder):
    return encode(source, source_ids, encoder)[0]


def decode_backward(target, memory, source_ids, target_ids, decoder, grad_output):
    inward, outward, cross_query, cross_memory, cross_outward, widen, narrow, gains, shifts = (
        decoder
    )
    unused_result, kept = decode(target, memory, source_ids, target_ids, decoder)
    (
        causal,
        across,
        self_kept,
        first_back,
        normed_low,
        query,
        paired,
        mixed,
        log_total,
        second_back,
        feed_kept,
        third_back,
    ) = kept
    width = cross_outward.shape[0]
    grad_sum, gain_last, shift_last = third_back(grad_output.astype(jnp.float32))
    grad_normed, grad_widen, grad_narrow = feed_backward(widen, narrow, feed_kept, grad_sum)
    grad_sum, gain_middle, shift_middle = second_back(grad_normed)
    grad_branch = grad_sum.astype(jnp.bfloat16)
    grad_cross_outward = weight_grad(mixed, grad_branch)
    grad_mixed = input_grad(grad_branch, cross_outward).astype(jnp.bfloat16)
    grad_query, grad_keys, grad_values = attend_backward(
        query, paired[:, :width], paired[:, width:], across, log_total, grad_mixed
    )
    grad_query = grad_query.astype(jnp.bfloat16)
    grad_paired = jnp.concatenate([grad_keys, grad_values], 1).astype(jnp.bfloat16)
    grad_cross_query = weight_grad(normed_low, grad_query)
    grad_cross_memory = weight_grad(memory, grad_paired)
    grad_memory = input_grad(grad_paired, cross_memory).astype(jnp.bfloat16)
    grad_normed = grad_sum + input_grad(grad_query, cross_query)
    grad_sum, gain_first, shift_first = first_back(grad_normed)
    grad_target, grad_inward, grad_outward = self_backward(
        target, causal, inward, outward, self_kept, grad_sum
    )
    deltas = (
        grad_inward,
        grad_outward,
        grad_cross_query,
        grad_cross_memory,
        grad_cross_outward,
        grad_widen,
        grad_narrow,
        jnp.stack([gain_first, gain_middle, gain_last]),
        jnp.stack([shift_first, shift_middle, shift_last]),
    )
    return (grad_target.astype(jnp.bfloat16), grad_memory, deltas)


def flatten(deltas, pieces, matrices):
    parts = [item.reshape(pieces, -1) for item in deltas[:matrices]]
    parts = parts + [item.T.reshape(pieces, -1) for item in deltas[matrices:]]
    return jnp.concatenate(parts, 1)


def unflatten(flat_row, templates, pieces, matrices):
    results = []
    offset = 0
    for place, shape in enumerate(templates):
        length = shape[0] * shape[1] // pieces
        piece = flat_row[offset : offset + length]
        offset = offset + length
        if place < matrices:
            results.append(piece.reshape(shape[0] // pieces, shape[1]))
        else:
            results.append(piece.reshape(shape[1] // pieces, shape[0]).T)
    return results


def column_halves(parts, matrices, side):
    results = []
    for place, item in enumerate(parts):
        if place < matrices:
            half_width = item.shape[1] // 2
            results.append(lax.dynamic_slice_in_dim(item, side * half_width, half_width, 1))
        else:
            results.append(item)
    return results


def packed_length(templates, pieces, matrices):
    total = 0
    for place, shape in enumerate(templates):
        if place < matrices:
            total = total + shape[0] // pieces * (shape[1] // 2)
        else:
            total = total + shape[0] * (shape[1] // pieces)
    return total


def pack_parts(parts, length):
    flat = jnp.concatenate([item.reshape(-1) for item in parts])
    return jnp.pad(flat, (0, length - flat.shape[0]))


def unpack_parts(flat, templates, pieces, matrices):
    results = []
    offset = 0
    for place, shape in enumerate(templates):
        if place < matrices:
            target_shape = (shape[0] // pieces, shape[1] // 2)
        else:
            target_shape = (shape[0], shape[1] // pieces)
        length = target_shape[0] * target_shape[1]
        results.append(flat[offset : offset + length].reshape(target_shape))
        offset = offset + length
    return results


def encoder_tick(source, source_ids, encoder, grad_memory, pieces, columns, blank):
    grad_source, deltas = encode_backward(source, source_ids, encoder, grad_memory)
    flat = flatten(deltas, pieces, 4)
    flat = jnp.pad(flat, ((0, 0), (0, columns - flat.shape[1])))
    return (grad_source, jnp.zeros_like(blank), flat)


def decoder_tick(target, memory, source_ids, target_ids, decoder, grad_output, pieces):
    grad_target, grad_memory, deltas = decode_backward(
        target, memory, source_ids, target_ids, decoder, grad_output
    )
    return (grad_target, grad_memory, flatten(deltas, pieces, 7))


def empty_tick(blank, columns, pieces):
    return (jnp.zeros_like(blank), jnp.zeros_like(blank), jnp.zeros((pieces, columns), jnp.float32))


def empty_result(blank):
    return jnp.zeros_like(blank)


def per_device(
    section_input,
    segments,
    cotangent,
    encoder_inward,
    encoder_outward,
    encoder_widen,
    encoder_narrow,
    encoder_gain,
    encoder_shift,
    decoder_inward,
    decoder_outward,
    decoder_cross_query,
    decoder_cross_memory,
    decoder_cross_outward,
    decoder_widen,
    decoder_narrow,
    decoder_gain,
    decoder_shift,
):
    encoder = (
        encoder_inward,
        encoder_outward,
        encoder_widen,
        encoder_narrow,
        encoder_gain,
        encoder_shift,
    )
    decoder = (
        decoder_inward,
        decoder_outward,
        decoder_cross_query,
        decoder_cross_memory,
        decoder_cross_outward,
        decoder_widen,
        decoder_narrow,
        decoder_gain,
        decoder_shift,
    )
    section = lax.axis_index("section")
    pieces = lax.axis_size("rows")
    micro = section_input.shape[1]
    source_ids = segments[0, :, 0]
    target_ids = segments[1, :, 0]
    blank = jnp.zeros(section_input.shape[2:], jnp.bfloat16)
    encoder_shapes = [item.shape for item in encoder]
    decoder_shapes = [item.shape for item in decoder]
    encoder_cols = sum((shape[0] * shape[1] for shape in encoder_shapes)) // pieces
    decoder_cols = sum((shape[0] * shape[1] for shape in decoder_shapes)) // pieces
    own = section_input[0]
    forward_ticks = [(tick if tick < micro else -1, tick - micro) for tick in range(2 * micro)]
    backward_ticks = [
        (2 * micro - 1 - tick if tick >= micro else -1, micro - 1 - tick if tick < micro else -1)
        for tick in range(2 * micro)
    ]
    memories = {}
    section_results = {}
    for first, second in forward_ticks:
        if first >= 0:
            run_first = partial(encoder_result, own[first], source_ids[first], encoder)
        else:
            run_first = partial(empty_result, blank)
        if second >= 0:
            run_second = partial(
                decoder_result,
                own[second],
                memories[second],
                source_ids[second],
                target_ids[second],
                decoder,
            )
        else:
            run_second = partial(empty_result, blank)
        produced = lax.cond(section == 0, run_first, run_second)
        if first >= 0:
            memories[first] = from_behind(produced, "section", 1)
            section_results[0, first] = produced
        if second >= 0:
            section_results[1, second] = produced
    returned = {}
    input_parts = {}
    summed_flat = jnp.zeros((pieces, decoder_cols), jnp.float32)
    for first, second in backward_ticks:
        if first >= 0:
            run_first = partial(
                encoder_tick,
                own[first],
                source_ids[first],
                encoder,
                returned[first],
                pieces,
                decoder_cols,
                blank,
            )
        else:
            run_first = partial(empty_tick, blank, decoder_cols, pieces)
        if second >= 0:
            run_second = partial(
                decoder_tick,
                own[second],
                memories[second],
                source_ids[second],
                target_ids[second],
                decoder,
                cotangent[second],
                pieces,
            )
        else:
            run_second = partial(empty_tick, blank, decoder_cols, pieces)
        grad_inputs, sent, flat = lax.cond(section == 0, run_first, run_second)
        summed_flat = summed_flat + flat
        if second >= 0:
            returned[second] = from_behind(sent, "section", -1)
            input_parts[1, second] = grad_inputs
        if first >= 0:
            input_parts[0, first] = grad_inputs
    results = jnp.stack(
        [
            jnp.where(
                section == 0, section_results[0, index_micro], section_results[1, index_micro]
            )
            for index_micro in range(micro)
        ]
    )[None]
    gradients = jnp.stack(
        [
            jnp.where(section == 0, input_parts[0, index_micro], input_parts[1, index_micro])
            for index_micro in range(micro)
        ]
    )[None]
    own_share = lax.psum_scatter(summed_flat, "rows", scatter_dimension=0, tiled=True)
    encoder_own = unflatten(own_share[0, :encoder_cols], encoder_shapes, pieces, 4)
    decoder_own = unflatten(own_share[0], decoder_shapes, pieces, 7)
    length = packed_length(decoder_shapes, pieces, 7)
    encoder_send = pack_parts(column_halves(encoder_own, 4, 1), length)
    decoder_send = pack_parts(column_halves(decoder_own, 7, 0), length)
    outgoing = jnp.where(section == 0, encoder_send, decoder_send)
    incoming = swapped(outgoing.astype(jnp.bfloat16), "section", 0).astype(outgoing.dtype)
    encoder_came = unpack_parts(incoming, encoder_shapes, pieces, 4)
    decoder_came = unpack_parts(incoming, decoder_shapes, pieces, 7)
    encoder_kept = column_halves(encoder_own, 4, 0)
    decoder_kept = column_halves(decoder_own, 7, 1)
    encoder_parts = [
        jnp.where(section == 0, kept, came) for kept, came in zip(encoder_kept, encoder_came)
    ]
    decoder_parts = [
        jnp.where(section == 0, came, kept) for kept, came in zip(decoder_kept, decoder_came)
    ]
    return (
        results,
        gradients,
        encoder_parts[0],
        encoder_parts[1],
        encoder_parts[2],
        encoder_parts[3],
        encoder_parts[4],
        encoder_parts[5],
        decoder_parts[0],
        decoder_parts[1],
        decoder_parts[2],
        decoder_parts[3],
        decoder_parts[4],
        decoder_parts[5],
        decoder_parts[6],
        decoder_parts[7],
        decoder_parts[8],
    )


def solution(mesh):
    placed = (
        P("section", None, "rows", None),
        P(None, None, "rows", None),
        P(None, "rows", None),
        P(),
        P(),
        P(),
        P(),
        P(),
        P(),
        P(),
        P(),
        P(),
        P(),
        P(),
        P(),
        P(),
        P(),
        P(),
    )
    return jax.shard_map(
        per_device,
        mesh=mesh,
        in_specs=placed,
        out_specs=(
            P("section", None, "rows", None),
            P("section", None, "rows", None),
            P("rows", "section"),
            P("rows", "section"),
            P("rows", "section"),
            P("rows", "section"),
            P(None, "rows"),
            P(None, "rows"),
            P("rows", "section"),
            P("rows", "section"),
            P("rows", "section"),
            P("rows", "section"),
            P("rows", "section"),
            P("rows", "section"),
            P("rows", "section"),
            P(None, "rows"),
            P(None, "rows"),
        ),
        check_vma=False,
    )
```

profile of v0, /device:TPU:0, one launch (start us, length us, event | category | flops | bytes accessed | tf_op | source)
XLA Modules:
  0.0 728.2 jit_solution(14679013183623717580)
XLA Ops:
  9.5 11.8 %conditional.10 = (bf16[128,512]{1,0:T(8,128)(2,1)}) conditional(s32[]{:T(128)} %convert_element_type.465, () %tuple.68, (bf16[128,512]{1,0:T(8,128)(2,1)S(1)}, bf16[512,1536]{1,0:T(8,128)(2,1)}, s32[1,128]{1,0:T(1,128)}, bf16[512,512]{1,0:T(8,128)(2,1)}, f32[2,512]{1,0:T(2,128)}, /*index=5*/f32[2,512]{1,0:T(2,128)}, bf16[512,2048]{1,0:T(8,128)(2,1)}, ...), branch_computations={%region_20.0_spmd, %region_21.28_spmd} | conditional | flops 861095424 | bytes 22799992 | solution.py:437
  23.3 21.4 %conditional.8 = (bf16[128,512]{1,0:T(8,128)(2,1)}) conditional(s32[]{:T(128)} %convert_element_type.465, () %tuple.64, (bf16[128,512]{1,0:T(8,128)(2,1)S(1)}, bf16[512,1536]{1,0:T(8,128)(2,1)}, s32[1,128]{1,0:T(1,128)}, bf16[512,512]{1,0:T(8,128)(2,1)}, f32[2,512]{1,0:T(2,128)}, /*index=5*/f32[2,512]{1,0:T(2,128)}, bf16[512,2048]{1,0:T(8,128)(2,1)}, ...), branch_computations={%region_0.0_spmd, %region_1.8_spmd} | conditional | flops 861095424 | bytes 21751416 | solution.py:437
  46.6 14.8 %conditional.14 = (bf16[128,512]{1,0:T(8,128)(2,1)}, bf16[128,512]{1,0:T(8,128)(2,1)}, f32[16,262336]{1,0:T(8,128)}) conditional(s32[]{:T(128)} %convert_element_type.465, (bf16[2,128,512]{2,1,0:T(8,128)(2,1)}, f32[3,512]{1,0:T(4,128)S(1)}, bf16[128,512]{1,0:T(8,128)(2,1)S(1)}, bf16[512,1536]{1,0:T(8,128)(2,1)}, s32[1,128]{1,0:T(1,128)}, ...), branch_computations={%region_83.108_spmd, %region_108.0_spmd} | conditional | flops 3449095680 | bytes 222904704 | solution.py:473
  55.4 6.0 broadcast.1041
  62.7 16.5 %conditional.12 = (bf16[128,512]{1,0:T(8,128)(2,1)}, bf16[128,512]{1,0:T(8,128)(2,1)}, f32[16,262336]{1,0:T(8,128)}) conditional(s32[]{:T(128)} %convert_element_type.465, (bf16[2,128,512]{2,1,0:T(8,128)(2,1)}, f32[3,512]{1,0:T(4,128)S(1)}, bf16[128,512]{1,0:T(8,128)(2,1)S(1)}, bf16[512,1536]{1,0:T(8,128)(2,1)}, s32[1,128]{1,0:T(1,128)}, ...), branch_computations={%region_40.65_spmd, %region_65.0_spmd} | conditional | flops 3449095680 | bytes 216586432 | solution.py:473
  73.2 6.0 broadcast.1015
  80.5 60.6 %collective-permute-done.3 = bf16[128,512]{1,0:T(8,128)(2,1)} collective-permute-done((bf16[128,512]{1,0:T(8,128)(2,1)}, bf16[128,512]{1,0:T(8,128)(2,1)}, u32[]{:S(2)}, u32[]{:S(2)}) %collective-permute-start.3) | collective-permute-done | bytes 131104 | tf_op jit(solution)/shard_map/ppermute | solution.py:20
  141.1 89.6 %conditional.15 = (bf16[128,512]{1,0:T(8,128)(2,1)}, f32[16,262336]{1,0:T(8,128)}) conditional(s32[]{:T(128)} %convert_element_type.465, () %tuple.76, (bf16[128,512]{1,0:T(8,128)(2,1)}, f32[2,512]{1,0:T(2,128)}, bf16[128,512]{1,0:T(8,128)(2,1)S(1)}, bf16[512,1536]{1,0:T(8,128)(2,1)}, s32[1,128]{1,0:T(1,128)}, ...), branch_computations={%region_109.0_spmd, %region_110.126_spmd} | conditional | flops 2536390400 | bytes 170783344 | solution.py:473
  188.8 4.0 fusion.340
  192.7 3.9 reshape.1468
  196.7 4.7 constant_dynamic-update-slice_fusion.19
  204.2 3.9 reshape.1469
  208.1 4.5 constant_dynamic-update-slice_fusion.18
  219.3 11.4 %pad.9 = f32[16,262336]{1,0:T(8,128)} pad(f32[16,196736]{1,0:T(8,128)} %dynamic-update-slice.29, f32[]{:T(128)} %constant.272.clone), padding=0_0x0_65600 | pad | bytes 29380612 | tf_op jit(solution)/shard_map/cond/branch_1_fun/jit(_pad)/pad | solution.py:345
  230.7 45.4 %collective-permute-done.2 = bf16[128,512]{1,0:T(8,128)(2,1)} collective-permute-done((bf16[128,512]{1,0:T(8,128)(2,1)}, bf16[128,512]{1,0:T(8,128)(2,1)}, u32[]{:S(2)}, u32[]{:S(2)}) %collective-permute-start.2) | collective-permute-done | bytes 131104 | tf_op jit(solution)/shard_map/ppermute | solution.py:20
  276.1 81.4 %conditional.13 = (bf16[128,512]{1,0:T(8,128)(2,1)}, f32[16,262336]{1,0:T(8,128)}) conditional(s32[]{:T(128)} %convert_element_type.465, () %tuple.72, (bf16[128,512]{1,0:T(8,128)(2,1)}, f32[2,512]{1,0:T(2,128)}, bf16[128,512]{1,0:T(8,128)(2,1)S(1)}, bf16[512,1536]{1,0:T(8,128)(2,1)}, s32[1,128]{1,0:T(1,128)}, ...), branch_computations={%region_66.0_spmd, %region_67.83_spmd} | conditional | flops 2536390400 | bytes 176028400 | solution.py:473
  322.6 3.9 reshape.1428
  326.6 4.7 constant_dynamic-update-slice_fusion.8
  338.0 4.5 constant_dynamic-update-slice_fusion.7
  345.9 11.4 %pad.8 = f32[16,262336]{1,0:T(8,128)} pad(f32[16,196736]{1,0:T(8,128)} %dynamic-update-slice.14, f32[]{:T(128)} %constant.242.clone), padding=0_0x0_65600 | pad | bytes 29380612 | tf_op jit(solution)/shard_map/cond/branch_1_fun/jit(_pad)/pad | solution.py:345
  357.5 27.6 %add_add_fusion.10 = f32[16,262336]{1,0:T(8,128)} fusion(f32[16,262336]{1,0:T(8,128)} %get-tuple-element.316, f32[16,262336]{1,0:T(8,128)} %get-tuple-element.315, f32[16,262336]{1,0:T(8,128)} %get-tuple-element.313, f32[16,262336]{1,0:T(8,128)} %get-tuple-element.314), kind=kLoop, calls=%fused_computation.630 | loop fusion | flops 12592128 | bytes 83947520 | tf_op jit(solution)/shard_map/add | solution.py:474
  391.1 293.0 %all-reduce.6.cloned.1.call-done = f32[16,262336]{1,0:T(8,128)} async-done(((f32[16,262336]{1,0:T(8,128)}), f32[16,262336]{1,0:T(8,128)}) %all-reduce.6.cloned.1.call-update) | async-done | bytes 16789520
  692.5 6.5 dynamic-slice_reduce_fusion.1
  708.0 5.3 collective-permute-done.4
  (447 shorter events, 188.6 us)
Async XLA Ops:
  7.2 676.9 %all-reduce.6.cloned.1.call-start = ((), (), s32[]{:S(2)}) async-start(), calls=%async_computation | async-start | bytes 33587200
  21.4 25.2 %collective-permute-start.1 = (bf16[128,512]{1,0:T(8,128)(2,1)}, bf16[128,512]{1,0:T(8,128)(2,1)}, u32[]{:S(2)}, u32[]{:S(2)}) collective-permute-start(bf16[128,512]{1,0:T(8,128)(2,1)} %get-tuple-element.643), channel_id=1, source_target_pairs={{0,16},{1,17},{2,18},{3,19},{4,20},{5,21},{6,22},{7,23},{8,24},{9,... | collective-permute-start | bytes 393224 | tf_op jit(solution)/shard_map/ppermute | solution.py:20
  23.3 23.3 %copy-start = (bf16[512,1024]{1,0:T(8,128)(2,1)S(1)}, bf16[512,1024]{1,0:T(8,128)(2,1)}, u32[]{:S(2)}) copy-start(bf16[512,1024]{1,0:T(8,128)(2,1)} %param.46) | copy-start | bytes 3145732
  23.3 23.3 %copy-start.126 = (f32[3,512]{1,0:T(4,128)S(1)}, f32[3,512]{1,0:T(4,128)}, u32[]{:S(2)}) copy-start(f32[3,512]{1,0:T(4,128)} %param.50) | copy-start | bytes 18436
  25.9 11.7 %copy-start.128 = (f32[2,512]{1,0:T(2,128)S(1)}, f32[2,512]{1,0:T(2,128)}, u32[]{:S(2)}) copy-start(f32[2,512]{1,0:T(2,128)} %get-tuple-element.196) | copy-start | bytes 12292 | tf_op jit(solution)/shard_map/cond
  25.9 11.7 %copy-start.149 = (f32[2,512]{1,0:T(2,128)S(1)}, f32[2,512]{1,0:T(2,128)}, u32[]{:S(2)}) copy-start(f32[2,512]{1,0:T(2,128)} %get-tuple-element.197) | copy-start | bytes 12292 | tf_op jit(solution)/shard_map/cond
  25.9 12.6 %copy-start.3 = (bf16[512,2048]{1,0:T(8,128)(2,1)S(1)}, bf16[512,2048]{1,0:T(8,128)(2,1)}, u32[]{:S(2)}) copy-start(bf16[512,2048]{1,0:T(8,128)(2,1)} %get-tuple-element.198) | copy-start | bytes 6291460 | tf_op jit(solution)/shard_map/cond
  44.7 18.0 %collective-permute-start = (bf16[128,512]{1,0:T(8,128)(2,1)}, bf16[128,512]{1,0:T(8,128)(2,1)}, u32[]{:S(2)}, u32[]{:S(2)}) collective-permute-start(bf16[128,512]{1,0:T(8,128)(2,1)} %get-tuple-element.641), channel_id=1, source_target_pairs={{0,16},{1,17},{2,18},{3,19},{4,20},{5,21},{6,22},{7,23},{8,24},{9,... | collective-permute-start | bytes 393224 | tf_op jit(solution)/shard_map/ppermute | solution.py:20
  61.4 79.7 %collective-permute-start.3 = (bf16[128,512]{1,0:T(8,128)(2,1)}, bf16[128,512]{1,0:T(8,128)(2,1)}, u32[]{:S(2)}, u32[]{:S(2)}) collective-permute-start(bf16[128,512]{1,0:T(8,128)(2,1)} %get-tuple-element.310), channel_id=1, source_target_pairs={{16,0},{17,1},{18,2},{19,3},{20,4},{21,5},{22,6},{23,7},{24,8},{25... | collective-permute-start | bytes 393224 | tf_op jit(solution)/shard_map/ppermute | solution.py:20
  62.7 78.4 %copy-start.1 = (bf16[512,2048]{1,0:T(8,128)(2,1)S(1)}, bf16[512,2048]{1,0:T(8,128)(2,1)}, u32[]{:S(2)}) copy-start(bf16[512,2048]{1,0:T(8,128)(2,1)} %param.39) | copy-start | bytes 6291460
  79.2 196.9 %collective-permute-start.2 = (bf16[128,512]{1,0:T(8,128)(2,1)}, bf16[128,512]{1,0:T(8,128)(2,1)}, u32[]{:S(2)}, u32[]{:S(2)}) collective-permute-start(bf16[128,512]{1,0:T(8,128)(2,1)} %get-tuple-element.307), channel_id=1, source_target_pairs={{16,0},{17,1},{18,2},{19,3},{20,4},{21,5},{22,6},{23,7},{24,8},{25... | collective-permute-start | bytes 393224 | tf_op jit(solution)/shard_map/ppermute | solution.py:20
  142.9 8.9 %copy-start.129 = (f32[2,512]{1,0:T(2,128)S(1)}, f32[2,512]{1,0:T(2,128)}, u32[]{:S(2)}) copy-start(f32[2,512]{1,0:T(2,128)} %get-tuple-element.272) | copy-start | bytes 12292 | tf_op jit(solution)/shard_map/cond
  151.5 7.8 %copy-start.42 = (f32[128,512]{1,0:T(8,128)}, f32[128,512]{1,0:T(8,128)S(1)}, u32[]{:S(2)}) copy-start(f32[128,512]{1,0:T(8,128)S(1)} %get-tuple-element.579) | copy-start | bytes 786436 | tf_op jit(solution)/shard_map/cond
  151.5 7.8 %copy-start.186 = (f32[128]{0:T(128)}, f32[128]{0:T(128)S(1)}, u32[]{:S(2)}) copy-start(f32[128]{0:T(128)S(1)} %broadcast_multiply_fusion.19) | copy-start | bytes 1540 | tf_op jit(solution)/shard_map/cond
  151.8 7.5 %copy-start.214 = (f32[128]{0:T(128)}, f32[128]{0:T(128)S(1)}, u32[]{:S(2)}) copy-start(f32[128]{0:T(128)S(1)} %fusion.333) | copy-start | bytes 1540 | tf_op jit(solution)/shard_map/cond
  208.1 7.8 %copy-start.198 = (f32[512]{0:T(512)S(1)}, f32[512]{0:T(512)}, u32[]{:S(2)}) copy-start(f32[512]{0:T(512)} %get-tuple-element.395) | copy-start | bytes 6148 | tf_op jit(solution)/shard_map/cond
  208.1 7.8 %copy-start.206 = (f32[512]{0:T(512)S(1)}, f32[512]{0:T(512)}, u32[]{:S(2)}) copy-start(f32[512]{0:T(512)} %get-tuple-element.394) | copy-start | bytes 6148 | tf_op jit(solution)/shard_map/cond
  278.0 8.2 %copy-start.130 = (f32[2,512]{1,0:T(2,128)S(1)}, f32[2,512]{1,0:T(2,128)}, u32[]{:S(2)}) copy-start(f32[2,512]{1,0:T(2,128)} %get-tuple-element.249) | copy-start | bytes 12292 | tf_op jit(solution)/shard_map/cond
  286.0 7.8 %copy-start.43 = (f32[128,512]{1,0:T(8,128)}, f32[128,512]{1,0:T(8,128)S(1)}, u32[]{:S(2)}) copy-start(f32[128,512]{1,0:T(8,128)S(1)} %get-tuple-element.535) | copy-start | bytes 786436 | tf_op jit(solution)/shard_map/cond
  286.0 7.8 %copy-start.188 = (f32[128]{0:T(128)}, f32[128]{0:T(128)S(1)}, u32[]{:S(2)}) copy-start(f32[128]{0:T(128)S(1)} %broadcast_multiply_fusion.14) | copy-start | bytes 1540 | tf_op jit(solution)/shard_map/cond
  286.2 7.6 %copy-start.216 = (f32[128]{0:T(128)}, f32[128]{0:T(128)S(1)}, u32[]{:S(2)}) copy-start(f32[128]{0:T(128)S(1)} %fusion.253) | copy-start | bytes 1540 | tf_op jit(solution)/shard_map/cond
  293.8 7.6 %copy-start.8 = (bf16[512,1536]{1,0:T(8,128)(2,1)S(1)}, bf16[512,1536]{1,0:T(8,128)(2,1)}, u32[]{:S(2)}) copy-start(bf16[512,1536]{1,0:T(8,128)(2,1)} %get-tuple-element.251) | copy-start | bytes 4718596 | tf_op jit(solution)/shard_map/cond
  692.5 13.8 %copy-start.125 = (bf16[128,512]{1,0:T(8,128)(2,1)S(1)}, bf16[128,512]{1,0:T(8,128)(2,1)}, u32[]{:S(2)}) copy-start(bf16[128,512]{1,0:T(8,128)(2,1)} %get-tuple-element.309) | copy-start | bytes 393220
  704.8 8.4 %collective-permute-start.4 = (bf16[131264]{0:T(1024)(128)(2,1)S(1)}, bf16[131264]{0:T(1024)(128)(2,1)S(1)}, u32[]{:S(2)}, u32[]{:S(2)}) collective-permute-start(bf16[131264]{0:T(1024)(128)(2,1)S(1)} %select_convert_fusion), channel_id=1, source_target_pairs={{0,16},{16,0},{1,17},{17,1},{2,18},{18,2},{3,19},{19,3},{4,20},{20... | collective-permute-start | bytes 787592 | tf_op jit(solution)/shard_map/ppermute | solution.py:30
  (76 other events, 282.7 us)
Sparse Core Ops, SparseCore 0:
  385.2 298.9 all-reduce.5
where the time goes:
time: 736 us; the launch traced here: 728 us
  waiting for transfers between devices  404 us (55%)
  local copies, waits for them, and re-layouts  163 us (22%)
  matrix products  65.8 us (9%)
  other arithmetic  54 us (7%)
  loops' own time  18.6 us (3%)
  between operations  14.8 us (2%)
  starting transfers between devices  7.99 us (1%)
    unnamed x2, waiting for transfers between devices  293 us
    ppermute x4, waiting for transfers between devices, from_behind(): lax.ppermute(value, axis, [(source, source + steps) for source in range(i...  106 us
    cond x182, local copies, waits for them, and re-layouts  36.9 us
    add x1, other arithmetic, per_device(): summed_flat = summed_flat + flat  27.6 us
    reshape x8, local copies, waits for them, and re-layouts, flatten(): parts = [item.reshape(pieces, -1) for item in deltas[:matrices]]  26.1 us
    pad x2, local copies, waits for them, and re-layouts, encoder_tick(): flat = jnp.pad(flat, ((0, 0), (0, columns - flat.shape[1])))  22.8 us
    dot_general x8, matrix products, weight_grad(): lax.dot_general(left, grad, (((0,), (0,)), ((), ())), preferred_element_t...  18.7 us
    another operation x4, loops' own time, per_device(): grad_inputs, sent, flat = lax.cond(section == 0, run_first, run_second)  18.1 us
  transfers between devices with their start and end apart: 6, of which 4 were waited for; matrix products, arithmetic and copies ran while one was open for 18% of the time, Pallas kernels for 0%

commit v1 on v0

v1 whole, which is shorter than its diff:
```python
from functools import partial
import math

import jax
import jax.numpy as jnp
from jax import lax
from jax.experimental import pallas as pl
from jax.experimental.pallas import tpu as pltpu
from jax.sharding import PartitionSpec as P

HEADS = 8
HEAD_DIM = 64
NEG = -1e30
EPS = 1e-05
GROUPS = 16
SLAB = 256
LANES = 128
PER_SLAB = SLAB // HEAD_DIM
BF = jnp.bfloat16
F32 = jnp.float32
FACTOR = 1.0 / math.sqrt(HEAD_DIM)
VMEM_LIMIT = 56 * 1024 * 1024
ANY = pl.BlockSpec(memory_space=pl.ANY)


def matmul(left, right):
    return lax.dot_general(left, right, (((1,), (0,)), ((), ())), preferred_element_type=F32)


def matmul_back(grad, weight):
    return lax.dot_general(grad, weight, (((1,), (1,)), ((), ())), preferred_element_type=F32)


def matmul_across(left, grad):
    return lax.dot_general(left, grad, (((0,), (0,)), ((), ())), preferred_element_type=F32)


def norm(summed, gain, shift):
    center = jnp.mean(summed, -1, keepdims=True)
    centered = summed - center
    spread = jnp.mean(centered * centered, -1, keepdims=True)
    scale = lax.rsqrt(spread + EPS)
    unit = centered * scale
    return unit * gain + shift, unit, scale


def norm_back(grad, unit, scale, gain):
    grad_gain = jnp.sum(grad * unit, 0, keepdims=True)
    grad_shift = jnp.sum(grad, 0, keepdims=True)
    inner = grad * gain
    center = jnp.mean(inner, -1, keepdims=True)
    along = jnp.mean(inner * unit, -1, keepdims=True)
    return scale * (inner - center - unit * along), grad_gain, grad_shift


def gelu_both(before):
    root = math.sqrt(2.0 / math.pi)
    square = before * before
    bent = jnp.tanh(root * before * (1.0 + 0.044715 * square))
    half = 0.5 * (1.0 + bent)
    slope = half + 0.5 * before * (1.0 - bent * bent) * (root * (1.0 + 3 * 0.044715 * square))
    return before * half, slope


def head_marks(dtype):
    lane = lax.broadcasted_iota(jnp.int32, (1, SLAB), 1) // HEAD_DIM
    return [(lane == h).astype(F32).astype(dtype) for h in range(PER_SLAB)]


def spread_heads(slab, marks):
    return jnp.concatenate([slab * mark for mark in marks], 0)


def gather_heads(stacked, rows):
    lane = lax.broadcasted_iota(jnp.int32, (1, SLAB), 1) // HEAD_DIM
    total = stacked[:rows]
    for h in range(1, PER_SLAB):
        total = jnp.where(lane == h, stacked[h * rows : (h + 1) * rows], total)
    return total


def attend(query, keys, values, allowed, chances_ref):
    rows = query.shape[0]
    marks = head_marks(BF)
    wide = jnp.concatenate([allowed] * PER_SLAB, 0)
    mixed = []
    for slab in range(query.shape[1] // SLAB):
        at = slice(slab * SLAB, (slab + 1) * SLAB)
        scores = matmul_back(spread_heads(query[:, at], marks), keys[:, at]) * FACTOR
        scores = jnp.where(wide, scores, NEG)
        weights = jnp.exp(scores - jnp.max(scores, -1, keepdims=True))
        chances = weights * (1.0 / jnp.sum(weights, -1, keepdims=True))
        chances_ref[slab] = chances
        mixed.append(gather_heads(matmul(chances.astype(BF), values[:, at]), rows).astype(BF))
    return jnp.concatenate(mixed, 1)


def attend_back(query, keys, values, chances_ref, grad_mixed):
    rows = query.shape[0]
    marks = head_marks(BF)
    grad_query, grad_keys, grad_values = [], [], []
    for slab in range(query.shape[1] // SLAB):
        at = slice(slab * SLAB, (slab + 1) * SLAB)
        chances = chances_ref[slab]
        spread_grad = spread_heads(grad_mixed[:, at], marks)
        grad_chances = matmul_back(spread_grad, values[:, at])
        grad_values.append(matmul_across(chances.astype(BF), spread_grad).astype(BF))
        held = jnp.sum(chances * grad_chances, -1, keepdims=True)
        grad_scores = (chances * (grad_chances - held)).astype(BF)
        grad_query.append((gather_heads(matmul(grad_scores, keys[:, at]), rows) * FACTOR).astype(BF))
        spread_query = spread_heads(query[:, at], marks)
        grad_keys.append((matmul_across(grad_scores, spread_query) * FACTOR).astype(BF))
    return [jnp.concatenate(item, 1) for item in (grad_query, grad_keys, grad_values)]


def tiles_of(array):
    return [array[:, at : at + LANES] for at in range(0, array.shape[1], LANES)]


class Room:
    def __init__(self, sources, targets, held_in, held_out, sem_in, sem_out):
        self.sources, self.targets = sources, targets
        self.held_in, self.held_out = held_in, held_out
        self.sem_in, self.sem_out = sem_in, sem_out
        self.arrived, self.sent = set(), []
        self.names_in, self.names_out = list(sources), list(targets)

    def copy_in(self, name, source=None):
        place = self.names_in.index(name)
        source = self.sources[name] if source is None else source
        return pltpu.make_async_copy(source, self.held_in[name], self.sem_in.at[place])

    def fetch(self, names):
        for name in names:
            self.copy_in(name).start()

    def get(self, name):
        if name not in self.arrived:
            source = self.sources[name]
            if source.shape != self.held_in[name].shape:
                source = source.at[0]
            self.copy_in(name, source).wait()
            self.arrived.add(name)
        return self.held_in[name]

    def put(self, name, value=None):
        if value is not None:
            self.held_out[name][...] = value
        place = self.names_out.index(name)
        copy = pltpu.make_async_copy(
            self.held_out[name], self.targets[name], self.sem_out.at[place]
        )
        copy.start()
        self.sent.append(copy)

    def finish(self):
        for copy in self.sent:
            copy.wait()


class Packet:
    def __init__(self, weights, extra=0):
        self.weights = dict(weights)
        self.left_at, self.grad_at = {}, {}
        left = grad = 0
        for name, (depth, width) in self.weights.items():
            self.left_at[name], self.grad_at[name] = left, grad
            left, grad = left + depth // 2, grad + width
        self.left, self.extra_at, self.grad = left, grad, grad + extra
        self.rows = {}
        top = 0
        for name, (depth, width) in self.weights.items():
            self.rows[name] = top
            top += depth // GROUPS * width // (2 * SLAB)
        self.small_at = top
        self.height = top + (16 if extra else 0)

    def shapes(self):
        return {
            "keep": jax.ShapeDtypeStruct((self.left, LANES), BF),
            "send": jax.ShapeDtypeStruct((self.left + self.grad, LANES), BF),
        }

    def scratch(self):
        return {
            "left": jax.ShapeDtypeStruct((2, self.left, LANES), BF),
            "grad": jax.ShapeDtypeStruct((self.grad, LANES), BF),
        }

    def stash(self, refs, name, left, grad):
        depth, width = self.weights[name]
        block = depth // GROUPS
        across = left.T
        for group in range(GROUPS):
            top = self.left_at[name] + group // 2 * block
            refs["left"][group % 2, top : top + block] = across[group * block : (group + 1) * block]
        for place, tile in enumerate(tiles_of(grad)):
            top = self.grad_at[name] + place * LANES
            refs["grad"][top : top + LANES] = tile

    def ship(self, refs, targets, sems, core):
        copies = [
            pltpu.make_async_copy(refs["left"].at[core], targets["keep"], sems.at[0]),
            pltpu.make_async_copy(
                refs["left"].at[1 - core], targets["send"].at[pl.ds(0, self.left)], sems.at[1]
            ),
            pltpu.make_async_copy(
                refs["grad"], targets["send"].at[pl.ds(self.left, self.grad)], sems.at[2]
            ),
        ]
        for copy in copies:
            copy.start()
        return copies


def call(body, inputs, outputs, scalars, flops, packets=None, single=(), extra=None):
    packets, extra = packets or {}, extra or {}
    outputs = dict(outputs)
    names_in, names_out = list(inputs), list(outputs)
    ways = [(name, way) for name in packets for way in ("keep", "send")]
    shapes_out = [outputs[name] for name in names_out]
    shapes_out += [packets[name].shapes()[way] for name, way in ways]
    stashes = [(name, part) for name in packets for part in ("left", "grad")]

    def kernel(*refs):
        refs = list(refs)
        scalar_ref = refs.pop(0)
        sources = {name: refs.pop(0) for name in names_in}
        targets = {name: refs.pop(0) for name in names_out}
        leaving = {key: refs.pop(0) for key in ways}
        held_in = {name: refs.pop(0) for name in names_in}
        held_out = {name: refs.pop(0) for name in names_out}
        stashed = {key: refs.pop(0) for key in stashes}
        held_out.update({name: refs.pop(0) for name in extra})
        sem_in, sem_out, sem_packet = refs
        room = Room(sources, targets, held_in, held_out, sem_in, sem_out)

        def stash(packet, name, left, grad):
            refs_here = {part: stashed[packet, part] for part in ("left", "grad")}
            packets[packet].stash(refs_here, name, left, grad)

        def ship(packet):
            refs_here = {part: stashed[packet, part] for part in ("left", "grad")}
            targets_here = {way: leaving[packet, way] for way in ("keep", "send")}
            sems = sem_packet.at[list(packets).index(packet)]
            room.sent += packets[packet].ship(refs_here, targets_here, sems, scalar_ref[1])

        room.stash, room.ship, room.stashed = stash, ship, stashed
        body(room, scalar_ref)
        room.finish()

    moved = sum(item.size * item.dtype.itemsize for item in list(inputs.values()) + shapes_out)
    results = pl.pallas_call(
        kernel,
        out_shape=shapes_out,
        in_specs=[pl.BlockSpec(memory_space=pltpu.SMEM)] + [ANY] * len(names_in),
        out_specs=[ANY] * len(shapes_out),
        scratch_shapes=[
            pltpu.VMEM(inputs[name].shape[name in single :], inputs[name].dtype) for name in names_in
        ]
        + [pltpu.VMEM(outputs[name].shape, outputs[name].dtype) for name in names_out]
        + [
            pltpu.VMEM(packets[name].scratch()[part].shape, BF) for name, part in stashes
        ]
        + [pltpu.VMEM(item.shape, item.dtype) for item in extra.values()]
        + [
            pltpu.SemaphoreType.DMA((len(names_in),)),
            pltpu.SemaphoreType.DMA((max(1, len(names_out)),)),
            pltpu.SemaphoreType.DMA((max(1, len(packets)), 3)),
        ],
        compiler_params=pltpu.CompilerParams(vmem_limit_bytes=VMEM_LIMIT),
        cost_estimate=pl.CostEstimate(flops=flops, bytes_accessed=moved, transcendentals=0),
    )(scalars, *inputs.values())
    rest = dict(zip(ways, results[len(names_out) :]))
    return dict(zip(names_out, results)), {
        name: (rest[name, "keep"], rest[name, "send"]) for name in packets
    }


def weight_grads(packet, names, keep, send, came, scalars, small=False):
    tops, height = {}, 0
    for name in names:
        depth, width = packet.weights[name]
        tops[name] = height
        height += depth // GROUPS * width // (2 * SLAB)
    small_at = height
    height += 16 if small else 0
    half = jax.ShapeDtypeStruct((GROUPS // 2, height, SLAB), BF)

    def kernel(scalar, keep_in, send_in, came_in, kept_out, sent_out, keep_ref, grad_ref, came_ref, packed, sems, sems_out):
        first = pltpu.make_async_copy(keep_in, keep_ref, sems.at[0])
        second = pltpu.make_async_copy(
            send_in.at[pl.ds(packet.left, packet.grad)], grad_ref, sems.at[1]
        )
        third = pltpu.make_async_copy(came_in, came_ref, sems.at[2])
        for copy in (first, second, third):
            copy.start()
        for copy in (first, second, third):
            copy.wait()
        core, mine = scalar[1], scalar[2]

        def place(side, block):
            spot = side * scalar[3]
            for bit in range(3):
                spot = spot + (block >> bit & 1) * scalar[4 + bit]
            return spot

        sent = []

        def ship(top, rows, which):
            for way, target in ((mine, kept_out), (1 - mine, sent_out)):
                copy = pltpu.make_async_copy(
                    packed.at[pl.ds(way * (GROUPS // 2), GROUPS // 2), pl.ds(top, rows)],
                    target.at[:, pl.ds(top, rows)],
                    sems_out.at[which, len(sent) % 2],
                )
                copy.start()
                sent.append(copy)

        for which, name in enumerate(names):
            depth, width = packet.weights[name]
            block, half_pieces = depth // GROUPS, width // (2 * SLAB)
            left_at, grad_at = packet.left_at[name], packet.grad_at[name]
            left = jnp.concatenate(
                [ref[left_at : left_at + depth // 2] for ref in (keep_ref, came_ref)], 1
            )
            for piece in range(width // SLAB):
                at = grad_at + piece * SLAB
                right = jnp.concatenate(
                    [
                        jnp.concatenate(
                            [ref[base + at + i * LANES : base + at + (i + 1) * LANES] for i in (0, 1)], 1
                        )
                        for ref, base in ((grad_ref, 0), (came_ref, packet.left))
                    ],
                    0,
                )
                tile = matmul(left, right).astype(BF)
                side, offset = divmod(piece, half_pieces)
                top = tops[name] + offset * block
                for number in range(GROUPS // 2):
                    packed[place(side, number), top : top + block] = tile[
                        number * block : (number + 1) * block
                    ]
            ship(tops[name], block * half_pieces, which)
        if small:
            at = packet.extra_at
            total = sum(
                jnp.concatenate(
                    [ref[base + at + 16 * i : base + at + 16 * (i + 1)].astype(F32) for i in range(4)], 1
                )
                for ref, base in ((grad_ref, 0), (came_ref, packet.left))
            )
            share = total.shape[1] // GROUPS
            for number in range(GROUPS // 2):
                turned = [
                    pltpu.roll(total, (total.shape[1] - (2 * number + i) * share) % total.shape[1], 1)
                    for i in (0, 1)
                ]
                part = jnp.where(core == 0, turned[0], turned[1])[:, :SLAB].astype(BF)
                for side in (0, 1):
                    packed[place(side, number), small_at : small_at + 16] = part
            ship(small_at, 16, len(names))
        for copy in sent:
            copy.wait()

    flops = sum(2 * 2 * LANES * packet.weights[name][0] * packet.weights[name][1] // 2 for name in names)
    return pl.pallas_call(
        kernel,
        out_shape=[half, half],
        in_specs=[pl.BlockSpec(memory_space=pltpu.SMEM)] + [ANY] * 3,
        out_specs=[ANY] * 2,
        scratch_shapes=[
            pltpu.VMEM(keep.shape, BF),
            pltpu.VMEM((packet.grad, LANES), BF),
            pltpu.VMEM(came.shape, BF),
            pltpu.VMEM((GROUPS, height, SLAB), BF),
            pltpu.SemaphoreType.DMA((3,)),
            pltpu.SemaphoreType.DMA((len(names) + 1, 2)),
        ],
        compiler_params=pltpu.CompilerParams(vmem_limit_bytes=VMEM_LIMIT),
        cost_estimate=pl.CostEstimate(
            flops=flops, bytes_accessed=4 * half.size + 6 * came.size, transcendentals=0
        ),
    )(scalars, keep, send, came)


def equal_ids(row_ids, column_ids):
    length = row_ids.shape[1]
    down = jnp.broadcast_to(row_ids.astype(F32), (length, length)).T
    return down == jnp.broadcast_to(column_ids.astype(F32), (length, length))


def scale_out(scale):
    return jnp.broadcast_to(scale, (scale.shape[0], 128))


def make_forward(width):
    def body(room, scalar):
        section = scalar[0]
        get, put, held = room.get, room.put, room.held_out
        start_forward(room, section)
        source_ids = get("segments")[0, pl.ds(section, 1), 0, :]
        target_ids = room.held_in["segments"][1, pl.ds(section, 1), 0, :]

        source = get("source")[...]
        gains, shifts = get("encoder_gain"), get("encoder_shift")
        put("e_projected", matmul(source, get("encoder_inward")[...]).astype(BF))
        projected = held["e_projected"]
        mixed = attend(
            projected[:, :width],
            projected[:, width : 2 * width],
            projected[:, 2 * width :],
            equal_ids(source_ids, source_ids),
            held["e_chances"],
        )
        put("e_chances")
        put("e_mixed", mixed)
        summed = source.astype(F32) + matmul(mixed, get("encoder_outward")[...])
        first, unit, scale = norm(summed, gains[0:1], shifts[0:1])
        put("e_unit0", unit)
        put("e_scale0", scale_out(scale))
        low = first.astype(BF)
        put("e_low", low)
        widen_forward(low, get("encoder_widen"), held["e_hidden"], held["e_slope"])
        put("e_hidden")
        put("e_slope")
        summed = first + matmul(held["e_hidden"][...], get("encoder_narrow")[...])
        result, unit, scale = norm(summed, gains[1:2], shifts[1:2])
        put("e_unit1", unit)
        put("e_scale1", scale_out(scale))
        memory = result.astype(BF)
        put("memory", memory)

        target = get("target")[...]
        gains, shifts = get("decoder_gain"), get("decoder_shift")
        put("d_projected", matmul(target, get("decoder_inward")[...]).astype(BF))
        projected = held["d_projected"]
        length = target.shape[0]
        rows = lax.broadcasted_iota(jnp.int32, (length, length), 0)
        columns = lax.broadcasted_iota(jnp.int32, (length, length), 1)
        mixed = attend(
            projected[:, :width],
            projected[:, width : 2 * width],
            projected[:, 2 * width :],
            equal_ids(target_ids, target_ids) & (rows >= columns),
            held["d_chances"],
        )
        put("d_chances")
        put("d_mixed", mixed)
        summed = target.astype(F32) + matmul(mixed, get("decoder_outward")[...])
        first, unit, scale = norm(summed, gains[0:1], shifts[0:1])
        put("d_unit0", unit)
        put("d_scale0", scale_out(scale))
        low = first.astype(BF)
        put("d_low", low)

        query = matmul(low, get("decoder_cross_query")[...]).astype(BF)
        put("c_query", query)
        put("c_paired", matmul(memory, get("decoder_cross_memory")[...]).astype(BF))
        paired = held["c_paired"]
        mixed = attend(
            query,
            paired[:, :width],
            paired[:, width:],
            equal_ids(target_ids, source_ids),
            held["c_chances"],
        )
        put("c_chances")
        put("c_mixed", mixed)
        summed = first + matmul(mixed, get("decoder_cross_outward")[...])
        second, unit1, scale1 = norm(summed, gains[1:2], shifts[1:2])
        put("d_unit1", unit1)
        put("d_scale1", scale_out(scale1))

        low = second.astype(BF)
        hidden_ref, slope_ref = room.held_out["d_hidden"], room.held_out["d_slope"]
        widen_forward(low, get("decoder_widen"), hidden_ref, slope_ref)
        summed = second + matmul(hidden_ref[...], get("decoder_narrow")[...])
        result, unit, scale = norm(summed, gains[2:3], shifts[2:3])
        put("output", result.astype(BF))

        grad_sum, grad_gain, grad_shift = norm_back(
            get("cotangent")[...].astype(F32), unit, scale, gains[2:3]
        )
        grad_low = grad_sum.astype(BF)
        room.stash("d_wide", "decoder_narrow", hidden_ref[...], grad_low)
        grad_before = widen_backward(grad_low, room.held_in["decoder_narrow"], slope_ref)
        room.stash("d_wide", "decoder_widen", low, grad_before)
        room.ship("d_wide")
        put("d_grad", grad_sum + matmul_back(grad_before, room.held_in["decoder_widen"][...]))
        put("d_small2", jnp.concatenate([grad_gain, grad_shift], 0))

    return body


def start_forward(room, section):
    room.copy_in("segments").start()

    @pl.when(section == 0)
    def _():
        room.copy_in("source", room.sources["source"].at[0]).start()
        room.copy_in("target").start()

    @pl.when(section != 0)
    def _():
        room.copy_in("source", room.sources["target"]).start()
        room.copy_in("target", room.sources["source"].at[1]).start()

    room.copy_in("cotangent", room.sources["cotangent"].at[section]).start()
    room.fetch(
        name
        for name in room.names_in
        if name not in ("segments", "source", "target", "cotangent")
    )


def widen_forward(low, widen_ref, hidden_ref, slope_ref):
    step = 512
    for at in range(0, widen_ref.shape[1], step):
        hidden, slope = gelu_both(matmul(low, widen_ref[:, at : at + step]))
        hidden_ref[:, at : at + step] = hidden.astype(BF)
        slope_ref[:, at : at + step] = slope


def widen_backward(grad_low, narrow_ref, slope_ref):
    step = 512
    parts = []
    for at in range(0, narrow_ref.shape[0], step):
        grad_hidden = matmul_back(grad_low, narrow_ref[at : at + step])
        parts.append((grad_hidden * slope_ref[:, at : at + step]).astype(BF))
    return jnp.concatenate(parts, 1)


def make_decoder_back(width):
    def body(room, scalar):
        get, put = room.get, room.put
        room.fetch(room.names_in)
        gains = get("decoder_gain")
        grad_sum, gain1, shift1 = norm_back(
            get("d_grad")[...], get("d_unit1")[...], get("d_scale1")[:, :1], gains[1:2]
        )
        grad_low = grad_sum.astype(BF)
        grad_mixed = matmul_back(grad_low, get("decoder_cross_outward")[...]).astype(BF)
        paired = get("c_paired")
        grad_query, grad_keys, grad_values = attend_back(
            get("c_query")[...], paired[:, :width], paired[:, width:], get("c_chances"), grad_mixed
        )
        grad_paired = jnp.concatenate([grad_keys, grad_values], 1)
        put(
            "grad_memory", matmul_back(grad_paired, get("decoder_cross_memory")[...]).astype(BF)
        )
        room.stash("d_rest", "decoder_cross_query", get("d_low")[...], grad_query)
        room.stash("d_rest", "decoder_cross_memory", get("memory")[...], grad_paired)
        room.stash("d_rest", "decoder_cross_outward", get("c_mixed")[...], grad_low)
        grad_normed = grad_sum + matmul_back(grad_query, get("decoder_cross_query")[...])
        grad_sum, gain0, shift0 = norm_back(
            grad_normed, get("d_unit0")[...], get("d_scale0")[:, :1], gains[0:1]
        )
        put("d_small01", jnp.concatenate([gain0, gain1, shift0, shift1], 0))
        grad_inputs = self_backward(room, "d", "decoder", "target", "d_rest", grad_sum, width)
        room.ship("d_rest")
        put("grad_inputs", grad_inputs.astype(BF))

    return body


def self_backward(room, short, layer, inputs, packet, grad_sum, width):
    get = room.get
    grad_low = grad_sum.astype(BF)
    grad_mixed = matmul_back(grad_low, get(layer + "_outward")[...]).astype(BF)
    projected = get(short + "_projected")
    grad_projected = jnp.concatenate(
        attend_back(
            projected[:, :width],
            projected[:, width : 2 * width],
            projected[:, 2 * width :],
            get(short + "_chances"),
            grad_mixed,
        ),
        1,
    )
    room.stash(packet, layer + "_inward", get(inputs)[...], grad_projected)
    room.stash(packet, layer + "_outward", get(short + "_mixed")[...], grad_low)
    return grad_sum + matmul_back(grad_projected, get(layer + "_inward")[...])


def make_encoder_back(width, packet):
    def body(room, scalar):
        get, put = room.get, room.put
        room.fetch(room.names_in)
        gains = get("encoder_gain")
        grad_sum, gain1, shift1 = norm_back(
            get("grad_memory")[...].astype(F32),
            get("e_unit1")[...],
            get("e_scale1")[:, :1],
            gains[1:2],
        )
        grad_low = grad_sum.astype(BF)
        room.stash("e_all", "encoder_narrow", get("e_hidden")[...], grad_low)
        grad_before = widen_backward(grad_low, get("encoder_narrow"), get("e_slope"))
        room.stash("e_all", "encoder_widen", get("e_low")[...], grad_before)
        grad_normed = grad_sum + matmul_back(grad_before, get("encoder_widen")[...])
        grad_sum, gain0, shift0 = norm_back(
            grad_normed, get("e_unit0")[...], get("e_scale0")[:, :1], gains[0:1]
        )
        inner, outer = get("d_small01")[...], get("d_small2")[...]
        small = jnp.concatenate(
            [gain0, gain1, shift0, shift1, inner[0:2], outer[0:1], inner[2:4], outer[1:2]]
            + [jnp.zeros((6, width), F32)],
            0,
        )
        for place, tile in enumerate(tiles_of(small.astype(BF))):
            top = packet.extra_at + 16 * place
            room.stashed["e_all", "grad"][top : top + 16] = tile
        grad_inputs = self_backward(room, "e", "encoder", "source", "e_all", grad_sum, width)
        room.ship("e_all")
        put("grad_inputs", grad_inputs.astype(BF))

    return body


def pair_swap(value, axis, apart):
    count = lax.axis_size(axis)
    return lax.ppermute(value, axis, [(i, i ^ apart) for i in range(count)])


def bit_of(step, section, row):
    return section if step == "section" else (row >> step) & 1


def reduce_group(kept, sent, orders, section, row):
    pieces = lax.axis_size("rows")
    for turn, pair in enumerate(zip(*orders)):
        route = []
        for device in range(2 * pieces):
            step = pair[device & 1]
            route.append((device, device ^ (pieces if step == "section" else 1 << step)))
        came = lax.ppermute(sent, ("section", "rows"), route)
        if turn == len(orders[0]) - 1:
            return kept[0].astype(F32) + came[0].astype(F32)
        following = [order[turn + 1] for order in orders]
        mine = jnp.where(
            row & 1 == 0, bit_of(following[0], section, row), bit_of(following[1], section, row)
        )
        kept, sent = halve(kept, came, mine)


def halve(kept, came, mine):
    count = kept.shape[0] // 2

    def half(which):
        one = lax.dynamic_slice_in_dim(kept, which * count, count, 0).astype(F32)
        two = lax.dynamic_slice_in_dim(came, which * count, count, 0).astype(F32)
        return (one + two).astype(BF)

    return half(mine), half(1 - mine)


def place_scalars(orders, section, row):
    core = row & 1

    def pick(values):
        return jnp.where(core == 0, values[0], values[1])

    mine = pick([bit_of(order[0], section, row) for order in orders])
    spots = [pick([8 >> order.index(step) for order in orders]) for step in STEPS]
    return jnp.stack([section, core, mine] + spots).astype(jnp.int32)


def spread_out(halves, core, top, count, share):
    both = jnp.stack(halves)[:, :, top : top + count * share].astype(F32)
    both = both.reshape(2, 2, 2, 2, count, share, SLAB)
    both = both.transpose(0, 3, 2, 1, 5, 4, 6).reshape(2, GROUPS // 2, 1, share, count * SLAB)
    held = jnp.concatenate([both * (core == 0), both * (core == 1)], 2)
    return held.reshape(2, GROUPS, share, count * SLAB)


ENCODER = ("inward", "outward", "widen", "narrow")
DECODER = ("inward", "outward", "cross_query", "cross_memory", "cross_outward", "widen", "narrow")
STEPS = ("section", 1, 2, 3)
CROSSED = (("section", 1, 2, 3), (1, "section", 2, 3))
UPWARD = ((2, 3, "section", 1), (2, 3, 1, "section"))
TEAMS = {
    "d_wide": ("d_wide", ("decoder_narrow", "decoder_widen"), False, CROSSED),
    "d_cross": (
        "d_rest",
        ("decoder_cross_query", "decoder_cross_memory", "decoder_cross_outward"),
        False,
        CROSSED,
    ),
    "d_self": ("d_rest", ("decoder_inward", "decoder_outward"), False, CROSSED),
    "e_wide": ("e_all", ("encoder_narrow", "encoder_widen"), False, CROSSED),
    "e_self": ("e_all", ("encoder_inward", "encoder_outward"), True, UPWARD),
}
PACKETS = {
    "d_wide": ("decoder_narrow", "decoder_widen"),
    "d_rest": (
        "decoder_cross_query",
        "decoder_cross_memory",
        "decoder_cross_outward",
        "decoder_inward",
        "decoder_outward",
    ),
    "e_all": ("encoder_narrow", "encoder_widen", "encoder_inward", "encoder_outward"),
}


def per_device(*arguments):
    names = ["section_input", "segments", "cotangent"]
    for layer, matrices in (("encoder", ENCODER), ("decoder", DECODER)):
        names += [f"{layer}_{short}" for short in matrices + ("gain", "shift")]
    given = dict(zip(names, arguments))
    section = lax.axis_index("section")
    row = lax.axis_index("rows")
    pieces = lax.axis_size("rows")
    core = row & 1
    even = pieces == GROUPS
    orders = {name: team[3] if even else CROSSED[:1] * 2 for name, team in TEAMS.items()}
    spots = {
        pair: place_scalars(pair, section if even else 0 * section, row if even else core)
        for pair in set(orders.values())
    }
    scalars = jnp.stack([section, core]).astype(jnp.int32)
    own = given["section_input"][0]
    length, width = own.shape[1:]
    wide = given["encoder_widen"].shape[1]
    other = pair_swap(
        lax.dynamic_index_in_dim(own, 1 - section, 0, keepdims=False), "section", 1
    )

    def low(*shape):
        return jax.ShapeDtypeStruct(shape, BF)

    def full(*shape):
        return jax.ShapeDtypeStruct(shape, F32)

    chances = full(width // SLAB, PER_SLAB * length, length)
    slabs = low(length, width)
    units = full(length, width)
    scales = full(length, 128)
    product = 2 * length * width * width

    def weights(layer, *short):
        return {f"{layer}_{name}": given[f"{layer}_{name}"] for name in short}

    forward_in = {
        "segments": given["segments"],
        "source": own,
        "target": other,
        **weights("encoder", "gain", "shift", "inward", "outward", "widen", "narrow"),
        **weights("decoder", "gain", "shift", "inward", "outward"),
        **weights("decoder", "cross_query", "cross_memory", "cross_outward", "widen", "narrow"),
        "cotangent": given["cotangent"],
    }
    forward_out = {
        "memory": slabs,
        "output": slabs,
        "e_projected": low(length, 3 * width),
        "e_chances": chances,
        "e_mixed": slabs,
        "e_unit0": units,
        "e_scale0": scales,
        "e_low": slabs,
        "e_hidden": low(length, wide),
        "e_slope": full(length, wide),
        "e_unit1": units,
        "e_scale1": scales,
        "d_projected": low(length, 3 * width),
        "d_chances": chances,
        "d_mixed": slabs,
        "d_unit0": units,
        "d_scale0": scales,
        "d_low": slabs,
        "c_query": slabs,
        "c_paired": low(length, 2 * width),
        "c_chances": chances,
        "c_mixed": slabs,
        "d_unit1": units,
        "d_scale1": scales,
        "d_grad": units,
        "d_small2": full(2, width),
    }
    packets = {
        name: Packet([(item, given[item].shape) for item in items], 64 if name == "e_all" else 0)
        for name, items in PACKETS.items()
    }
    parcels = {}

    def send_parcels(made):
        for name, (keep, sent) in made.items():
            parcels[name] = (keep, sent, pair_swap(sent, "rows", 1))

    kept, made = call(
        make_forward(width),
        forward_in,
        forward_out,
        scalars,
        36 * product,
        {"d_wide": packets["d_wide"]},
        ("source", "cotangent"),
        {"d_hidden": low(length, wide), "d_slope": full(length, wide)},
    )
    send_parcels(made)

    def pick(*keys):
        return {key: kept[key] for key in keys}

    source = jnp.where(section == 0, own[0], other)
    target = jnp.where(section == 0, other, own[1])
    back_in = {
        **weights("decoder", "gain"),
        **pick("d_grad", "d_unit1", "d_scale1"),
        **weights("decoder", "cross_outward"),
        **pick("c_query", "c_paired", "c_chances"),
        **weights("decoder", "cross_memory"),
        **pick("d_low", "memory", "c_mixed"),
        **weights("decoder", "cross_query"),
        **pick("d_unit0", "d_scale0"),
        **weights("decoder", "outward"),
        **pick("d_projected", "d_chances"),
        "target": target,
        **pick("d_mixed"),
        **weights("decoder", "inward"),
    }
    back_out = {
        "grad_memory": slabs,
        "d_small01": full(4, width),
        "grad_inputs": slabs,
    }
    decoded, made = call(
        make_decoder_back(width),
        back_in,
        back_out,
        scalars,
        10 * product,
        {"d_rest": packets["d_rest"]},
    )
    send_parcels(made)

    back_in = {
        **weights("encoder", "gain"),
        "grad_memory": decoded["grad_memory"],
        **pick("e_unit1", "e_scale1", "e_hidden"),
        **weights("encoder", "narrow"),
        **pick("e_slope", "e_low"),
        **weights("encoder", "widen"),
        **pick("e_unit0", "e_scale0"),
        "d_small01": decoded["d_small01"],
        **pick("d_small2"),
        **weights("encoder", "outward"),
        **pick("e_projected", "e_chances"),
        "source": source,
        **pick("e_mixed"),
        **weights("encoder", "inward"),
    }
    ended, made = call(
        make_encoder_back(width, packets["e_all"]),
        back_in,
        {"grad_inputs": slabs},
        scalars,
        13 * product,
        {"e_all": packets["e_all"]},
    )
    send_parcels(made)

    halves = {}
    for name, (packet, items, small, unused) in TEAMS.items():
        halves[name] = weight_grads(
            packets[packet], items, *parcels[packet], spots[orders[name]], small
        )

    def sides(source_side, target_side):
        mine = jnp.where(section == 0, source_side, target_side)
        theirs = pair_swap(
            jnp.where(section == 0, target_side, source_side), "section", 1
        )
        return jnp.stack(
            [jnp.where(section == 0, mine, theirs), jnp.where(section == 0, theirs, mine)]
        )[None]

    results = sides(kept["memory"], kept["output"])
    gradients = sides(ended["grad_inputs"], decoded["grad_inputs"])

    deltas, small = {}, None
    for name, (packet, items, with_small, unused) in TEAMS.items():
        if even:
            block = reduce_group(*halves[name], orders[name], section, row)
        top = 0
        for item in items:
            depth, columns = given[item].shape
            count = columns // (2 * SLAB)
            share = depth // GROUPS
            if even:
                parts = [block[top + i * share : top + (i + 1) * share] for i in range(count)]
                deltas[item] = jnp.concatenate(parts, 1)
            else:
                whole = spread_out(halves[name], core, top, count, share)
                deltas[item] = whole.reshape(2, depth, columns // 2)
            top += count * share
        if with_small and even:
            small = block[top : top + 10, : width // pieces]
        elif with_small:
            small = spread_out(halves[name], core, top, 1, 16)[0, :, :10, : width // GROUPS]
            small = lax.psum(jnp.moveaxis(small, 1, 0).reshape(10, width), ("section", "rows"))
            small = lax.dynamic_slice_in_dim(small, row * (width // pieces), width // pieces, 1)
    if not even:
        for item, part in deltas.items():
            part = lax.psum_scatter(part, "rows", scatter_dimension=1, tiled=True)
            deltas[item] = lax.psum_scatter(part, "section", scatter_dimension=0, tiled=True)[0]

    return (
        results,
        gradients,
        deltas["encoder_inward"],
        deltas["encoder_outward"],
        deltas["encoder_widen"],
        deltas["encoder_narrow"],
        small[0:2],
        small[2:4],
        deltas["decoder_inward"],
        deltas["decoder_outward"],
        deltas["decoder_cross_query"],
        deltas["decoder_cross_memory"],
        deltas["decoder_cross_outward"],
        deltas["decoder_widen"],
        deltas["decoder_narrow"],
        small[4:7],
        small[7:10],
    )


def solution(mesh):
    weights = (P(),) * 15
    shares = P("rows", "section")
    small = P(None, "rows")
    sides = P("section", None, "rows", None)
    return jax.shard_map(
        per_device,
        mesh=mesh,
        in_specs=(sides, P(None, None, "rows", None), P(None, "rows", None)) + weights,
        out_specs=(sides, sides)
        + (shares,) * 4
        + (small,) * 2
        + (shares,) * 7
        + (small,) * 2,
        check_vma=False,
    )
```

time: 736 us -> 140 us (0.19); the launches traced: 728 us -> 140 us
  waiting for transfers between devices: 404 us -> 39.7 us
  local copies, waits for them, and re-layouts: 163 us -> 8.81 us
  matrix products: 65.8 us -> 0 us
  Pallas kernels: 0 us -> 50 us
  other arithmetic: 54 us -> 8.88 us
  starting transfers between devices: 7.99 us -> 31.6 us
  loops' own time: 18.6 us -> 0 us
  between operations: 14.8 us -> 0.96 us
    unnamed x2 -> x0, waiting for transfers between devices: 293 us -> none
    ppermute x5 -> x26, waiting for transfers between devices: 111 us -> 39.7 us  [the longest x20 36.8 us: reduce_group(): came = lax.ppermute(sent, ('section', 'rows'), route)]
    dot_general x46 -> x0, matrix products: 63.5 us -> none  [the longest x8 18.7 us: weight_grad(): lax.dot_general(left, grad, (((0,), (0,)), ((), ())), preferred_element_t...]
    pallas_call x0 -> x8, Pallas kernels: none -> 50 us  [the longest x3 29.3 us: call(): pl.pallas_call(kernel, out_shape=shapes_out, in_specs=[pl.BlockSpec(memor...]
    cond x182 -> x0, local copies, waits for them, and re-layouts: 36.9 us -> none
    slice x44 -> x9, local copies, waits for them, and re-layouts: 35.8 us -> 4.39 us  [the longest x7 3.23 us: per_device(): parts = [block[top + i * share:top + (i + 1) * share] for i in range(count)]]
    reshape x40 -> x0, local copies, waits for them, and re-layouts: 30 us -> none  [the longest x8 26.1 us: flatten(): parts = [item.reshape(pieces, -1) for item in deltas[:matrices]]]
    add x3 -> x5, other arithmetic: 29.1 us -> 0.17 us  [reduce_group(): return kept[0].astype(F32) + came[0].astype(F32)]
  transfers between devices with their start and end apart: 6 -> 26, of which waited for: 4 -> 11; matrix products, arithmetic and copies ran while one was open for 18% -> 8% of each run, Pallas kernels for 0% -> 21%
where the time goes in v1:
time: 140 us
  Pallas kernels  50 us (36%)
  waiting for transfers between devices  39.7 us (28%)
  starting transfers between devices  31.6 us (23%)
  other arithmetic  8.88 us (6%)
  local copies, waits for them, and re-layouts  8.81 us (6%)
    ppermute x20, waiting for transfers between devices, reduce_group(): came = lax.ppermute(sent, ('section', 'rows'), route)  36.8 us
    pallas_call x3, Pallas kernels, call(): pl.pallas_call(kernel, out_shape=shapes_out, in_specs=[pl.BlockSpec(memor...  29.3 us
    ppermute x20, starting transfers between devices, reduce_group(): came = lax.ppermute(sent, ('section', 'rows'), route)  24.8 us
    pallas_call x5, Pallas kernels, weight_grads(): pl.pallas_call(kernel, out_shape=[half, half], in_specs=[pl.BlockSpec(mem...  20.7 us
    ppermute x6, starting transfers between devices, pair_swap(): return lax.ppermute(value, axis, [(i, i ^ apart) for i in range(count)])  6.77 us
    concatenate x5, other arithmetic, per_device(): deltas[item] = jnp.concatenate(parts, 1)  3.26 us
    slice x7, local copies, waits for them, and re-layouts, per_device(): parts = [block[top + i * share:top + (i + 1) * share] for i in range(count)]  3.23 us
    ppermute x6, waiting for transfers between devices, pair_swap(): return lax.ppermute(value, axis, [(i, i ^ apart) for i in range(count)])  2.92 us
  transfers between devices with their start and end apart: 26, of which 11 were waited for; matrix products, arithmetic and copies ran while one was open for 8% of the time, Pallas kernels for 21%

profile of v1, /device:TPU:0, one launch (start us, length us, event | category | flops | bytes accessed | tf_op | source)
XLA Modules:
  0.0 140.0 jit_solution(11123348387341336213)
XLA Ops:
  1.6 3.0 %collective-permute-start = (bf16[128,512]{1,0:T(8,128)(2,1)S(1)}, bf16[128,512]{1,0:T(8,128)(2,1)S(1)}, u32[]{:S(2)}, u32[]{:S(2)}) collective-permute-start(bf16[128,512]{1,0:T(8,128)(2,1)S(1)} %dynamic-slice_bitcast_fusion), channel_id=1, source_target_pairs={{0,16},{16,0},{1,17},{17,1},{2,18},{18,2},{3,19},{19,3},{4,20},{20... | collective-permute-start | bytes 393224 | tf_op jit(solution)/shard_map/ppermute | solution.py:625
  5.2 2.9 %collective-permute-done.refs_3_ = bf16[128,512]{1,0:T(8,128)(2,1)S(1)} collective-permute-done((bf16[128,512]{1,0:T(8,128)(2,1)S(1)}, bf16[128,512]{1,0:T(8,128)(2,1)S(1)}, u32[]{:S(2)}, u32[]{:S(2)}) %collective-permute-start) | collective-permute-done | bytes 131104 | tf_op jit(solution)/shard_map/ppermute | solution.py:625
  9.8 13.4 %shard_map.305 = (bf16[128,512]{1,0:T(8,128)(2,1)}, bf16[128,512]{1,0:T(8,128)(2,1)}, bf16[128,1536]{1,0:T(8,128)(2,1)}, f32[2,512,128]{2,1,0:T(8,128)}, bf16[12...) custom-call(s32[2]{0:T(128)} %pad_add_fusion.refs_0_, ...), custom_call_target="tpu_custom_call" | custom-call | flops 2415919104 | bytes 23488512 | tf_op jit(solution)/shard_map/pallas_call | solution.py:253
  23.3 7.6 %shard_map.306 = (bf16[128,512]{1,0:T(8,128)(2,1)}, f32[4,512]{1,0:T(4,128)}, bf16[128,512]{1,0:T(8,128)(2,1)}, bf16[1280,128]{1,0:T(8,128)(2,1)}, bf16[5376,128]{1,0:T(8,128)(2,1)}) custom-call(s32[2]{0:T(128)} %pad_add_fusion.refs_0_, f32[3,512]{1,0:T(4,128)} %refs_1_.4, f32[128,512]{1,0:T(8,128)} %get-tuple-element.65.refs_2_, ...), custom_call_target="tpu_custom_call" | custom-call | flops 671088640 | bytes 9582592 | tf_op jit(solution)/shard_map/pallas_call | solution.py:253
  31.5 8.3 %shard_map.307 = (bf16[128,512]{1,0:T(8,128)(2,1)}, bf16[1792,128]{1,0:T(8,128)(2,1)}, bf16[6464,128]{1,0:T(8,128)(2,1)}) custom-call(s32[2]{0:T(128)} %pad_add_fusion.refs_0_, f32[2,512]{1,0:T(2,128)} %refs_1_.5, bf16[128,512]{1,0:T(8,128)(2,1)} %get-tuple-element.78.refs_2_, f32[128,512]{1,0:T(8,128)} %get-tuple-element.79.refs_3_, ...), custom_call_target="tpu_custom_call" | custom-call | flops 872415232 | bytes 12222464 | tf_op jit(solution)/shard_map/pallas_call | solution.py:253
  41.2 1.8 %collective-permute-start.1 = (bf16[128,512]{1,0:T(8,128)(2,1)S(1)}, bf16[128,512]{1,0:T(8,128)(2,1)S(1)}, u32[]{:S(2)}, u32[]{:S(2)}) collective-permute-start(bf16[128,512]{1,0:T(8,128)(2,1)S(1)} %broadcast_select_fusion.2), channel_id=1, source_target_pairs={{0,16},{16,0},{1,17},{17,1},{2,18},{18,2},{3,19},{19,3},{4,20},{20... | collective-permute-start | bytes 393224 | tf_op jit(solution)/shard_map/ppermute | solution.py:625
  44.3 4.1 %shard_map.312 = (bf16[8,256,256]{2,1,0:T(8,128)(2,1)}, bf16[8,256,256]{2,1,0:T(8,128)(2,1)}) custom-call(s32[7]{0:T(128)} %stack.75.scalar, bf16[1280,128]{1,0:T(8,128)(2,1)} %get-tuple-element.105.keep_in, bf16[3840,128]{1,0:T(8,128)(2,1)} %get-tuple-element.106.send_in, bf16[3840,128]{1,0:T(8,128)(2,1)} %collective-permute-done.21.came_in), custom_call_target="tpu_custom_call" | custom-call | flops 536870912 | bytes 5046272 | tf_op jit(solution)/shard_map/pallas_call | solution.py:368
  50.4 3.9 %shard_map.310 = (bf16[8,128,256]{2,1,0:T(8,128)(2,1)}, bf16[8,128,256]{2,1,0:T(8,128)(2,1)}) custom-call(s32[7]{0:T(128)} %stack.75.scalar, bf16[1280,128]{1,0:T(8,128)(2,1)} %get-tuple-element.99.keep_in, bf16[5376,128]{1,0:T(8,128)(2,1)} %get-tuple-element.100.send_in, bf16[5376,128]{1,0:T(8,128)(2,1)} %copy-done.1), custom_call_target="tpu_custom_call" | custom-call | flops 268435456 | bytes 5177344 | tf_op jit(solution)/shard_map/pallas_call | solution.py:368
  55.6 3.8 %shard_map.311 = (bf16[8,128,256]{2,1,0:T(8,128)(2,1)}, bf16[8,128,256]{2,1,0:T(8,128)(2,1)}) custom-call(s32[7]{0:T(128)} %stack.75.scalar, bf16[1280,128]{1,0:T(8,128)(2,1)} %get-tuple-element.99.keep_in, bf16[5376,128]{1,0:T(8,128)(2,1)} %get-tuple-element.100.send_in, bf16[5376,128]{1,0:T(8,128)(2,1)} %copy-done.1), custom_call_target="tpu_custom_call" | custom-call | flops 268435456 | bytes 5177344 | tf_op jit(solution)/shard_map/pallas_call | solution.py:368
  63.0 4.3 %shard_map.308 = (bf16[8,144,256]{2,1,0:T(8,128)(2,1)}, bf16[8,144,256]{2,1,0:T(8,128)(2,1)}) custom-call(s32[7]{0:T(128)} %stack.71.scalar, bf16[1792,128]{1,0:T(8,128)(2,1)} %get-tuple-element.93.keep_in, bf16[6464,128]{1,0:T(8,128)(2,1)} %get-tuple-element.94.send_in, bf16[6464,128]{1,0:T(8,128)(2,1)} %copy-done), custom_call_target="tpu_custom_call" | custom-call | flops 268435456 | bytes 6144000 | tf_op jit(solution)/shard_map/pallas_call | solution.py:368
  69.2 1.8 %collective-permute-start.14 = (bf16[4,128,256]{2,1,0:T(8,128)(2,1)S(1)}, bf16[4,128,256]{2,1,0:T(8,128)(2,1)S(1)}, u32[]{:S(2)}, u32[]{:S(2)}) collective-permute-start(bf16[4,128,256]{2,1,0:T(8,128)(2,1)S(1)} %get-tuple-element.120), channel_id=1, source_target_pairs={{0,2},{1,17},{2,0},{3,19},{4,6},{5,21},{6,4},{7,23},{8,10},{9,25},... | collective-permute-start | bytes 786440 | tf_op jit(solution)/shard_map/ppermute | solution.py:639
  71.1 6.6 %collective-permute-done.17 = bf16[8,128,256]{2,1,0:T(8,128)(2,1)S(1)} collective-permute-done((bf16[8,128,256]{2,1,0:T(8,128)(2,1)}, bf16[8,128,256]{2,1,0:T(8,128)(2,1)S(1)}, u32[]{:S(2)}, u32[]{:S(2)}) %collective-permute-start.17) | collective-permute-done | bytes 524320 | tf_op jit(solution)/shard_map/ppermute | solution.py:639
  77.8 1.9 %collective-permute-start.18 = (bf16[4,128,256]{2,1,0:T(8,128)(2,1)S(1)}, bf16[4,128,256]{2,1,0:T(8,128)(2,1)S(1)}, u32[]{:S(2)}, u32[]{:S(2)}) collective-permute-start(bf16[4,128,256]{2,1,0:T(8,128)(2,1)S(1)} %get-tuple-element.118), channel_id=1, source_target_pairs={{0,2},{1,17},{2,0},{3,19},{4,6},{5,21},{6,4},{7,23},{8,10},{9,25},... | collective-permute-start | bytes 786440 | tf_op jit(solution)/shard_map/ppermute | solution.py:639
  79.7 4.5 %shard_map.309 = (bf16[8,256,256]{2,1,0:T(8,128)(2,1)}, bf16[8,256,256]{2,1,0:T(8,128)(2,1)}) custom-call(s32[7]{0:T(128)} %stack.75.scalar, bf16[1792,128]{1,0:T(8,128)(2,1)} %get-tuple-element.93.keep_in, bf16[6464,128]{1,0:T(8,128)(2,1)} %get-tuple-element.94.send_in, bf16[6464,128]{1,0:T(8,128)(2,1)} %copy-done), custom_call_target="tpu_custom_call" | custom-call | flops 536870912 | bytes 7061504 | tf_op jit(solution)/shard_map/pallas_call | solution.py:368
  88.6 2.5 %collective-permute-start.5 = (bf16[4,144,256]{2,1,0:T(8,128)(2,1)S(1)}, bf16[4,144,256]{2,1,0:T(8,128)(2,1)S(1)}, u32[]{:S(2)}, u32[]{:S(2)}) collective-permute-start(bf16[4,144,256]{2,1,0:T(8,128)(2,1)S(1)} %get-tuple-element.114), channel_id=1, source_target_pairs={{0,8},{1,9},{2,10},{3,11},{4,12},{5,13},{6,14},{7,15},{8,0},{9,1},... | collective-permute-start | bytes 884744 | tf_op jit(solution)/shard_map/ppermute | solution.py:639
  91.7 3.6 %collective-permute-start.16 = (bf16[1,128,256]{2,1,0:T(8,128)(2,1)S(1)}, bf16[1,128,256]{2,1,0:T(8,128)(2,1)S(1)}, u32[]{:S(2)}, u32[]{:S(2)}) collective-permute-start(bf16[1,128,256]{2,1,0:T(8,128)(2,1)S(1)} %add_convert_fusion.28), channel_id=1, source_target_pairs={{0,8},{1,9},{2,10},{3,11},{4,12},{5,13},{6,14},{7,15},{8,0},{9,1},... | collective-permute-start | bytes 196616 | tf_op jit(solution)/shard_map/ppermute | solution.py:639
  95.3 2.8 %collective-permute-start.20 = (bf16[1,128,256]{2,1,0:T(8,128)(2,1)S(1)}, bf16[1,128,256]{2,1,0:T(8,128)(2,1)S(1)}, u32[]{:S(2)}, u32[]{:S(2)}) collective-permute-start(bf16[1,128,256]{2,1,0:T(8,128)(2,1)S(1)} %add_convert_fusion.26), channel_id=1, source_target_pairs={{0,8},{1,9},{2,10},{3,11},{4,12},{5,13},{6,14},{7,15},{8,0},{9,1},... | collective-permute-start | bytes 196616 | tf_op jit(solution)/shard_map/ppermute | solution.py:639
  98.1 7.5 %collective-permute-done.16 = bf16[1,128,256]{2,1,0:T(8,128)(2,1)S(1)} collective-permute-done((bf16[1,128,256]{2,1,0:T(8,128)(2,1)S(1)}, bf16[1,128,256]{2,1,0:T(8,128)(2,1)S(1)}, u32[]{:S(2)}, u32[]{:S(2)}) %collective-permute-start.16) | collective-permute-done | bytes 65568 | tf_op jit(solution)/shard_map/ppermute | solution.py:639
  109.8 4.4 %collective-permute-done.6 = bf16[2,144,256]{2,1,0:T(8,128)(2,1)S(1)} collective-permute-done((bf16[2,144,256]{2,1,0:T(8,128)(2,1)S(1)}, bf16[2,144,256]{2,1,0:T(8,128)(2,1)S(1)}, u32[]{:S(2)}, u32[]{:S(2)}) %collective-permute-start.6) | collective-permute-done | bytes 147488 | tf_op jit(solution)/shard_map/ppermute | solution.py:639
  116.7 2.0 %collective-permute-done.7 = bf16[1,144,256]{2,1,0:T(8,128)(2,1)S(1)} collective-permute-done((bf16[1,144,256]{2,1,0:T(8,128)(2,1)S(1)}, bf16[1,144,256]{2,1,0:T(8,128)(2,1)S(1)}, u32[]{:S(2)}, u32[]{:S(2)}) %collective-permute-start.7) | collective-permute-done | bytes 73760 | tf_op jit(solution)/shard_map/ppermute | solution.py:639
  121.2 3.0 %collective-permute-done.9 = bf16[4,256,256]{2,1,0:T(8,128)(2,1)S(1)} collective-permute-done((bf16[4,256,256]{2,1,0:T(8,128)(2,1)S(1)}, bf16[4,256,256]{2,1,0:T(8,128)(2,1)S(1)}, u32[]{:S(2)}, u32[]{:S(2)}) %collective-permute-start.9) | collective-permute-done | bytes 524320 | tf_op jit(solution)/shard_map/ppermute | solution.py:639
  124.5 3.0 %collective-permute-done.25 = bf16[1,256,256]{2,1,0:T(8,128)(2,1)S(1)} collective-permute-done((bf16[1,256,256]{2,1,0:T(8,128)(2,1)S(1)}, bf16[1,256,256]{2,1,0:T(8,128)(2,1)S(1)}, u32[]{:S(2)}, u32[]{:S(2)}) %collective-permute-start.25) | collective-permute-done | bytes 131104 | tf_op jit(solution)/shard_map/ppermute | solution.py:639
  128.2 4.1 %collective-permute-done.10 = bf16[2,256,256]{2,1,0:T(8,128)(2,1)S(1)} collective-permute-done((bf16[2,256,256]{2,1,0:T(8,128)(2,1)S(1)}, bf16[2,256,256]{2,1,0:T(8,128)(2,1)S(1)}, u32[]{:S(2)}, u32[]{:S(2)}) %collective-permute-start.10) | collective-permute-done | bytes 262176 | tf_op jit(solution)/shard_map/ppermute | solution.py:639
  133.0 5.6 %collective-permute-done.11 = bf16[1,256,256]{2,1,0:T(8,128)(2,1)S(1)} collective-permute-done((bf16[1,256,256]{2,1,0:T(8,128)(2,1)S(1)}, bf16[1,256,256]{2,1,0:T(8,128)(2,1)S(1)}, u32[]{:S(2)}, u32[]{:S(2)}) %collective-permute-start.11) | collective-permute-done | bytes 131104 | tf_op jit(solution)/shard_map/ppermute | solution.py:639
  (105 shorter events, 32.5 us)
Async XLA Ops:
  1.6 6.5 %collective-permute-start = (bf16[128,512]{1,0:T(8,128)(2,1)S(1)}, bf16[128,512]{1,0:T(8,128)(2,1)S(1)}, u32[]{:S(2)}, u32[]{:S(2)}) collective-permute-start(bf16[128,512]{1,0:T(8,128)(2,1)S(1)} %dynamic-slice_bitcast_fusion), channel_id=1, source_target_pairs={{0,16},{16,0},{1,17},{17,1},{2,18},{18,2},{3,19},{19,3},{4,20},{20... | collective-permute-start | bytes 393224 | tf_op jit(solution)/shard_map/ppermute | solution.py:625
  30.9 18.4 %collective-permute-start.12 = (bf16[5376,128]{1,0:T(8,128)(2,1)}, bf16[5376,128]{1,0:T(8,128)(2,1)S(1)}, u32[]{:S(2)}, u32[]{:S(2)}) collective-permute-start(bf16[5376,128]{1,0:T(8,128)(2,1)} %get-tuple-element.100.send_in), channel_id=1, source_target_pairs={{0,1},{1,0},{2,3},{3,2},{4,5},{5,4},{6,7},{7,6},{8,9},{9,8},{10,11... | collective-permute-start | bytes 4128776 | tf_op jit(solution)/shard_map/ppermute | solution.py:625
  31.0 13.3 %collective-permute-start.21 = (bf16[3840,128]{1,0:T(8,128)(2,1)}, bf16[3840,128]{1,0:T(8,128)(2,1)}, u32[]{:S(2)}, u32[]{:S(2)}) collective-permute-start(bf16[3840,128]{1,0:T(8,128)(2,1)} %get-tuple-element.106.send_in), channel_id=1, source_target_pairs={{0,1},{1,0},{2,3},{3,2},{4,5},{5,4},{6,7},{7,6},{8,9},{9,8},{10,11... | collective-permute-start | bytes 2949128 | tf_op jit(solution)/shard_map/ppermute | solution.py:625
  39.8 22.0 %collective-permute-start.3 = (bf16[6464,128]{1,0:T(8,128)(2,1)}, bf16[6464,128]{1,0:T(8,128)(2,1)S(1)}, u32[]{:S(2)}, u32[]{:S(2)}) collective-permute-start(bf16[6464,128]{1,0:T(8,128)(2,1)} %get-tuple-element.94.send_in), channel_id=1, source_target_pairs={{0,1},{1,0},{2,3},{3,2},{4,5},{5,4},{6,7},{7,6},{8,9},{9,8},{10,11... | collective-permute-start | bytes 4964360 | tf_op jit(solution)/shard_map/ppermute | solution.py:625
  41.2 8.1 %collective-permute-start.1 = (bf16[128,512]{1,0:T(8,128)(2,1)S(1)}, bf16[128,512]{1,0:T(8,128)(2,1)S(1)}, u32[]{:S(2)}, u32[]{:S(2)}) collective-permute-start(bf16[128,512]{1,0:T(8,128)(2,1)S(1)} %broadcast_select_fusion.2), channel_id=1, source_target_pairs={{0,16},{16,0},{1,17},{17,1},{2,18},{18,2},{3,19},{19,3},{4,20},{20... | collective-permute-start | bytes 393224 | tf_op jit(solution)/shard_map/ppermute | solution.py:625
  43.0 18.0 %collective-permute-start.2 = (bf16[128,512]{1,0:T(8,128)(2,1)S(1)}, bf16[128,512]{1,0:T(8,128)(2,1)S(1)}, u32[]{:S(2)}, u32[]{:S(2)}) collective-permute-start(bf16[128,512]{1,0:T(8,128)(2,1)S(1)} %broadcast_select_fusion), channel_id=1, source_target_pairs={{0,16},{16,0},{1,17},{17,1},{2,18},{18,2},{3,19},{19,3},{4,20},{20... | collective-permute-start | bytes 393224 | tf_op jit(solution)/shard_map/ppermute | solution.py:625
  48.4 36.8 %collective-permute-start.22 = (bf16[8,256,256]{2,1,0:T(8,128)(2,1)}, bf16[8,256,256]{2,1,0:T(8,128)(2,1)S(1)}, u32[]{:S(2)}, u32[]{:S(2)}) collective-permute-start(bf16[8,256,256]{2,1,0:T(8,128)(2,1)} %get-tuple-element.108), channel_id=1, source_target_pairs={{0,16},{1,3},{2,18},{3,1},{4,20},{5,7},{6,22},{7,5},{8,24},{9,11},... | collective-permute-start | bytes 3145736 | tf_op jit(solution)/shard_map/ppermute | solution.py:639
  54.3 14.7 %collective-permute-start.13 = (bf16[8,128,256]{2,1,0:T(8,128)(2,1)}, bf16[8,128,256]{2,1,0:T(8,128)(2,1)S(1)}, u32[]{:S(2)}, u32[]{:S(2)}) collective-permute-start(bf16[8,128,256]{2,1,0:T(8,128)(2,1)} %get-tuple-element.102), channel_id=1, source_target_pairs={{0,16},{1,3},{2,18},{3,1},{4,20},{5,7},{6,22},{7,5},{8,24},{9,11},... | collective-permute-start | bytes 1572872 | tf_op jit(solution)/shard_map/ppermute | solution.py:639
  59.4 18.3 %collective-permute-start.17 = (bf16[8,128,256]{2,1,0:T(8,128)(2,1)}, bf16[8,128,256]{2,1,0:T(8,128)(2,1)S(1)}, u32[]{:S(2)}, u32[]{:S(2)}) collective-permute-start(bf16[8,128,256]{2,1,0:T(8,128)(2,1)} %get-tuple-element.104), channel_id=1, source_target_pairs={{0,16},{1,3},{2,18},{3,1},{4,20},{5,7},{6,22},{7,5},{8,24},{9,11},... | collective-permute-start | bytes 1572872 | tf_op jit(solution)/shard_map/ppermute | solution.py:639
  67.3 21.2 %collective-permute-start.4 = (bf16[8,144,256]{2,1,0:T(8,128)(2,1)}, bf16[8,144,256]{2,1,0:T(8,128)(2,1)S(1)}, u32[]{:S(2)}, u32[]{:S(2)}) collective-permute-start(bf16[8,144,256]{2,1,0:T(8,128)(2,1)} %get-tuple-element.96), channel_id=1, source_target_pairs={{0,4},{1,5},{2,6},{3,7},{4,0},{5,1},{6,2},{7,3},{8,12},{9,13},{10,... | collective-permute-start | bytes 1769480 | tf_op jit(solution)/shard_map/ppermute | solution.py:639
  69.2 16.9 %collective-permute-start.14 = (bf16[4,128,256]{2,1,0:T(8,128)(2,1)S(1)}, bf16[4,128,256]{2,1,0:T(8,128)(2,1)S(1)}, u32[]{:S(2)}, u32[]{:S(2)}) collective-permute-start(bf16[4,128,256]{2,1,0:T(8,128)(2,1)S(1)} %get-tuple-element.120), channel_id=1, source_target_pairs={{0,2},{1,17},{2,0},{3,19},{4,6},{5,21},{6,4},{7,23},{8,10},{9,25},... | collective-permute-start | bytes 786440 | tf_op jit(solution)/shard_map/ppermute | solution.py:639
  77.8 9.6 %collective-permute-start.18 = (bf16[4,128,256]{2,1,0:T(8,128)(2,1)S(1)}, bf16[4,128,256]{2,1,0:T(8,128)(2,1)S(1)}, u32[]{:S(2)}, u32[]{:S(2)}) collective-permute-start(bf16[4,128,256]{2,1,0:T(8,128)(2,1)S(1)} %get-tuple-element.118), channel_id=1, source_target_pairs={{0,2},{1,17},{2,0},{3,19},{4,6},{5,21},{6,4},{7,23},{8,10},{9,25},... | collective-permute-start | bytes 786440 | tf_op jit(solution)/shard_map/ppermute | solution.py:639
  84.2 30.5 %collective-permute-start.8 = (bf16[8,256,256]{2,1,0:T(8,128)(2,1)}, bf16[8,256,256]{2,1,0:T(8,128)(2,1)S(1)}, u32[]{:S(2)}, u32[]{:S(2)}) collective-permute-start(bf16[8,256,256]{2,1,0:T(8,128)(2,1)} %get-tuple-element.98), channel_id=1, source_target_pairs={{0,16},{1,3},{2,18},{3,1},{4,20},{5,7},{6,22},{7,5},{8,24},{9,11},... | collective-permute-start | bytes 3145736 | tf_op jit(solution)/shard_map/ppermute | solution.py:639
  85.5 23.4 %collective-permute-start.23 = (bf16[4,256,256]{2,1,0:T(8,128)(2,1)S(1)}, bf16[4,256,256]{2,1,0:T(8,128)(2,1)S(1)}, u32[]{:S(2)}, u32[]{:S(2)}) collective-permute-start(bf16[4,256,256]{2,1,0:T(8,128)(2,1)S(1)} %get-tuple-element.110), channel_id=1, source_target_pairs={{0,2},{1,17},{2,0},{3,19},{4,6},{5,21},{6,4},{7,23},{8,10},{9,25},... | collective-permute-start | bytes 1572872 | tf_op jit(solution)/shard_map/ppermute | solution.py:639
  87.5 7.8 %collective-permute-start.19 = (bf16[2,128,256]{2,1,0:T(8,128)(2,1)S(1)}, bf16[2,128,256]{2,1,0:T(8,128)(2,1)S(1)}, u32[]{:S(2)}, u32[]{:S(2)}) collective-permute-start(bf16[2,128,256]{2,1,0:T(8,128)(2,1)S(1)} %get-tuple-element.126), channel_id=1, source_target_pairs={{0,4},{1,5},{2,6},{3,7},{4,0},{5,1},{6,2},{7,3},{8,12},{9,13},{10,... | collective-permute-start | bytes 393224 | tf_op jit(solution)/shard_map/ppermute | solution.py:639
  88.6 19.0 %collective-permute-start.5 = (bf16[4,144,256]{2,1,0:T(8,128)(2,1)S(1)}, bf16[4,144,256]{2,1,0:T(8,128)(2,1)S(1)}, u32[]{:S(2)}, u32[]{:S(2)}) collective-permute-start(bf16[4,144,256]{2,1,0:T(8,128)(2,1)S(1)} %get-tuple-element.114), channel_id=1, source_target_pairs={{0,8},{1,9},{2,10},{3,11},{4,12},{5,13},{6,14},{7,15},{8,0},{9,1},... | collective-permute-start | bytes 884744 | tf_op jit(solution)/shard_map/ppermute | solution.py:639
  91.7 13.9 %collective-permute-start.16 = (bf16[1,128,256]{2,1,0:T(8,128)(2,1)S(1)}, bf16[1,128,256]{2,1,0:T(8,128)(2,1)S(1)}, u32[]{:S(2)}, u32[]{:S(2)}) collective-permute-start(bf16[1,128,256]{2,1,0:T(8,128)(2,1)S(1)} %add_convert_fusion.28), channel_id=1, source_target_pairs={{0,8},{1,9},{2,10},{3,11},{4,12},{5,13},{6,14},{7,15},{8,0},{9,1},... | collective-permute-start | bytes 196616 | tf_op jit(solution)/shard_map/ppermute | solution.py:639
  95.3 11.0 %collective-permute-start.20 = (bf16[1,128,256]{2,1,0:T(8,128)(2,1)S(1)}, bf16[1,128,256]{2,1,0:T(8,128)(2,1)S(1)}, u32[]{:S(2)}, u32[]{:S(2)}) collective-permute-start(bf16[1,128,256]{2,1,0:T(8,128)(2,1)S(1)} %add_convert_fusion.26), channel_id=1, source_target_pairs={{0,8},{1,9},{2,10},{3,11},{4,12},{5,13},{6,14},{7,15},{8,0},{9,1},... | collective-permute-start | bytes 196616 | tf_op jit(solution)/shard_map/ppermute | solution.py:639
  107.7 6.5 %collective-permute-start.6 = (bf16[2,144,256]{2,1,0:T(8,128)(2,1)S(1)}, bf16[2,144,256]{2,1,0:T(8,128)(2,1)S(1)}, u32[]{:S(2)}, u32[]{:S(2)}) collective-permute-start(bf16[2,144,256]{2,1,0:T(8,128)(2,1)S(1)} %get-tuple-element.124), channel_id=1, source_target_pairs={{0,16},{1,3},{2,18},{3,1},{4,20},{5,7},{6,22},{7,5},{8,24},{9,11},... | collective-permute-start | bytes 442376 | tf_op jit(solution)/shard_map/ppermute | solution.py:639
  109.0 11.4 %collective-permute-start.24 = (bf16[2,256,256]{2,1,0:T(8,128)(2,1)S(1)}, bf16[2,256,256]{2,1,0:T(8,128)(2,1)S(1)}, u32[]{:S(2)}, u32[]{:S(2)}) collective-permute-start(bf16[2,256,256]{2,1,0:T(8,128)(2,1)S(1)} %get-tuple-element.116), channel_id=1, source_target_pairs={{0,4},{1,5},{2,6},{3,7},{4,0},{5,1},{6,2},{7,3},{8,12},{9,13},{10,... | collective-permute-start | bytes 786440 | tf_op jit(solution)/shard_map/ppermute | solution.py:639
  115.0 9.2 %collective-permute-start.9 = (bf16[4,256,256]{2,1,0:T(8,128)(2,1)S(1)}, bf16[4,256,256]{2,1,0:T(8,128)(2,1)S(1)}, u32[]{:S(2)}, u32[]{:S(2)}) collective-permute-start(bf16[4,256,256]{2,1,0:T(8,128)(2,1)S(1)} %get-tuple-element.112), channel_id=1, source_target_pairs={{0,2},{1,17},{2,0},{3,19},{4,6},{5,21},{6,4},{7,23},{8,10},{9,25},... | collective-permute-start | bytes 1572872 | tf_op jit(solution)/shard_map/ppermute | solution.py:639
  120.5 7.0 %collective-permute-start.25 = (bf16[1,256,256]{2,1,0:T(8,128)(2,1)S(1)}, bf16[1,256,256]{2,1,0:T(8,128)(2,1)S(1)}, u32[]{:S(2)}, u32[]{:S(2)}) collective-permute-start(bf16[1,256,256]{2,1,0:T(8,128)(2,1)S(1)} %add_convert_fusion.16), channel_id=1, source_target_pairs={{0,8},{1,9},{2,10},{3,11},{4,12},{5,13},{6,14},{7,15},{8,0},{9,1},... | collective-permute-start | bytes 393224 | tf_op jit(solution)/shard_map/ppermute | solution.py:639
  124.4 7.8 %collective-permute-start.10 = (bf16[2,256,256]{2,1,0:T(8,128)(2,1)S(1)}, bf16[2,256,256]{2,1,0:T(8,128)(2,1)S(1)}, u32[]{:S(2)}, u32[]{:S(2)}) collective-permute-start(bf16[2,256,256]{2,1,0:T(8,128)(2,1)S(1)} %get-tuple-element.122), channel_id=1, source_target_pairs={{0,4},{1,5},{2,6},{3,7},{4,0},{5,1},{6,2},{7,3},{8,12},{9,13},{10,... | collective-permute-start | bytes 786440 | tf_op jit(solution)/shard_map/ppermute | solution.py:639
  132.3 6.3 %collective-permute-start.11 = (bf16[1,256,256]{2,1,0:T(8,128)(2,1)S(1)}, bf16[1,256,256]{2,1,0:T(8,128)(2,1)S(1)}, u32[]{:S(2)}, u32[]{:S(2)}) collective-permute-start(bf16[1,256,256]{2,1,0:T(8,128)(2,1)S(1)} %add_convert_fusion.22), channel_id=1, source_target_pairs={{0,8},{1,9},{2,10},{3,11},{4,12},{5,13},{6,14},{7,15},{8,0},{9,1},... | collective-permute-start | bytes 393224 | tf_op jit(solution)/shard_map/ppermute | solution.py:639
  (14 other events, 86.9 us)

commit v2 on v0

v2 whole, which is shorter than its diff:
```python
import math
from types import SimpleNamespace
from types import SimpleNamespace
from types import SimpleNamespace

import jax
import jax.numpy as jnp
from jax import lax
from jax.experimental import pallas as pl
from jax.experimental.pallas import tpu as pltpu
from jax.sharding import PartitionSpec as P

HEADS = 8
HEAD_DIM = 64
NEG = -1e30
EPS = 1e-05
GROUPS = 16
SLAB = 256
LANES = 128
PER_SLAB = SLAB // HEAD_DIM
BF = jnp.bfloat16
F32 = jnp.float32
def lasting(span):
    return pl.CostEstimate(flops=int(span * 8e9), bytes_accessed=1, transcendentals=0)


FACTOR = 1.0 / math.sqrt(HEAD_DIM)
HBM = pl.BlockSpec(memory_space=pltpu.HBM)
VMEM = pl.BlockSpec(memory_space=pltpu.VMEM)


def matmul(left, right):
    return lax.dot_general(left, right, (((1,), (0,)), ((), ())), preferred_element_type=F32)


def matmul_back(grad, weight):
    return lax.dot_general(grad, weight, (((1,), (1,)), ((), ())), preferred_element_type=F32)


def matmul_across(left, grad):
    return lax.dot_general(left, grad, (((0,), (0,)), ((), ())), preferred_element_type=F32)


def norm(summed, gain, shift):
    center = jnp.mean(summed, -1, keepdims=True)
    centered = summed - center
    spread = jnp.mean(centered * centered, -1, keepdims=True)
    scale = lax.rsqrt(spread + EPS)
    unit = centered * scale
    return unit * gain + shift, unit, scale


def norm_back(grad, unit, scale, gain):
    grad_gain = jnp.sum(grad * unit, 0, keepdims=True)
    grad_shift = jnp.sum(grad, 0, keepdims=True)
    inner = grad * gain
    center = jnp.mean(inner, -1, keepdims=True)
    along = jnp.mean(inner * unit, -1, keepdims=True)
    return scale * (inner - center - unit * along), grad_gain, grad_shift


def gelu_both(before):
    root = math.sqrt(2.0 / math.pi)
    square = before * before
    bent = jnp.tanh(root * before * (1.0 + 0.044715 * square))
    half = 0.5 * (1.0 + bent)
    slope = half + 0.5 * before * (1.0 - bent * bent) * (root * (1.0 + 3 * 0.044715 * square))
    return before * half, slope


def head_marks(dtype):
    lane = lax.broadcasted_iota(jnp.int32, (1, SLAB), 1) // HEAD_DIM
    return [(lane == h).astype(F32).astype(dtype) for h in range(PER_SLAB)]


def spread_heads(slab, marks):
    return jnp.concatenate([slab * mark for mark in marks], 0)


def gather_heads(stacked, rows):
    lane = lax.broadcasted_iota(jnp.int32, (1, SLAB), 1) // HEAD_DIM
    total = stacked[:rows]
    for h in range(1, PER_SLAB):
        total = jnp.where(lane == h, stacked[h * rows : (h + 1) * rows], total)
    return total


def attend(query, keys, values, allowed, chances_ref):
    rows = query.shape[0]
    marks = head_marks(BF)
    wide = jnp.concatenate([allowed] * PER_SLAB, 0)
    mixed = []
    for slab in range(query.shape[1] // SLAB):
        at = slice(slab * SLAB, (slab + 1) * SLAB)
        scores = matmul_back(spread_heads(query[:, at], marks), keys[:, at]) * FACTOR
        scores = jnp.where(wide, scores, NEG)
        weights = jnp.exp(scores - jnp.max(scores, -1, keepdims=True))
        chances = weights * (1.0 / jnp.sum(weights, -1, keepdims=True))
        chances_ref[slab] = chances
        mixed.append(gather_heads(matmul(chances.astype(BF), values[:, at]), rows).astype(BF))
    return jnp.concatenate(mixed, 1)


def attend_back(query, keys, values, chances_ref, grad_mixed):
    rows = query.shape[0]
    marks = head_marks(BF)
    grad_query, grad_keys, grad_values = [], [], []
    for slab in range(query.shape[1] // SLAB):
        at = slice(slab * SLAB, (slab + 1) * SLAB)
        chances = chances_ref[slab]
        spread_grad = spread_heads(grad_mixed[:, at], marks)
        grad_chances = matmul_back(spread_grad, values[:, at])
        grad_values.append(matmul_across(chances.astype(BF), spread_grad).astype(BF))
        held = jnp.sum(chances * grad_chances, -1, keepdims=True)
        grad_scores = (chances * (grad_chances - held)).astype(BF)
        grad_query.append((gather_heads(matmul(grad_scores, keys[:, at]), rows) * FACTOR).astype(BF))
        spread_query = spread_heads(query[:, at], marks)
        grad_keys.append((matmul_across(grad_scores, spread_query) * FACTOR).astype(BF))
    return [jnp.concatenate(item, 1) for item in (grad_query, grad_keys, grad_values)]


def tiles_of(array):
    return [array[:, at : at + LANES] for at in range(0, array.shape[1], LANES)]


class Entry:
    def __init__(self, array):
        self.arrays = (array,)
        self.shape, self.dtype = array.shape[1:], array.dtype

    def pieces(self, refs, section):
        return [(None, refs[0].at[section])]


class Either:
    def __init__(self, *pair):
        pair = [item if isinstance(item, tuple) else (item, None) for item in pair]
        self.arrays = tuple(array for array, unused in pair)
        self.entries = [entry for unused, entry in pair]
        first = self.arrays[0]
        self.shape = first.shape if self.entries[0] is None else first.shape[1:]
        self.dtype = first.dtype

    def pieces(self, refs, section):
        return [
            (here, ref if entry is None else ref.at[entry])
            for here, (ref, entry) in enumerate(zip(refs, self.entries))
        ]


class Whole:
    def __init__(self, array):
        self.arrays = (array,)
        self.shape, self.dtype = array.shape, array.dtype

    def pieces(self, refs, section):
        return [(None, refs[0])]


class Room:
    def __init__(self, inputs, sources, held, sems):
        self.inputs, self.sources, self.held, self.sems = inputs, sources, held, sems
        self.section = lax.axis_index("section")
        self.core = lax.axis_index("rows") & 1
        self.arrived = set()
        for place, name in enumerate(inputs):
            for here, source in inputs[name].pieces(sources[name], self.section):
                copy = pltpu.make_async_copy(source, held[name], sems.at[place])
                if here is None:
                    copy.start()
                else:
                    pl.when(self.section == here)(copy.start)

    def __getattr__(self, name):
        if name in self.inputs and name not in self.arrived:
            self.arrived.add(name)
            place = list(self.inputs).index(name)
            source = self.inputs[name].pieces(self.sources[name], self.section)[0][1]
            pltpu.make_async_copy(source, self.held[name], self.sems.at[place]).wait()
        return self.held[name]

    def finish(self):
        for name in self.inputs:
            getattr(self, name)

    def either(self, here, there):
        return jnp.where(self.section == 0, here[...], there[...])


class Packet:
    def __init__(self, extra=0, **weights):
        self.shapes = {name: array.shape for name, array in weights.items()}
        self.left_at, self.grad_at = {}, {}
        left = grad = 0
        for name, (depth, width) in self.shapes.items():
            self.left_at[name], self.grad_at[name] = left, grad
            left, grad = left + depth // 2, grad + width
        self.left, self.extra_at, self.grad = left, grad, grad + extra

    def leaving(self):
        return [
            pltpu.VMEM((self.left, LANES), BF),
            pltpu.VMEM((self.left + self.grad, LANES), BF),
        ]

    def bind(self, room, refs):
        self.room, (self.keep, self.send) = room, refs

    def stash(self, **operands):
        even = self.room.core == 0
        for name, (left, grad) in operands.items():
            depth, width = self.shapes[name]
            block = depth // GROUPS
            across = left.T
            for group in range(0, GROUPS, 2):
                first = across[group * block : (group + 1) * block]
                second = across[(group + 1) * block : (group + 2) * block]
                top = self.left_at[name] + group // 2 * block
                self.keep[top : top + block] = jnp.where(even, first, second)
                self.send[top : top + block] = jnp.where(even, second, first)
            for place, tile in enumerate(tiles_of(grad)):
                top = self.left + self.grad_at[name] + place * LANES
                self.send[top : top + LANES] = tile


def far_away(array):
    return pltpu.with_memory_space_constraint(array, pltpu.HBM)


def pinned(array):
    return pltpu.with_memory_space_constraint(array, pltpu.VMEM)


def call(body, inputs, near, outputs, loads, span, limit, packet=None, extra=None):
    extra = extra or {}
    inputs = {
        name: item if hasattr(item, "pieces") else Whole(item) for name, item in inputs.items()
    }
    inputs.update({name: Whole(item) for name, item in loads.items()})
    arrays = [array for item in inputs.values() for array in item.arrays]
    outputs = {
        **outputs,
        **{name: jax.ShapeDtypeStruct(item.shape, item.dtype) for name, item in loads.items()},
    }
    shapes_out = [pltpu.VMEM(item.shape, item.dtype) for item in outputs.values()]
    shapes_out += packet.leaving() if packet else []
    brought = [name for name in inputs if name not in loads]

    def kernel(*refs):
        refs = list(refs)

        def take(count):
            taken = refs[:count]
            del refs[:count]
            return taken

        sources = {name: take(len(item.arrays)) for name, item in inputs.items()}
        held = dict(zip(near, take(len(near))))
        held.update(zip(outputs, take(len(outputs))))
        leaving = take(2) if packet else None
        held.update(zip(brought, take(len(brought))))
        held.update(zip(extra, take(len(extra))))
        room = Room(inputs, sources, held, refs[0])
        if packet:
            packet.bind(room, leaving)
        body(room)
        room.finish()

    scratch = [inputs[name] for name in brought] + list(extra.values())
    results = pl.pallas_call(
        kernel,
        out_shape=shapes_out,
        in_specs=[HBM] * len(arrays) + [VMEM] * len(near),
        out_specs=[VMEM] * len(shapes_out),
        scratch_shapes=[pltpu.VMEM(item.shape, item.dtype) for item in scratch]
        + [pltpu.SemaphoreType.DMA((max(1, len(inputs)),))],
        compiler_params=pltpu.CompilerParams(vmem_limit_bytes=limit << 20),
        cost_estimate=lasting(span),
    )(*(far_away(item) for item in arrays), *(pinned(item) for item in near.values()))
    return SimpleNamespace(**dict(zip(outputs, results))), tuple(results[len(outputs) :])


def place_of(side, block, orders, core):
    spots = []
    for order in orders:
        spot = side * (8 >> order.index(SIDE))
        for bit in range(3):
            spot = spot + (block >> bit & 1) * (8 >> order.index(bit + 1))
        spots.append(spot)
    return jnp.where(core == 0, spots[0], spots[1])


def bit_of(step, section, row):
    return section if step == SIDE else (row >> step) & 1


def weight_grads(parcels, names, orders, even, small=False):
    parts = [
        (packet, which, name)
        for which, (packet, *unused) in enumerate(parcels)
        for name in packet.shapes
        if name in names
    ]
    height = sum(
        packet.shapes[name][0] // GROUPS * packet.shapes[name][1] // (2 * SLAB)
        for packet, unused, name in parts
    )
    small_at = height
    height += 16 if small else 0
    half = pltpu.VMEM((GROUPS // 2, height, SLAB), BF)

    def kernel(*refs):
        *operands, kept_out, sent_out, packed = refs
        row = lax.axis_index("rows")
        core = row & 1
        if even:
            first = [bit_of(order[0], lax.axis_index("section"), row) for order in orders]
            mine = jnp.where(core == 0, first[0], first[1])
        else:
            mine = 0

        base = 0
        for packet, which, name in parts:
            keep_ref, send_ref, came_ref = operands[3 * which : 3 * which + 3]
            depth, width = packet.shapes[name]
            block, half_pieces = depth // GROUPS, width // (2 * SLAB)
            left_at, grad_at = packet.left_at[name], packet.left + packet.grad_at[name]
            left = jnp.concatenate(
                [ref[left_at : left_at + depth // 2] for ref in (keep_ref, came_ref)], 1
            )
            for piece in range(width // SLAB):
                at = grad_at + piece * SLAB
                right = jnp.concatenate(
                    [
                        jnp.concatenate([ref[at : at + LANES], ref[at + LANES : at + 2 * LANES]], 1)
                        for ref in (send_ref, came_ref)
                    ],
                    0,
                )
                tile = matmul(left, right).astype(BF)
                side, offset = divmod(piece, half_pieces)
                top = base + offset * block
                for number in range(GROUPS // 2):
                    packed[place_of(side, number, orders, core), top : top + block] = tile[
                        number * block : (number + 1) * block
                    ]
            base += block * half_pieces
        if small:
            packet = parcels[0][0]
            at = packet.left + packet.extra_at
            total = sum(
                jnp.concatenate([ref[at + 16 * i : at + 16 * i + 16] for i in range(4)], 1).astype(F32)
                for ref in operands[1:3]
            )
            width = total.shape[1]
            share = width // GROUPS
            for number in range(GROUPS // 2):
                turned = [
                    pltpu.roll(total, (width - (2 * number + i) * share) % width, 1) for i in (0, 1)
                ]
                part = jnp.where(core == 0, turned[0], turned[1])[:, :SLAB].astype(BF)
                for side in (0, 1):
                    packed[place_of(side, number, orders, core), small_at : small_at + 16] = part
        count = GROUPS // 2
        sent_out[...] = packed[pl.ds((1 - mine) * count, count)]
        kept_out[...] = packed[pl.ds(mine * count, count)]

    arrays = [array for unused, *rest in parcels for array in rest]
    return pl.pallas_call(
        kernel,
        out_shape=[half, half],
        in_specs=[VMEM] * len(arrays),
        out_specs=[VMEM] * 2,
        scratch_shapes=[pltpu.VMEM((GROUPS, height, SLAB), BF)],
        compiler_params=pltpu.CompilerParams(vmem_limit_bytes=16 << 20),
        cost_estimate=lasting(3.5),
    )(*(pinned(item) for item in arrays))


def equal_ids(row_ids, column_ids):
    length = row_ids.shape[1]
    down = jnp.broadcast_to(row_ids.astype(F32), (length, length)).T
    return down == jnp.broadcast_to(column_ids.astype(F32), (length, length))


def scale_out(scale):
    return jnp.broadcast_to(scale, (scale.shape[0], LANES))


def thirds(projected):
    width = projected.shape[1] // 3
    return [projected[:, i * width : (i + 1) * width] for i in range(3)]


def self_part(room, tokens, ids, causal, inward, outward, gain, shift):
    room.projected[...] = matmul(tokens, inward[...]).astype(BF)
    length = tokens.shape[0]
    rows = lax.broadcasted_iota(jnp.int32, (length, length), 0)
    columns = lax.broadcasted_iota(jnp.int32, (length, length), 1)
    reach = jnp.where(causal, 0, length)
    allowed = equal_ids(ids, ids) & (rows + reach >= columns)
    mixed = attend(*thirds(room.projected), allowed, room.chances)
    room.mixed[...] = mixed
    summed = tokens.astype(F32) + matmul(mixed, outward[...])
    first, unit, scale = norm(summed, gain, shift)
    room.unit[...] = unit
    room.scale[...] = scale_out(scale)
    return first


def own_body(room):
    section = room.section
    ids = room.segments[pl.ds(section, 1), pl.ds(section, 1), 0, :][0]
    gain = jnp.where(section == 0, room.encoder_gain[0:1], room.decoder_gain[0:1])
    shift = jnp.where(section == 0, room.encoder_shift[0:1], room.decoder_shift[0:1])
    room.first[...] = self_part(
        room, room.tokens[...], ids, section == 1, room.inward, room.outward, gain, shift
    )


def forward_body(room, packet):
    section = room.section
    source_ids = room.segments[0, pl.ds(section, 1), 0, :]
    target_ids = room.segments[1, pl.ds(section, 1), 0, :]
    ids = jnp.where(section == 0, target_ids, source_ids)
    gain = jnp.where(section == 0, room.decoder_gain[0:1], room.encoder_gain[0:1])
    shift = jnp.where(section == 0, room.decoder_shift[0:1], room.encoder_shift[0:1])
    other = self_part(
        room, room.tokens[...], ids, section == 0, room.inward, room.outward, gain, shift
    )
    own = room.own_first[...]

    first = jnp.where(section == 0, own, other)
    low = first.astype(BF)
    widen_forward(low, room.encoder_widen, room.e_hidden, room.e_slope)
    room.e_low[...] = low
    summed = first + matmul(room.e_hidden[...], room.encoder_narrow[...])
    result, unit, scale = norm(summed, room.encoder_gain[1:2], room.encoder_shift[1:2])
    memory = result.astype(BF)
    room.e_unit1[...] = unit
    room.e_scale1[...] = scale_out(scale)
    room.memory[...] = memory

    first = jnp.where(section == 0, other, own)
    low = first.astype(BF)
    query = matmul(low, room.decoder_cross_query[...]).astype(BF)
    paired = matmul(memory, room.decoder_cross_memory[...]).astype(BF)
    room.d_low[...] = low
    room.c_query[...] = query
    room.c_paired[...] = paired
    width = query.shape[1]
    mixed = attend(
        query,
        room.c_paired[:, :width],
        room.c_paired[:, width:],
        equal_ids(target_ids, source_ids),
        room.c_chances,
    )
    room.c_mixed[...] = mixed
    summed = first + matmul(mixed, room.decoder_cross_outward[...])
    second, unit, scale = norm(summed, room.decoder_gain[1:2], room.decoder_shift[1:2])
    room.d_unit1[...] = unit
    room.d_scale1[...] = scale_out(scale)

    low = second.astype(BF)
    widen_forward(low, room.decoder_widen, room.d_hidden, room.d_slope)
    summed = second + matmul(room.d_hidden[...], room.decoder_narrow[...])
    gain = room.decoder_gain[2:3]
    result, unit, scale = norm(summed, gain, room.decoder_shift[2:3])
    room.output[...] = result.astype(BF)

    grad_sum, grad_gain, grad_shift = norm_back(
        room.cotangent[...].astype(F32), unit, scale, gain
    )
    grad_low = grad_sum.astype(BF)
    grad_before = widen_backward(grad_low, room.decoder_narrow, room.d_slope)
    packet.stash(
        decoder_narrow=(room.d_hidden[...], grad_low), decoder_widen=(low, grad_before)
    )
    room.d_grad[...] = grad_sum + matmul_back(grad_before, room.decoder_widen[...])
    room.d_small2[...] = jnp.concatenate([grad_gain, grad_shift], 0)


def widen_forward(low, widen_ref, hidden_ref, slope_ref):
    step = 512
    for at in range(0, widen_ref.shape[1], step):
        hidden, slope = gelu_both(matmul(low, widen_ref[:, at : at + step]))
        hidden_ref[:, at : at + step] = hidden.astype(BF)
        slope_ref[:, at : at + step] = slope


def widen_backward(grad_low, narrow_ref, slope_ref):
    step = 512
    parts = []
    for at in range(0, narrow_ref.shape[0], step):
        grad_hidden = matmul_back(grad_low, narrow_ref[at : at + step])
        parts.append((grad_hidden * slope_ref[:, at : at + step]).astype(BF))
    return jnp.concatenate(parts, 1)


def cross_back_body(room, packet):
    gain = room.decoder_gain
    grad_sum, gain1, shift1 = norm_back(
        room.d_grad[...], room.d_unit1[...], room.d_scale1[:, :1], gain[1:2]
    )
    grad_low = grad_sum.astype(BF)
    grad_mixed = matmul_back(grad_low, room.decoder_cross_outward[...]).astype(BF)
    paired = room.c_paired
    query = room.c_query[...]
    width = query.shape[1]
    grad_query, grad_keys, grad_values = attend_back(
        query, paired[:, :width], paired[:, width:], room.c_chances, grad_mixed
    )
    grad_paired = jnp.concatenate([grad_keys, grad_values], 1)
    packet.stash(
        decoder_cross_query=(room.d_low[...], grad_query),
        decoder_cross_memory=(room.memory[...], grad_paired),
        decoder_cross_outward=(room.c_mixed[...], grad_low),
    )
    room.grad_memory[...] = matmul_back(grad_paired, room.decoder_cross_memory[...]).astype(BF)
    grad_normed = grad_sum + matmul_back(grad_query, room.decoder_cross_query[...])
    grad_sum, gain0, shift0 = norm_back(
        grad_normed,
        room.either(room.far_unit, room.near_unit),
        room.either(room.far_scale, room.near_scale)[:, :1],
        gain[0:1],
    )
    room.d_grad0[...] = grad_sum
    room.d_small01[...] = jnp.concatenate([gain0, gain1, shift0, shift1], 0)


def self_back(grad_sum, inward, outward, tokens, projected, chances, mixed):
    grad_low = grad_sum.astype(BF)
    grad_mixed = matmul_back(grad_low, outward[...]).astype(BF)
    grad_projected = jnp.concatenate(attend_back(*thirds(projected), chances, grad_mixed), 1)
    pairs = ((tokens, grad_projected), (mixed, grad_low))
    return pairs, grad_sum + matmul_back(grad_projected, inward[...])


def decoder_self_body(room, packet):
    either = room.either
    (inward, outward), grad_inputs = self_back(
        room.d_grad0[...],
        room.decoder_inward,
        room.decoder_outward,
        room.tokens[...],
        either(room.far_projected, room.near_projected),
        either(room.far_chances, room.near_chances),
        either(room.far_mixed, room.near_mixed),
    )
    packet.stash(decoder_inward=inward, decoder_outward=outward)
    room.d_inputs[...] = grad_inputs.astype(BF)


def encoder_back_body(room, packet):
    gain = room.encoder_gain
    grad_sum, gain1, shift1 = norm_back(
        room.grad_memory[...].astype(F32), room.e_unit1[...], room.e_scale1[:, :1], gain[1:2]
    )
    grad_low = grad_sum.astype(BF)
    grad_before = widen_backward(grad_low, room.encoder_narrow, room.e_slope)
    packet.stash(
        encoder_narrow=(room.e_hidden[...], grad_low), encoder_widen=(room.e_low[...], grad_before)
    )
    grad_normed = grad_sum + matmul_back(grad_before, room.encoder_widen[...])
    either = room.either
    grad_sum, gain0, shift0 = norm_back(
        grad_normed,
        either(room.near_unit, room.far_unit),
        either(room.near_scale, room.far_scale)[:, :1],
        gain[0:1],
    )
    inner, outer = room.d_small01[...], room.d_small2[...]
    small = jnp.concatenate(
        [gain0, gain1, shift0, shift1, inner[0:2], outer[0:1], inner[2:4], outer[1:2]]
        + [jnp.zeros((6, inner.shape[1]), F32)],
        0,
    )
    for place, tile in enumerate(tiles_of(small.astype(BF))):
        top = packet.left + packet.extra_at + 16 * place
        packet.send[top : top + 16] = tile
    (inward, outward), grad_inputs = self_back(
        grad_sum,
        room.encoder_inward,
        room.encoder_outward,
        room.tokens[...],
        either(room.near_projected, room.far_projected),
        either(room.near_chances, room.far_chances),
        either(room.near_mixed, room.far_mixed),
    )
    packet.stash(encoder_inward=inward, encoder_outward=outward)
    here, there = grad_inputs.astype(BF), room.d_inputs[...]
    room.sides_mine[0] = either(room.memory, room.output)
    room.sides_mine[1] = jnp.where(room.section == 0, here, there)
    room.sides_theirs[0] = either(room.output, room.memory)
    room.sides_theirs[1] = jnp.where(room.section == 0, there, here)


class Line:
    def __init__(self):
        self.last = None

    def after(self, *values):
        if self.last is None:
            return values
        return lax.optimization_barrier((values, self.last))[0]

    def mark(self, value):
        self.last = value


def pair_swap(value, axis, apart):
    count = lax.axis_size(axis)
    return lax.ppermute(value, axis, [(i, i ^ apart) for i in range(count)])


def halve(kept, came, following):
    count, height = kept.shape[0] // 2, kept.shape[1]
    half = pltpu.VMEM((count, height, SLAB), BF)

    def kernel(kept_ref, came_ref, kept_out, sent_out):
        section, row = lax.axis_index("section"), lax.axis_index("rows")
        bits = [bit_of(step, section, row) for step in following]
        mine = jnp.where(row & 1 == 0, bits[0], bits[1])
        for which, out in ((1 - mine, sent_out), (mine, kept_out)):
            part = pl.ds(which * count, count)
            out[...] = (kept_ref[part].astype(F32) + came_ref[part].astype(F32)).astype(BF)

    return pl.pallas_call(
        kernel,
        out_shape=[half, half],
        in_specs=[VMEM] * 2,
        out_specs=[VMEM] * 2,
        compiler_params=pltpu.CompilerParams(vmem_limit_bytes=4 << 20),
        cost_estimate=lasting(2),
    )(pinned(kept), pinned(came))


class Team:
    def __init__(self, line, orders, small=False, **weights):
        self.line, self.orders, self.small = line, orders, small
        self.shapes = {name: array.shape for name, array in weights.items()}
        self.even = lax.axis_size("rows") == GROUPS
        self.turn = 0
        self.done = {}

    def grads(self, *parcels):
        tied = self.line.after(*(parts for unused, parts in parcels))
        parcels = [(packet, *parts) for (packet, unused), parts in zip(parcels, tied)]
        self.kept, self.sent = weight_grads(
            parcels, list(self.shapes), self.orders, self.even, self.small
        )
        self.line.mark(self.sent)
        if self.even:
            self.go()

    def go(self):
        pieces = lax.axis_size("rows")
        route = []
        for device in range(2 * pieces):
            step = self.orders[device & 1][self.turn]
            route.append((device, device ^ (pieces if step == SIDE else 1 << step)))
        self.came = lax.ppermute(self.sent, ("section", "rows"), route)

    def step(self):
        if not self.even:
            return
        self.turn += 1
        kept, came = self.line.after(self.kept, self.came)
        following = [order[self.turn] for order in self.orders]
        self.kept, self.sent = halve(kept, came, following)
        self.line.mark(self.sent)
        self.go()

    def end(self):
        pieces = lax.axis_size("rows")
        if not self.even:
            return self.end_uneven()
        kept, came = self.line.after(self.kept, self.came)
        shapes = list(self.shapes.values())
        outs = [jax.ShapeDtypeStruct((depth // pieces, width // 2), F32) for depth, width in shapes]
        counts = (2, 2, 3, 3) if self.small else ()
        lanes = 512 // pieces
        outs += [jax.ShapeDtypeStruct((count, lanes), F32) for count in counts]

        def kernel(kept_ref, came_ref, *out_refs):
            top = 0
            for (depth, width), out_ref in zip(shapes, out_refs):
                share = depth // pieces
                for at in range(0, width // 2, SLAB):
                    rows = slice(top, top + share)
                    out_ref[:, at : at + SLAB] = kept_ref[0, rows].astype(F32) + came_ref[
                        0, rows
                    ].astype(F32)
                    top += share
            if counts:
                rows = slice(top, top + 16)
                total = kept_ref[0, rows].astype(F32) + came_ref[0, rows].astype(F32)
                top = 0
                for count, out_ref in zip(counts, out_refs[len(shapes) :]):
                    out_ref[...] = total[top : top + count, :lanes]
                    top += count

        results = pl.pallas_call(
            kernel,
            out_shape=outs,
            in_specs=[VMEM] * 2,
            out_specs=[VMEM] * len(outs),
            compiler_params=pltpu.CompilerParams(vmem_limit_bytes=8 << 20),
            cost_estimate=lasting(1.6),
        )(pinned(kept), pinned(came))
        self.line.mark(results[0])
        self.done = dict(zip(self.shapes, results))
        self.shares = results[len(shapes) :]

    def spread(self, top, count, share):
        core = lax.axis_index("rows") & 1
        both = jnp.stack([self.kept, self.sent])[:, :, top : top + count * share].astype(F32)
        both = both.reshape(2, 2, 2, 2, count, share, SLAB)
        both = both.transpose(0, 3, 2, 1, 5, 4, 6)
        both = both.reshape(2, GROUPS // 2, 1, share, count * SLAB)
        held = jnp.concatenate([both * (core == 0), both * (core == 1)], 2)
        return held.reshape(2, GROUPS, share, count * SLAB)

    def end_uneven(self):
        pieces = lax.axis_size("rows")
        top = 0
        for name, (depth, width) in self.shapes.items():
            share, count = depth // GROUPS, width // (2 * SLAB)
            part = self.spread(top, count, share).reshape(2, depth, width // 2)
            part = lax.psum_scatter(part, "rows", scatter_dimension=1, tiled=True)
            self.done[name] = lax.psum_scatter(part, "section", scatter_dimension=0, tiled=True)[0]
            top += count * share
        if self.small:
            width = 512
            part = self.spread(top, 1, 16)[0, :, :10, : width // GROUPS]
            part = lax.psum(jnp.moveaxis(part, 1, 0).reshape(10, width), ("section", "rows"))
            start = lax.axis_index("rows") * (width // pieces)
            part = lax.dynamic_slice_in_dim(part, start, width // pieces, 1)
            self.shares = (part[0:2], part[2:4], part[4:7], part[7:10])


SIDE = 0
XYZ, YXZ = (SIDE, 1, 2, 3), (1, SIDE, 2, 3)
XZY, YZX = (SIDE, 2, 3, 1), (1, 2, 3, SIDE)
ZXY, ZYX = (2, 3, SIDE, 1), (2, 3, 1, SIDE)
W_ORDERS = (YXZ, ZXY)
Q_ORDERS = (ZYX, YXZ)
E_ORDERS = (XYZ, YXZ)
S_ORDERS = (ZXY, YZX)


def per_device(
    section_input,
    segments,
    cotangent,
    encoder_inward,
    encoder_outward,
    encoder_widen,
    encoder_narrow,
    encoder_gain,
    encoder_shift,
    decoder_inward,
    decoder_outward,
    decoder_cross_query,
    decoder_cross_memory,
    decoder_cross_outward,
    decoder_widen,
    decoder_narrow,
    decoder_gain,
    decoder_shift,
):
    section = lax.axis_index("section")
    own = section_input[0]
    length, width = own.shape[1:]
    wide = encoder_widen.shape[1]

    def low(*shape):
        return jax.ShapeDtypeStruct(shape, BF)

    def full(*shape):
        return jax.ShapeDtypeStruct(shape, F32)

    slabs, units, scales = low(length, width), full(length, width), full(length, LANES)
    chances = full(width // SLAB, PER_SLAB * length, length)
    attended = dict(
        projected=low(length, 3 * width), chances=chances, mixed=slabs, unit=units, scale=scales
    )
    line = Line()

    def run(body, inputs, near, outputs, loads, span, limit, packet=None, extra=None):
        near = dict(near)
        for name in list(near)[:1]:
            (near[name],) = line.after(near[name])
        kept, leaving = call(
            body if packet is None else (lambda room: body(room, packet)),
            inputs,
            near,
            outputs,
            loads,
            span,
            limit,
            packet,
            extra,
        )
        line.mark(list(vars(kept).values())[0])
        if packet is None:
            return kept
        return kept, leaving + (pair_swap(leaving[1], "rows", 1),)

    other = pair_swap(
        lax.dynamic_index_in_dim(own, 1 - section, 0, keepdims=False), "section", 1
    )
    near = run(
        own_body,
        dict(
            segments=segments,
            tokens=Entry(own),
            inward=Either(encoder_inward, decoder_inward),
            encoder_gain=encoder_gain,
            decoder_gain=decoder_gain,
            encoder_shift=encoder_shift,
            decoder_shift=decoder_shift,
            outward=Either(encoder_outward, decoder_outward),
        ),
        {},
        dict(first=units, **attended),
        {},
        4,
        8,
    )

    wide_packet = Packet(decoder_narrow=decoder_narrow, decoder_widen=decoder_widen)
    far, d_wide = run(
        forward_body,
        dict(
            segments=segments,
            tokens=other,
            inward=Either(decoder_inward, encoder_inward),
            decoder_gain=decoder_gain,
            encoder_shift=encoder_shift,
            decoder_shift=decoder_shift,
            outward=Either(decoder_outward, encoder_outward),
            decoder_widen=decoder_widen,
            decoder_narrow=decoder_narrow,
            cotangent=Entry(cotangent),
        ),
        dict(own_first=near.first),
        dict(
            memory=slabs,
            output=slabs,
            **attended,
            e_low=slabs,
            e_hidden=low(length, wide),
            e_slope=full(length, wide),
            e_unit1=units,
            e_scale1=scales,
            d_low=slabs,
            c_query=slabs,
            c_paired=low(length, 2 * width),
            c_chances=chances,
            c_mixed=slabs,
            d_unit1=units,
            d_scale1=scales,
            d_grad=units,
            d_small2=full(2, width),
        ),
        dict(
            encoder_gain=encoder_gain,
            encoder_widen=encoder_widen,
            encoder_narrow=encoder_narrow,
            decoder_cross_query=decoder_cross_query,
            decoder_cross_memory=decoder_cross_memory,
            decoder_cross_outward=decoder_cross_outward,
            decoder_outward=decoder_outward,
            decoder_inward=decoder_inward,
            encoder_outward=encoder_outward,
            encoder_inward=encoder_inward,
        ),
        11,
        24,
        wide_packet,
        dict(d_hidden=low(length, wide), d_slope=full(length, wide)),
    )

    cross_packet = Packet(
        decoder_cross_query=decoder_cross_query,
        decoder_cross_memory=decoder_cross_memory,
        decoder_cross_outward=decoder_cross_outward,
    )
    crossed, d_cross = run(
        cross_back_body,
        dict(decoder_gain=decoder_gain),
        dict(
            d_grad=far.d_grad,
            d_unit1=far.d_unit1,
            d_scale1=far.d_scale1,
            c_query=far.c_query,
            c_paired=far.c_paired,
            c_chances=far.c_chances,
            d_low=far.d_low,
            memory=far.memory,
            c_mixed=far.c_mixed,
            decoder_cross_outward=far.decoder_cross_outward,
            decoder_cross_memory=far.decoder_cross_memory,
            decoder_cross_query=far.decoder_cross_query,
            near_unit=near.unit,
            near_scale=near.scale,
            far_unit=far.unit,
            far_scale=far.scale,
        ),
        dict(grad_memory=slabs, d_grad0=units, d_small01=full(4, width)),
        {},
        4.7,
        8,
        cross_packet,
    )

    def d_self_run():
        packet = Packet(decoder_inward=decoder_inward, decoder_outward=decoder_outward)
        return packet, *run(
            decoder_self_body,
            dict(tokens=Either(other, (own, 1))),
            dict(
                d_grad0=crossed.d_grad0,
                decoder_outward=far.decoder_outward,
                decoder_inward=far.decoder_inward,
                near_projected=near.projected,
                near_chances=near.chances,
                near_mixed=near.mixed,
                far_projected=far.projected,
                far_chances=far.chances,
                far_mixed=far.mixed,
            ),
            dict(d_inputs=slabs),
            {},
            5,
            8,
            packet,
        )

    def encoder_run(d_inputs):
        packet = Packet(
            64,
            encoder_narrow=encoder_narrow,
            encoder_widen=encoder_widen,
            encoder_inward=encoder_inward,
            encoder_outward=encoder_outward,
        )
        sides = low(2, length, width)
        return packet, *run(
            encoder_back_body,
            dict(tokens=Either((own, 0), other)),
            dict(
                encoder_gain=far.encoder_gain,
                grad_memory=crossed.grad_memory,
                e_unit1=far.e_unit1,
                e_scale1=far.e_scale1,
                encoder_narrow=far.encoder_narrow,
                e_slope=far.e_slope,
                e_hidden=far.e_hidden,
                e_low=far.e_low,
                encoder_widen=far.encoder_widen,
                d_small01=crossed.d_small01,
                d_small2=far.d_small2,
                encoder_outward=far.encoder_outward,
                encoder_inward=far.encoder_inward,
                near_unit=near.unit,
                near_scale=near.scale,
                near_projected=near.projected,
                near_chances=near.chances,
                near_mixed=near.mixed,
                far_unit=far.unit,
                far_scale=far.scale,
                far_projected=far.projected,
                far_chances=far.chances,
                far_mixed=far.mixed,
                d_inputs=d_inputs,
                memory=far.memory,
                output=far.output,
            ),
            dict(sides_mine=sides, sides_theirs=sides),
            {},
            8,
            12,
            packet,
        )

    team_w = Team(line, W_ORDERS, decoder_narrow=decoder_narrow, decoder_widen=decoder_widen)
    team_q = Team(
        line,
        Q_ORDERS,
        decoder_cross_query=decoder_cross_query,
        decoder_cross_memory=decoder_cross_memory,
        decoder_cross_outward=decoder_cross_outward,
        decoder_inward=decoder_inward,
        decoder_outward=decoder_outward,
    )
    team_e = Team(line, E_ORDERS, encoder_narrow=encoder_narrow, encoder_widen=encoder_widen)
    team_s = Team(
        line, S_ORDERS, True, encoder_inward=encoder_inward, encoder_outward=encoder_outward
    )
    team_w.grads((wide_packet, d_wide))
    self_packet, turned, d_self = d_self_run()
    encoder_packet, ended, e_all = encoder_run(turned.d_inputs)
    team_q.grads((cross_packet, d_cross), (self_packet, d_self))
    (theirs,) = line.after(ended.sides_theirs)
    theirs = pair_swap(theirs, "section", 1)
    team_e.grads((encoder_packet, e_all))
    team_w.step()
    team_q.step()
    team_s.grads((encoder_packet, e_all))
    team_e.step()
    team_w.step()
    team_s.step()
    team_q.step()
    team_e.step()
    team_w.step()
    team_s.step()
    team_q.step()
    team_e.step()
    team_s.step()
    mine, theirs = line.after(ended.sides_mine, theirs)
    results, gradients = (
        jnp.stack(
            [
                jnp.where(section == 0, mine[i], theirs[i]),
                jnp.where(section == 0, theirs[i], mine[i]),
            ]
        )[None]
        for i in (0, 1)
    )
    line.mark(gradients)
    team_w.end()
    team_q.end()
    team_s.end()
    team_e.end()

    done = {}
    for team in (team_w, team_q, team_e, team_s):
        done.update(team.done)
    deltas = SimpleNamespace(**done)
    shares = team_s.shares
    return (
        results,
        gradients,
        deltas.encoder_inward,
        deltas.encoder_outward,
        deltas.encoder_widen,
        deltas.encoder_narrow,
        shares[0],
        shares[1],
        deltas.decoder_inward,
        deltas.decoder_outward,
        deltas.decoder_cross_query,
        deltas.decoder_cross_memory,
        deltas.decoder_cross_outward,
        deltas.decoder_widen,
        deltas.decoder_narrow,
        shares[2],
        shares[3],
    )


def solution(mesh):
    weights = (P(),) * 15
    shares = P("rows", "section")
    small = P(None, "rows")
    sides = P("section", None, "rows", None)
    return jax.shard_map(
        per_device,
        mesh=mesh,
        in_specs=(sides, P(None, None, "rows", None), P(None, "rows", None)) + weights,
        out_specs=(sides, sides)
        + (shares,) * 4
        + (small,) * 2
        + (shares,) * 7
        + (small,) * 2,
        check_vma=False,
    )
```

time: 736 us -> 106 us (0.14)
  the two profiles are of different devices: /device:TPU:0 before, /device:TPU:1 now
where the time goes in v2:
time: 106 us
  waiting for transfers between devices  37.1 us (35%)
  Pallas kernels  34.8 us (33%)
  starting transfers between devices  28.7 us (27%)
  other arithmetic  2.46 us (2%)
  local copies, waits for them, and re-layouts  1.57 us (1%)
    ppermute x16, waiting for transfers between devices, go(): self.came = lax.ppermute(self.sent, ('section', 'rows'), route)  37.1 us
    pallas_call x5, Pallas kernels, call(): pl.pallas_call(kernel, out_shape=shapes_out, in_specs=[HBM] * len(arrays)...  24.3 us
    ppermute x16, starting transfers between devices, go(): self.came = lax.ppermute(self.sent, ('section', 'rows'), route)  23.1 us
    ppermute x6, starting transfers between devices, pair_swap(): return lax.ppermute(value, axis, [(i, i ^ apart) for i in range(count)])  5.65 us
    pallas_call x4, Pallas kernels, weight_grads(): pl.pallas_call(kernel, out_shape=[half, half], in_specs=[VMEM] * len(arra...  4.99 us
    pallas_call x4, Pallas kernels, end(): pl.pallas_call(kernel, out_shape=outs, in_specs=[VMEM] * 2, out_specs=[VM...  2.81 us
    pallas_call x12, Pallas kernels, halve(): pl.pallas_call(kernel, out_shape=[half, half], in_specs=[VMEM] * 2, out_s...  2.74 us
  transfers between devices with their start and end apart: 22, of which 7 were waited for; matrix products, arithmetic and copies ran while one was open for 2% of the time, Pallas kernels for 22%

profile of v2, /device:TPU:1, one launch (start us, length us, event | category | flops | bytes accessed | tf_op | source)
XLA Modules:
  0.0 105.5 jit_solution(16278578649128693758)
XLA Ops:
  1.6 2.1 %collective-permute-start = (bf16[128,512]{1,0:T(8,128)(2,1)S(1)}, bf16[128,512]{1,0:T(8,128)(2,1)S(1)}, u32[]{:S(2)}, u32[]{:S(2)}) collective-permute-start(bf16[128,512]{1,0:T(8,128)(2,1)S(1)} %dynamic-slice_bitcast_fusion), channel_id=1, source_target_pairs={{0,16},{16,0},{1,17},{17,1},{2,18},{18,2},{3,19},{19,3},{4,20},{20... | collective-permute-start | bytes 393224 | tf_op jit(solution)/shard_map/ppermute | solution.py:614
  3.7 3.2 %shard_map.305 = (f32[128,512]{1,0:T(8,128)S(1)}, bf16[128,1536]{1,0:T(8,128)(2,1)S(1)}, f32[2,512,128]{2,1,0:T(8,128)S(1)}, bf16[128,512]{1,0:T(8,128)(2,1)S(1)...) custom-call(s32[2,2,1,128]{3,2,1,0:T(1,128)} %refs_0_.4, bf16[2,128,512]{2,1,0:T(8,128)(2,1)} %bitcast.7, ...), custom_call_target="tpu_custom_call" | custom-call | flops 32000000000 | bytes 1 | tf_op jit(solution)/shard_map/pallas_call | solution.py:270
  7.6 10.9 %shard_map.306 = (bf16[128,512]{1,0:T(8,128)(2,1)S(1)}, bf16[128,512]{1,0:T(8,128)(2,1)S(1)}, bf16[128,1536]{1,0:T(8,128)(2,1)S(1)}, f32[2,512,128]{2,1,0:T(8,12...) custom-call(s32[2,2,1,128]{3,2,1,0:T(1,128)} %refs_0_.4, ...), custom_call_target="tpu_custom_call" | custom-call | flops 88000004096 | bytes 1 | tf_op jit(solution)/shard_map/pallas_call | solution.py:270
  19.8 2.5 %shard_map.307 = (bf16[128,512]{1,0:T(8,128)(2,1)S(1)}, f32[128,512]{1,0:T(8,128)S(1)}, f32[4,512]{1,0:T(4,128)S(1)}, bf16[768,128]{1,0:T(8,128)(2,1)S(1)}, bf16[2816,128]{1,0:T(8,128)(2,1)S(1)}) custom-call(f32[3,512]{1,0:T(4,128)} %refs_0_.5, f32[128,512]{1,0:T(8,128)S(1)} %get-tuple-element.172.refs_1_, f32[128,512]{1,0:T(8,128)S(1)} %get-tuple-element.173.refs_2_, ...), custom_call_target="tpu_custom_call" | custom-call | flops 37600002048 | bytes 1 | tf_op jit(solution)/shard_map/pallas_call | solution.py:270
  22.4 2.1 %shard_map.308 = (bf16[8,256,256]{2,1,0:T(8,128)(2,1)S(1)}, bf16[8,256,256]{2,1,0:T(8,128)(2,1)}) custom-call(bf16[1280,128]{1,0:T(8,128)(2,1)S(1)} %get-tuple-element.191.refs_0_, bf16[3840,128]{1,0:T(8,128)(2,1)S(1)} %get-tuple-element.192.refs_1_, bf16[3840,128]{1,0:T(8,128)(2,1)S(1)} %collective-permute-done.1.refs_2_), custom_call_target="tpu_custom_call" | custom-call | flops 28000000000 | bytes 1 | tf_op jit(solution)/shard_map/pallas_call | solution.py:369
  24.5 1.5 %collective-permute-start.7 = (bf16[8,256,256]{2,1,0:T(8,128)(2,1)}, bf16[8,256,256]{2,1,0:T(8,128)(2,1)}, u32[]{:S(2)}, u32[]{:S(2)}) collective-permute-start(bf16[8,256,256]{2,1,0:T(8,128)(2,1)} %get-tuple-element.194), channel_id=1, source_target_pairs={{0,2},{1,5},{2,0},{3,7},{4,6},{5,1},{6,4},{7,3},{8,10},{9,13},{10,... | collective-permute-start | bytes 3145736 | tf_op jit(solution)/shard_map/ppermute | solution.py:663
  26.0 2.6 %shard_map.309 = (bf16[128,512]{1,0:T(8,128)(2,1)S(1)}, bf16[512,128]{1,0:T(8,128)(2,1)S(1)}, bf16[2560,128]{1,0:T(8,128)(2,1)S(1)}) custom-call(bf16[128,512]{1,0:T(8,128)(2,1)} %copy-done, bf16[2,128,512]{2,1,0:T(8,128)(2,1)} %bitcast.8, f32[128,512]{1,0:T(8,128)S(1)} %get-tuple-element.195.refs_2_, bf16[512,512]{1,0:T(8,128)(2,1)S(1)} %get-tuple-element.196.refs_3_, ...), custom_call_target="tpu_custom_call" | custom-call | flops 40000000000 | bytes 1 | tf_op jit(solution)/shard_map/pallas_call | solution.py:270
  29.4 5.0 %shard_map.310 = (bf16[2,128,512]{2,1,0:T(8,128)(2,1)S(1)}, bf16[2,128,512]{2,1,0:T(8,128)(2,1)}, bf16[1792,128]{1,0:T(8,128)(2,1)S(1)}, bf16[6464,128]{1,0:T(8,128)(2,1)S(1)}) custom-call(bf16[2,128,512]{2,1,0:T(8,128)(2,1)} %bitcast.9, bf16[128,512]{1,0:T(8,128)(2,1)} %copy-done, f32[2,512]{1,0:T(2,128)S(1)} %get-tuple-element.205.refs_2_, ...), custom_call_target="tpu_custom_call" | custom-call | flops 64000000000 | bytes 1 | tf_op jit(solution)/shard_map/pallas_call | solution.py:270
  39.9 1.5 %shard_map.313 = (bf16[4,256,256]{2,1,0:T(8,128)(2,1)S(1)}, bf16[4,256,256]{2,1,0:T(8,128)(2,1)S(1)}) custom-call(bf16[8,256,256]{2,1,0:T(8,128)(2,1)S(1)} %get-tuple-element.240.kept_ref, bf16[8,256,256]{2,1,0:T(8,128)(2,1)} %collective-permute-done.7.came_ref), custom_call_target="tpu_custom_call" | custom-call | flops 16000000000 | bytes 1 | tf_op jit(solution)/shard_map/pallas_call | solution.py:629
  41.4 2.4 %collective-permute-start.9 = (bf16[4,256,256]{2,1,0:T(8,128)(2,1)S(1)}, bf16[4,256,256]{2,1,0:T(8,128)(2,1)S(1)}, u32[]{:S(2)}, u32[]{:S(2)}) collective-permute-start(bf16[4,256,256]{2,1,0:T(8,128)(2,1)S(1)} %get-tuple-element.242), channel_id=1, source_target_pairs={{0,16},{1,9},{2,18},{3,11},{4,20},{5,13},{6,22},{7,15},{8,24},{9,1... | collective-permute-start | bytes 1572872 | tf_op jit(solution)/shard_map/ppermute | solution.py:663
  43.8 7.1 %collective-permute-done.6.came_ref = bf16[8,256,256]{2,1,0:T(8,128)(2,1)S(1)} collective-permute-done((bf16[8,256,256]{2,1,0:T(8,128)(2,1)S(1)}, bf16[8,256,256]{2,1,0:T(8,128)(2,1)S(1)}, u32[]{:S(2)}, u32[]{:S(2)}) %collective-permute-start.6) | collective-permute-done | bytes 1048608 | tf_op jit(solution)/shard_map/ppermute | solution.py:663
  51.1 1.5 %collective-permute-start.14 = (bf16[4,256,256]{2,1,0:T(8,128)(2,1)S(1)}, bf16[4,256,256]{2,1,0:T(8,128)(2,1)S(1)}, u32[]{:S(2)}, u32[]{:S(2)}) collective-permute-start(bf16[4,256,256]{2,1,0:T(8,128)(2,1)S(1)} %get-tuple-element.245), channel_id=1, source_target_pairs={{0,8},{1,17},{2,10},{3,19},{4,12},{5,21},{6,14},{7,23},{8,0},{9,25... | collective-permute-start | bytes 1572872 | tf_op jit(solution)/shard_map/ppermute | solution.py:663
  54.5 7.6 %collective-permute-done.10.came_ref = bf16[8,256,256]{2,1,0:T(8,128)(2,1)S(1)} collective-permute-done((bf16[8,256,256]{2,1,0:T(8,128)(2,1)S(1)}, bf16[8,256,256]{2,1,0:T(8,128)(2,1)S(1)}, u32[]{:S(2)}, u32[]{:S(2)}) %collective-permute-start.10) | collective-permute-done | bytes 1048608 | tf_op jit(solution)/shard_map/ppermute | solution.py:663
  62.3 1.5 %collective-permute-start.13 = (bf16[4,256,256]{2,1,0:T(8,128)(2,1)S(1)}, bf16[4,256,256]{2,1,0:T(8,128)(2,1)S(1)}, u32[]{:S(2)}, u32[]{:S(2)}) collective-permute-start(bf16[4,256,256]{2,1,0:T(8,128)(2,1)S(1)} %get-tuple-element.255), channel_id=1, source_target_pairs={{0,2},{1,17},{2,0},{3,19},{4,6},{5,21},{6,4},{7,23},{8,10},{9,25},... | collective-permute-start | bytes 1572872 | tf_op jit(solution)/shard_map/ppermute | solution.py:663
  64.1 7.6 %collective-permute-done.8.came_ref = bf16[8,144,256]{2,1,0:T(8,128)(2,1)S(1)} collective-permute-done((bf16[8,144,256]{2,1,0:T(8,128)(2,1)S(1)}, bf16[8,144,256]{2,1,0:T(8,128)(2,1)S(1)}, u32[]{:S(2)}, u32[]{:S(2)}) %collective-permute-start.8) | collective-permute-done | bytes 589856 | tf_op jit(solution)/shard_map/ppermute | solution.py:663
  71.8 2.7 %collective-permute-start.11 = (bf16[4,144,256]{2,1,0:T(8,128)(2,1)S(1)}, bf16[4,144,256]{2,1,0:T(8,128)(2,1)S(1)}, u32[]{:S(2)}, u32[]{:S(2)}) collective-permute-start(bf16[4,144,256]{2,1,0:T(8,128)(2,1)S(1)} %get-tuple-element.262), channel_id=1, source_target_pairs={{0,8},{1,5},{2,10},{3,7},{4,12},{5,1},{6,14},{7,3},{8,0},{9,13},{1... | collective-permute-start | bytes 884744 | tf_op jit(solution)/shard_map/ppermute | solution.py:663
  74.9 1.5 %collective-permute-start.16 = (bf16[2,256,256]{2,1,0:T(8,128)(2,1)S(1)}, bf16[2,256,256]{2,1,0:T(8,128)(2,1)S(1)}, u32[]{:S(2)}, u32[]{:S(2)}) collective-permute-start(bf16[2,256,256]{2,1,0:T(8,128)(2,1)S(1)} %get-tuple-element.271), channel_id=1, source_target_pairs={{0,4},{1,5},{2,6},{3,7},{4,0},{5,1},{6,2},{7,3},{8,12},{9,13},{10,... | collective-permute-start | bytes 786440 | tf_op jit(solution)/shard_map/ppermute | solution.py:663
  76.4 1.8 %collective-permute-start.20 = (bf16[1,256,256]{2,1,0:T(8,128)(2,1)S(1)}, bf16[1,256,256]{2,1,0:T(8,128)(2,1)S(1)}, u32[]{:S(2)}, u32[]{:S(2)}) collective-permute-start(bf16[1,256,256]{2,1,0:T(8,128)(2,1)S(1)} %get-tuple-element.274), channel_id=1, source_target_pairs={{0,8},{1,3},{2,10},{3,1},{4,12},{5,7},{6,14},{7,5},{8,0},{9,11},{1... | collective-permute-start | bytes 393224 | tf_op jit(solution)/shard_map/ppermute | solution.py:663
  78.2 5.2 %collective-permute-done.11.came_ref = bf16[4,144,256]{2,1,0:T(8,128)(2,1)S(1)} collective-permute-done((bf16[4,144,256]{2,1,0:T(8,128)(2,1)S(1)}, bf16[4,144,256]{2,1,0:T(8,128)(2,1)S(1)}, u32[]{:S(2)}, u32[]{:S(2)}) %collective-permute-start.11) | collective-permute-done | bytes 294944 | tf_op jit(solution)/shard_map/ppermute | solution.py:663
  83.5 5.1 %collective-permute-start.15 = (bf16[2,144,256]{2,1,0:T(8,128)(2,1)S(1)}, bf16[2,144,256]{2,1,0:T(8,128)(2,1)S(1)}, u32[]{:S(2)}, u32[]{:S(2)}) collective-permute-start(bf16[2,144,256]{2,1,0:T(8,128)(2,1)S(1)} %get-tuple-element.278), channel_id=1, source_target_pairs={{0,16},{1,9},{2,18},{3,11},{4,20},{5,13},{6,22},{7,15},{8,24},{9,1... | collective-permute-start | bytes 442376 | tf_op jit(solution)/shard_map/ppermute | solution.py:663
  88.6 3.4 %collective-permute-done.17.came_ref = bf16[2,256,256]{2,1,0:T(8,128)(2,1)S(1)} collective-permute-done((bf16[2,256,256]{2,1,0:T(8,128)(2,1)S(1)}, bf16[2,256,256]{2,1,0:T(8,128)(2,1)S(1)}, u32[]{:S(2)}, u32[]{:S(2)}) %collective-permute-start.17) | collective-permute-done | bytes 262176 | tf_op jit(solution)/shard_map/ppermute | solution.py:663
  92.2 3.4 %collective-permute-done.16.came_ref = bf16[2,256,256]{2,1,0:T(8,128)(2,1)S(1)} collective-permute-done((bf16[2,256,256]{2,1,0:T(8,128)(2,1)S(1)}, bf16[2,256,256]{2,1,0:T(8,128)(2,1)S(1)}, u32[]{:S(2)}, u32[]{:S(2)}) %collective-permute-start.16) | collective-permute-done | bytes 262176 | tf_op jit(solution)/shard_map/ppermute | solution.py:663
  96.0 1.4 %collective-permute-start.18 = (bf16[1,144,256]{2,1,0:T(8,128)(2,1)S(1)}, bf16[1,144,256]{2,1,0:T(8,128)(2,1)S(1)}, u32[]{:S(2)}, u32[]{:S(2)}) collective-permute-start(bf16[1,144,256]{2,1,0:T(8,128)(2,1)S(1)} %get-tuple-element.289), channel_id=1, source_target_pairs={{0,2},{1,17},{2,0},{3,19},{4,6},{5,21},{6,4},{7,23},{8,10},{9,25},... | collective-permute-start | bytes 221192 | tf_op jit(solution)/shard_map/ppermute | solution.py:663
  99.9 2.8 %collective-permute-done.19.came_ref = bf16[1,256,256]{2,1,0:T(8,128)(2,1)S(1)} collective-permute-done((bf16[1,256,256]{2,1,0:T(8,128)(2,1)S(1)}, bf16[1,256,256]{2,1,0:T(8,128)(2,1)S(1)}, u32[]{:S(2)}, u32[]{:S(2)}) %collective-permute-start.19) | collective-permute-done | bytes 131104 | tf_op jit(solution)/shard_map/ppermute | solution.py:663
  (51 shorter events, 18.2 us)
Async XLA Ops:
  1.6 5.3 %collective-permute-start = (bf16[128,512]{1,0:T(8,128)(2,1)S(1)}, bf16[128,512]{1,0:T(8,128)(2,1)S(1)}, u32[]{:S(2)}, u32[]{:S(2)}) collective-permute-start(bf16[128,512]{1,0:T(8,128)(2,1)S(1)} %dynamic-slice_bitcast_fusion), channel_id=1, source_target_pairs={{0,16},{16,0},{1,17},{17,1},{2,18},{18,2},{3,19},{19,3},{4,20},{20... | collective-permute-start | bytes 393224 | tf_op jit(solution)/shard_map/ppermute | solution.py:614
  6.9 0.7 copy-start
  18.5 3.9 %collective-permute-start.1 = (bf16[3840,128]{1,0:T(8,128)(2,1)S(1)}, bf16[3840,128]{1,0:T(8,128)(2,1)S(1)}, u32[]{:S(2)}, u32[]{:S(2)}) collective-permute-start(bf16[3840,128]{1,0:T(8,128)(2,1)S(1)} %get-tuple-element.192.refs_1_), channel_id=1, source_target_pairs={{0,1},{1,0},{2,3},{3,2},{4,5},{5,4},{6,7},{7,6},{8,9},{9,8},{10,11... | collective-permute-start | bytes 2949128 | tf_op jit(solution)/shard_map/ppermute | solution.py:614
  22.3 12.3 %collective-permute-start.2 = (bf16[2816,128]{1,0:T(8,128)(2,1)S(1)}, bf16[2816,128]{1,0:T(8,128)(2,1)S(1)}, u32[]{:S(2)}, u32[]{:S(2)}) collective-permute-start(bf16[2816,128]{1,0:T(8,128)(2,1)S(1)} %get-tuple-element.225.refs_1_), channel_id=1, source_target_pairs={{0,1},{1,0},{2,3},{3,2},{4,5},{5,4},{6,7},{7,6},{8,9},{9,8},{10,11... | collective-permute-start | bytes 2162696 | tf_op jit(solution)/shard_map/ppermute | solution.py:614
  24.5 15.4 %collective-permute-start.7 = (bf16[8,256,256]{2,1,0:T(8,128)(2,1)}, bf16[8,256,256]{2,1,0:T(8,128)(2,1)}, u32[]{:S(2)}, u32[]{:S(2)}) collective-permute-start(bf16[8,256,256]{2,1,0:T(8,128)(2,1)} %get-tuple-element.194), channel_id=1, source_target_pairs={{0,2},{1,5},{2,0},{3,7},{4,6},{5,1},{6,4},{7,3},{8,10},{9,13},{10,... | collective-permute-start | bytes 3145736 | tf_op jit(solution)/shard_map/ppermute | solution.py:663
  28.6 5.9 %collective-permute-start.3 = (bf16[2560,128]{1,0:T(8,128)(2,1)S(1)}, bf16[2560,128]{1,0:T(8,128)(2,1)S(1)}, u32[]{:S(2)}, u32[]{:S(2)}) collective-permute-start(bf16[2560,128]{1,0:T(8,128)(2,1)S(1)} %get-tuple-element.228.refs_4_), channel_id=1, source_target_pairs={{0,1},{1,0},{2,3},{3,2},{4,5},{5,4},{6,7},{7,6},{8,9},{9,8},{10,11... | collective-permute-start | bytes 1966088 | tf_op jit(solution)/shard_map/ppermute | solution.py:614
  34.5 3.6 %collective-permute-start.5 = (bf16[6464,128]{1,0:T(8,128)(2,1)S(1)}, bf16[6464,128]{1,0:T(8,128)(2,1)S(1)}, u32[]{:S(2)}, u32[]{:S(2)}) collective-permute-start(bf16[6464,128]{1,0:T(8,128)(2,1)S(1)} %get-tuple-element.247.refs_1_), channel_id=1, source_target_pairs={{0,1},{1,0},{2,3},{3,2},{4,5},{5,4},{6,7},{7,6},{8,9},{9,8},{10,11... | collective-permute-start | bytes 4964360 | tf_op jit(solution)/shard_map/ppermute | solution.py:614
  35.7 15.1 %collective-permute-start.6 = (bf16[8,256,256]{2,1,0:T(8,128)(2,1)S(1)}, bf16[8,256,256]{2,1,0:T(8,128)(2,1)S(1)}, u32[]{:S(2)}, u32[]{:S(2)}) collective-permute-start(bf16[8,256,256]{2,1,0:T(8,128)(2,1)S(1)} %get-tuple-element.230), channel_id=1, source_target_pairs={{0,4},{1,3},{2,6},{3,1},{4,0},{5,7},{6,2},{7,5},{8,12},{9,11},{10,... | collective-permute-start | bytes 3145736 | tf_op jit(solution)/shard_map/ppermute | solution.py:663
  36.8 60.6 %collective-permute-start.4 = (bf16[2,128,512]{2,1,0:T(8,128)(2,1)}, bf16[2,128,512]{2,1,0:T(8,128)(2,1)}, u32[]{:S(2)}, u32[]{:S(2)}) collective-permute-start(bf16[2,128,512]{2,1,0:T(8,128)(2,1)} %get-tuple-element.231), channel_id=1, source_target_pairs={{0,16},{16,0},{1,17},{17,1},{2,18},{18,2},{3,19},{19,3},{4,20},{20... | collective-permute-start | bytes 786440 | tf_op jit(solution)/shard_map/ppermute | solution.py:614
  39.2 22.8 %collective-permute-start.10 = (bf16[8,256,256]{2,1,0:T(8,128)(2,1)S(1)}, bf16[8,256,256]{2,1,0:T(8,128)(2,1)S(1)}, u32[]{:S(2)}, u32[]{:S(2)}) collective-permute-start(bf16[8,256,256]{2,1,0:T(8,128)(2,1)S(1)} %get-tuple-element.239), channel_id=1, source_target_pairs={{0,16},{1,3},{2,18},{3,1},{4,20},{5,7},{6,22},{7,5},{8,24},{9,11},... | collective-permute-start | bytes 3145736 | tf_op jit(solution)/shard_map/ppermute | solution.py:663
  41.4 22.4 %collective-permute-start.9 = (bf16[4,256,256]{2,1,0:T(8,128)(2,1)S(1)}, bf16[4,256,256]{2,1,0:T(8,128)(2,1)S(1)}, u32[]{:S(2)}, u32[]{:S(2)}) collective-permute-start(bf16[4,256,256]{2,1,0:T(8,128)(2,1)S(1)} %get-tuple-element.242), channel_id=1, source_target_pairs={{0,16},{1,9},{2,18},{3,11},{4,20},{5,13},{6,22},{7,15},{8,24},{9,1... | collective-permute-start | bytes 1572872 | tf_op jit(solution)/shard_map/ppermute | solution.py:663
  51.1 23.4 %collective-permute-start.14 = (bf16[4,256,256]{2,1,0:T(8,128)(2,1)S(1)}, bf16[4,256,256]{2,1,0:T(8,128)(2,1)S(1)}, u32[]{:S(2)}, u32[]{:S(2)}) collective-permute-start(bf16[4,256,256]{2,1,0:T(8,128)(2,1)S(1)} %get-tuple-element.245), channel_id=1, source_target_pairs={{0,8},{1,17},{2,10},{3,19},{4,12},{5,21},{6,14},{7,23},{8,0},{9,25... | collective-permute-start | bytes 1572872 | tf_op jit(solution)/shard_map/ppermute | solution.py:663
  53.2 18.5 %collective-permute-start.8 = (bf16[8,144,256]{2,1,0:T(8,128)(2,1)S(1)}, bf16[8,144,256]{2,1,0:T(8,128)(2,1)S(1)}, u32[]{:S(2)}, u32[]{:S(2)}) collective-permute-start(bf16[8,144,256]{2,1,0:T(8,128)(2,1)S(1)} %get-tuple-element.250), channel_id=1, source_target_pairs={{0,4},{1,3},{2,6},{3,1},{4,0},{5,7},{6,2},{7,5},{8,12},{9,11},{10,... | collective-permute-start | bytes 1769480 | tf_op jit(solution)/shard_map/ppermute | solution.py:663
  62.3 12.4 %collective-permute-start.13 = (bf16[4,256,256]{2,1,0:T(8,128)(2,1)S(1)}, bf16[4,256,256]{2,1,0:T(8,128)(2,1)S(1)}, u32[]{:S(2)}, u32[]{:S(2)}) collective-permute-start(bf16[4,256,256]{2,1,0:T(8,128)(2,1)S(1)} %get-tuple-element.255), channel_id=1, source_target_pairs={{0,2},{1,17},{2,0},{3,19},{4,6},{5,21},{6,4},{7,23},{8,10},{9,25},... | collective-permute-start | bytes 1572872 | tf_op jit(solution)/shard_map/ppermute | solution.py:663
  64.0 12.4 %collective-permute-start.12 = (bf16[2,256,256]{2,1,0:T(8,128)(2,1)S(1)}, bf16[2,256,256]{2,1,0:T(8,128)(2,1)S(1)}, u32[]{:S(2)}, u32[]{:S(2)}) collective-permute-start(bf16[2,256,256]{2,1,0:T(8,128)(2,1)S(1)} %get-tuple-element.258), channel_id=1, source_target_pairs={{0,4},{1,17},{2,6},{3,19},{4,0},{5,21},{6,2},{7,23},{8,12},{9,25},... | collective-permute-start | bytes 786440 | tf_op jit(solution)/shard_map/ppermute | solution.py:663
  71.8 11.6 %collective-permute-start.11 = (bf16[4,144,256]{2,1,0:T(8,128)(2,1)S(1)}, bf16[4,144,256]{2,1,0:T(8,128)(2,1)S(1)}, u32[]{:S(2)}, u32[]{:S(2)}) collective-permute-start(bf16[4,144,256]{2,1,0:T(8,128)(2,1)S(1)} %get-tuple-element.262), channel_id=1, source_target_pairs={{0,8},{1,5},{2,10},{3,7},{4,12},{5,1},{6,14},{7,3},{8,0},{9,13},{1... | collective-permute-start | bytes 884744 | tf_op jit(solution)/shard_map/ppermute | solution.py:663
  74.6 17.4 %collective-permute-start.17 = (bf16[2,256,256]{2,1,0:T(8,128)(2,1)S(1)}, bf16[2,256,256]{2,1,0:T(8,128)(2,1)S(1)}, u32[]{:S(2)}, u32[]{:S(2)}) collective-permute-start(bf16[2,256,256]{2,1,0:T(8,128)(2,1)S(1)} %get-tuple-element.268), channel_id=1, source_target_pairs={{0,2},{1,5},{2,0},{3,7},{4,6},{5,1},{6,4},{7,3},{8,10},{9,13},{10,... | collective-permute-start | bytes 786440 | tf_op jit(solution)/shard_map/ppermute | solution.py:663
  74.9 20.8 %collective-permute-start.16 = (bf16[2,256,256]{2,1,0:T(8,128)(2,1)S(1)}, bf16[2,256,256]{2,1,0:T(8,128)(2,1)S(1)}, u32[]{:S(2)}, u32[]{:S(2)}) collective-permute-start(bf16[2,256,256]{2,1,0:T(8,128)(2,1)S(1)} %get-tuple-element.271), channel_id=1, source_target_pairs={{0,4},{1,5},{2,6},{3,7},{4,0},{5,1},{6,2},{7,3},{8,12},{9,13},{10,... | collective-permute-start | bytes 786440 | tf_op jit(solution)/shard_map/ppermute | solution.py:663
  76.4 22.7 %collective-permute-start.20 = (bf16[1,256,256]{2,1,0:T(8,128)(2,1)S(1)}, bf16[1,256,256]{2,1,0:T(8,128)(2,1)S(1)}, u32[]{:S(2)}, u32[]{:S(2)}) collective-permute-start(bf16[1,256,256]{2,1,0:T(8,128)(2,1)S(1)} %get-tuple-element.274), channel_id=1, source_target_pairs={{0,8},{1,3},{2,10},{3,1},{4,12},{5,7},{6,14},{7,5},{8,0},{9,11},{1... | collective-permute-start | bytes 393224 | tf_op jit(solution)/shard_map/ppermute | solution.py:663
  83.5 12.5 %collective-permute-start.15 = (bf16[2,144,256]{2,1,0:T(8,128)(2,1)S(1)}, bf16[2,144,256]{2,1,0:T(8,128)(2,1)S(1)}, u32[]{:S(2)}, u32[]{:S(2)}) collective-permute-start(bf16[2,144,256]{2,1,0:T(8,128)(2,1)S(1)} %get-tuple-element.278), channel_id=1, source_target_pairs={{0,16},{1,9},{2,18},{3,11},{4,20},{5,13},{6,22},{7,15},{8,24},{9,1... | collective-permute-start | bytes 442376 | tf_op jit(solution)/shard_map/ppermute | solution.py:663
  92.1 10.6 %collective-permute-start.19 = (bf16[1,256,256]{2,1,0:T(8,128)(2,1)S(1)}, bf16[1,256,256]{2,1,0:T(8,128)(2,1)S(1)}, u32[]{:S(2)}, u32[]{:S(2)}) collective-permute-start(bf16[1,256,256]{2,1,0:T(8,128)(2,1)S(1)} %get-tuple-element.283), channel_id=1, source_target_pairs={{0,16},{1,9},{2,18},{3,11},{4,20},{5,13},{6,22},{7,15},{8,24},{9,1... | collective-permute-start | bytes 393224 | tf_op jit(solution)/shard_map/ppermute | solution.py:663
  95.7 9.1 %collective-permute-start.21 = (bf16[1,256,256]{2,1,0:T(8,128)(2,1)S(1)}, bf16[1,256,256]{2,1,0:T(8,128)(2,1)S(1)}, u32[]{:S(2)}, u32[]{:S(2)}) collective-permute-start(bf16[1,256,256]{2,1,0:T(8,128)(2,1)S(1)} %get-tuple-element.286), channel_id=1, source_target_pairs={{0,8},{1,9},{2,10},{3,11},{4,12},{5,13},{6,14},{7,15},{8,0},{9,1},... | collective-permute-start | bytes 393224 | tf_op jit(solution)/shard_map/ppermute | solution.py:663
  96.0 8.1 %collective-permute-start.18 = (bf16[1,144,256]{2,1,0:T(8,128)(2,1)S(1)}, bf16[1,144,256]{2,1,0:T(8,128)(2,1)S(1)}, u32[]{:S(2)}, u32[]{:S(2)}) collective-permute-start(bf16[1,144,256]{2,1,0:T(8,128)(2,1)S(1)} %get-tuple-element.289), channel_id=1, source_target_pairs={{0,2},{1,17},{2,0},{3,19},{4,6},{5,21},{6,4},{7,23},{8,10},{9,25},... | collective-permute-start | bytes 221192 | tf_op jit(solution)/shard_map/ppermute | solution.py:663

commit v3 on v2

--- a/solution.py
+++ b/solution.py
@@ -158,8 +158,9 @@
 
 
 class Room:
-    def __init__(self, inputs, sources, held, sems):
+    def __init__(self, inputs, sources, held, sems, away):
         self.inputs, self.sources, self.held, self.sems = inputs, sources, held, sems
+        self.away, self.left = away, {}
         self.section = lax.axis_index("section")
         self.core = lax.axis_index("rows") & 1
         self.arrived = set()
@@ -179,9 +180,19 @@
             pltpu.make_async_copy(source, self.held[name], self.sems.at[place]).wait()
         return self.held[name]
 
+    def leave(self, *names):
+        for name, (target, sem) in self.away.items():
+            if name in names:
+                copy = pltpu.make_async_copy(self.held[name], target, sem)
+                copy.start()
+                self.left[name] = copy
+
     def finish(self):
+        self.leave(*(name for name in self.away if name not in self.left))
         for name in self.inputs:
             getattr(self, name)
+        for copy in self.left.values():
+            copy.wait()
 
     def either(self, here, there):
         return jnp.where(self.section == 0, here[...], there[...])
@@ -231,12 +242,14 @@
     return pltpu.with_memory_space_constraint(array, pltpu.VMEM)
 
 
-def call(body, inputs, near, outputs, loads, span, limit, packet=None, extra=None):
-    extra = extra or {}
+def call(body, inputs, near, outputs, loads, span, limit, packet=None, extra=None, away=None, late=None):
+    extra, away = extra or {}, away or {}
     inputs = {
         name: item if hasattr(item, "pieces") else Whole(item) for name, item in inputs.items()
     }
-    inputs.update({name: Whole(item) for name, item in loads.items()})
+    loads = {name: item if hasattr(item, "pieces") else Whole(item) for name, item in loads.items()}
+    inputs.update(loads)
+    inputs.update({name: item if hasattr(item, "pieces") else Whole(item) for name, item in (late or {}).items()})
     arrays = [array for item in inputs.values() for array in item.arrays]
     outputs = {
         **outputs,
@@ -244,6 +257,7 @@
     }
     shapes_out = [pltpu.VMEM(item.shape, item.dtype) for item in outputs.values()]
     shapes_out += packet.leaving() if packet else []
+    shapes_out += [pltpu.HBM(item.shape, item.dtype) for item in away.values()]
     brought = [name for name in inputs if name not in loads]
 
     def kernel(*refs):
@@ -258,26 +272,36 @@
         held = dict(zip(near, take(len(near))))
         held.update(zip(outputs, take(len(outputs))))
         leaving = take(2) if packet else None
+        targets = take(len(away))
         held.update(zip(brought, take(len(brought))))
         held.update(zip(extra, take(len(extra))))
-        room = Room(inputs, sources, held, refs[0])
+        held.update(zip(away, take(len(away))))
+        away_to = {
+            name: (target, refs[1].at[place])
+            for place, (name, target) in enumerate(zip(away, targets))
+        }
+        room = Room(inputs, sources, held, refs[0], away_to)
         if packet:
             packet.bind(room, leaving)
         body(room)
         room.finish()
 
-    scratch = [inputs[name] for name in brought] + list(extra.values())
+    scratch = [inputs[name] for name in brought] + list(extra.values()) + list(away.values())
     results = pl.pallas_call(
         kernel,
         out_shape=shapes_out,
         in_specs=[HBM] * len(arrays) + [VMEM] * len(near),
-        out_specs=[VMEM] * len(shapes_out),
+        out_specs=[VMEM] * (len(shapes_out) - len(away)) + [HBM] * len(away),
         scratch_shapes=[pltpu.VMEM(item.shape, item.dtype) for item in scratch]
-        + [pltpu.SemaphoreType.DMA((max(1, len(inputs)),))],
+        + [pltpu.SemaphoreType.DMA((max(1, len(inputs)),))]
+        + [pltpu.SemaphoreType.DMA((max(1, len(away)),))],
         compiler_params=pltpu.CompilerParams(vmem_limit_bytes=limit << 20),
         cost_estimate=lasting(span),
     )(*(far_away(item) for item in arrays), *(pinned(item) for item in near.values()))
-    return SimpleNamespace(**dict(zip(outputs, results))), tuple(results[len(outputs) :])
+    made = dict(zip(outputs, results))
+    made.update(zip(away, results[len(results) - len(away) :]))
+    leaving = tuple(results[len(outputs) : len(results) - len(away)])
+    return SimpleNamespace(**made), leaving
 
 
 def place_of(side, block, orders, core):
@@ -372,7 +396,7 @@
         in_specs=[VMEM] * len(arrays),
         out_specs=[VMEM] * 2,
         scratch_shapes=[pltpu.VMEM((GROUPS, height, SLAB), BF)],
-        compiler_params=pltpu.CompilerParams(vmem_limit_bytes=16 << 20),
+        compiler_params=pltpu.CompilerParams(vmem_limit_bytes=8 << 20),
         cost_estimate=lasting(3.5),
     )(*(pinned(item) for item in arrays))
 
@@ -394,6 +418,7 @@
 
 def self_part(room, tokens, ids, causal, inward, outward, gain, shift):
     room.projected[...] = matmul(tokens, inward[...]).astype(BF)
+    room.leave("projected")
     length = tokens.shape[0]
     rows = lax.broadcasted_iota(jnp.int32, (length, length), 0)
     columns = lax.broadcasted_iota(jnp.int32, (length, length), 1)
@@ -401,6 +426,7 @@
     allowed = equal_ids(ids, ids) & (rows + reach >= columns)
     mixed = attend(*thirds(room.projected), allowed, room.chances)
     room.mixed[...] = mixed
+    room.leave("chances", "mixed")
     summed = tokens.astype(F32) + matmul(mixed, outward[...])
     first, unit, scale = norm(summed, gain, shift)
     room.unit[...] = unit
@@ -543,7 +569,7 @@
         room.d_grad0[...],
         room.decoder_inward,
         room.decoder_outward,
-        room.tokens[...],
+        either(room.far_tokens, room.near_tokens),
         either(room.far_projected, room.near_projected),
         either(room.far_chances, room.near_chances),
         either(room.far_mixed, room.near_mixed),
@@ -583,7 +609,7 @@
         grad_sum,
         room.encoder_inward,
         room.encoder_outward,
-        room.tokens[...],
+        either(room.near_tokens, room.far_tokens),
         either(room.near_projected, room.far_projected),
         either(room.near_chances, room.far_chances),
         either(room.near_mixed, room.far_mixed),
@@ -614,7 +640,7 @@
     return lax.ppermute(value, axis, [(i, i ^ apart) for i in range(count)])
 
 
-def halve(kept, came, following):
+def halve(kept, came, following, span):
     count, height = kept.shape[0] // 2, kept.shape[1]
     half = pltpu.VMEM((count, height, SLAB), BF)
 
@@ -631,8 +657,8 @@
         out_shape=[half, half],
         in_specs=[VMEM] * 2,
         out_specs=[VMEM] * 2,
-        compiler_params=pltpu.CompilerParams(vmem_limit_bytes=4 << 20),
-        cost_estimate=lasting(2),
+        compiler_params=pltpu.CompilerParams(vmem_limit_bytes=2 << 20),
+        cost_estimate=lasting(span),
     )(pinned(kept), pinned(came))
 
 
@@ -662,13 +688,13 @@
             route.append((device, device ^ (pieces if step == SIDE else 1 << step)))
         self.came = lax.ppermute(self.sent, ("section", "rows"), route)
 
-    def step(self):
+    def step(self, span=2):
         if not self.even:
             return
         self.turn += 1
         kept, came = self.line.after(self.kept, self.came)
         following = [order[self.turn] for order in self.orders]
-        self.kept, self.sent = halve(kept, came, following)
+        self.kept, self.sent = halve(kept, came, following, span)
         self.line.mark(self.sent)
         self.go()
 
@@ -706,7 +732,7 @@
             out_shape=outs,
             in_specs=[VMEM] * 2,
             out_specs=[VMEM] * len(outs),
-            compiler_params=pltpu.CompilerParams(vmem_limit_bytes=8 << 20),
+            compiler_params=pltpu.CompilerParams(vmem_limit_bytes=2 << 20),
             cost_estimate=lasting(1.6),
         )(pinned(kept), pinned(came))
         self.line.mark(results[0])
@@ -744,10 +770,6 @@
 XYZ, YXZ = (SIDE, 1, 2, 3), (1, SIDE, 2, 3)
 XZY, YZX = (SIDE, 2, 3, 1), (1, 2, 3, SIDE)
 ZXY, ZYX = (2, 3, SIDE, 1), (2, 3, 1, SIDE)
-W_ORDERS = (YXZ, ZXY)
-Q_ORDERS = (ZYX, YXZ)
-E_ORDERS = (XYZ, YXZ)
-S_ORDERS = (ZXY, YZX)
 
 
 def per_device(
@@ -788,7 +810,7 @@
     )
     line = Line()
 
-    def run(body, inputs, near, outputs, loads, span, limit, packet=None, extra=None):
+    def run(body, inputs, near, outputs, loads, span, limit, packet=None, extra=None, away=None, late=None):
         near = dict(near)
         for name in list(near)[:1]:
             (near[name],) = line.after(near[name])
@@ -802,6 +824,8 @@
             limit,
             packet,
             extra,
+            away,
+            late,
         )
         line.mark(list(vars(kept).values())[0])
         if packet is None:
@@ -818,16 +842,20 @@
             tokens=Entry(own),
             inward=Either(encoder_inward, decoder_inward),
             encoder_gain=encoder_gain,
+            encoder_shift=encoder_shift,
             decoder_gain=decoder_gain,
-            encoder_shift=encoder_shift,
             decoder_shift=decoder_shift,
             outward=Either(encoder_outward, decoder_outward),
         ),
         {},
-        dict(first=units, **attended),
         {},
+        dict(
+            other_inward=Either(decoder_inward, encoder_inward),
+            other_outward=Either(decoder_outward, encoder_outward),
+        ),
         4,
-        8,
+        6,
+        away=dict(first=units, **attended),
     )
 
     wide_packet = Packet(decoder_narrow=decoder_narrow, decoder_widen=decoder_widen)
@@ -835,17 +863,15 @@
         forward_body,
         dict(
             segments=segments,
-            tokens=other,
-            inward=Either(decoder_inward, encoder_inward),
-            decoder_gain=decoder_gain,
             encoder_shift=encoder_shift,
             decoder_shift=decoder_shift,
-            outward=Either(decoder_outward, encoder_outward),
-            decoder_widen=decoder_widen,
-            decoder_narrow=decoder_narrow,
-            cotangent=Entry(cotangent),
+            own_first=near.first,
         ),
-        dict(own_first=near.first),
+        dict(
+            tokens=other,
+            inward=near.other_inward,
+            outward=near.other_outward,
+        ),
         dict(
             memory=slabs,
             output=slabs,
@@ -867,20 +893,22 @@
         ),
         dict(
             encoder_gain=encoder_gain,
+            decoder_gain=decoder_gain,
             encoder_widen=encoder_widen,
             encoder_narrow=encoder_narrow,
             decoder_cross_query=decoder_cross_query,
             decoder_cross_memory=decoder_cross_memory,
             decoder_cross_outward=decoder_cross_outward,
-            decoder_outward=decoder_outward,
-            decoder_inward=decoder_inward,
-            encoder_outward=encoder_outward,
-            encoder_inward=encoder_inward,
         ),
         11,
-        24,
+        14,
         wide_packet,
         dict(d_hidden=low(length, wide), d_slope=full(length, wide)),
+        late=dict(
+            decoder_widen=decoder_widen,
+            decoder_narrow=decoder_narrow,
+            cotangent=Entry(cotangent),
+        ),
     )
 
     cross_packet = Packet(
@@ -890,9 +918,10 @@
     )
     crossed, d_cross = run(
         cross_back_body,
-        dict(decoder_gain=decoder_gain),
+        dict(near_unit=near.unit, near_scale=near.scale),
         dict(
             d_grad=far.d_grad,
+            decoder_gain=far.decoder_gain,
             d_unit1=far.d_unit1,
             d_scale1=far.d_scale1,
             c_query=far.c_query,
@@ -904,15 +933,13 @@
             decoder_cross_outward=far.decoder_cross_outward,
             decoder_cross_memory=far.decoder_cross_memory,
             decoder_cross_query=far.decoder_cross_query,
-            near_unit=near.unit,
-            near_scale=near.scale,
             far_unit=far.unit,
             far_scale=far.scale,
         ),
         dict(grad_memory=slabs, d_grad0=units, d_small01=full(4, width)),
         {},
         4.7,
-        8,
+        5,
         cross_packet,
     )
 
@@ -920,14 +947,17 @@
         packet = Packet(decoder_inward=decoder_inward, decoder_outward=decoder_outward)
         return packet, *run(
             decoder_self_body,
-            dict(tokens=Either(other, (own, 1))),
             dict(
-                d_grad0=crossed.d_grad0,
-                decoder_outward=far.decoder_outward,
-                decoder_inward=far.decoder_inward,
+                decoder_outward=decoder_outward,
                 near_projected=near.projected,
                 near_chances=near.chances,
+                near_tokens=Entry(own),
                 near_mixed=near.mixed,
+                decoder_inward=decoder_inward,
+            ),
+            dict(
+                far_tokens=other,
+                d_grad0=crossed.d_grad0,
                 far_projected=far.projected,
                 far_chances=far.chances,
                 far_mixed=far.mixed,
@@ -935,7 +965,7 @@
             dict(d_inputs=slabs),
             {},
             5,
-            8,
+            5,
             packet,
         )
 
@@ -950,8 +980,18 @@
         sides = low(2, length, width)
         return packet, *run(
             encoder_back_body,
-            dict(tokens=Either((own, 0), other)),
             dict(
+                near_unit=near.unit,
+                near_scale=near.scale,
+                near_projected=near.projected,
+                near_chances=near.chances,
+                near_tokens=Entry(own),
+                near_mixed=near.mixed,
+                encoder_outward=encoder_outward,
+                encoder_inward=encoder_inward,
+            ),
+            dict(
+                far_tokens=other,
                 encoder_gain=far.encoder_gain,
                 grad_memory=crossed.grad_memory,
                 e_unit1=far.e_unit1,
@@ -963,13 +1003,6 @@
                 encoder_widen=far.encoder_widen,
                 d_small01=crossed.d_small01,
                 d_small2=far.d_small2,
-                encoder_outward=far.encoder_outward,
-                encoder_inward=far.encoder_inward,
-                near_unit=near.unit,
-                near_scale=near.scale,
-                near_projected=near.projected,
-                near_chances=near.chances,
-                near_mixed=near.mixed,
                 far_unit=far.unit,
                 far_scale=far.scale,
                 far_projected=far.projected,
@@ -982,44 +1015,72 @@
             dict(sides_mine=sides, sides_theirs=sides),
             {},
             8,
-            12,
+            8,
             packet,
         )
 
-    team_w = Team(line, W_ORDERS, decoder_narrow=decoder_narrow, decoder_widen=decoder_widen)
+    team_w = Team(
+        line,
+        (YZX, ZXY),
+        False,
+        decoder_narrow=decoder_narrow,
+        decoder_widen=decoder_widen,
+    )
     team_q = Team(
         line,
-        Q_ORDERS,
+        (XYZ, XYZ),
+        False,
         decoder_cross_query=decoder_cross_query,
         decoder_cross_memory=decoder_cross_memory,
         decoder_cross_outward=decoder_cross_outward,
+    )
+    team_r = Team(
+        line,
+        (XZY, YZX),
+        False,
         decoder_inward=decoder_inward,
         decoder_outward=decoder_outward,
     )
-    team_e = Team(line, E_ORDERS, encoder_narrow=encoder_narrow, encoder_widen=encoder_widen)
+    team_e = Team(
+        line,
+        (XYZ, YXZ),
+        False,
+        encoder_narrow=encoder_narrow,
+        encoder_widen=encoder_widen,
+    )
     team_s = Team(
-        line, S_ORDERS, True, encoder_inward=encoder_inward, encoder_outward=encoder_outward
+        line,
+        (YXZ, XZY),
+        True,
+        encoder_inward=encoder_inward,
+        encoder_outward=encoder_outward,
     )
     team_w.grads((wide_packet, d_wide))
+    team_q.grads((cross_packet, d_cross))
     self_packet, turned, d_self = d_self_run()
     encoder_packet, ended, e_all = encoder_run(turned.d_inputs)
-    team_q.grads((cross_packet, d_cross), (self_packet, d_self))
-    (theirs,) = line.after(ended.sides_theirs)
-    theirs = pair_swap(theirs, "section", 1)
+    team_r.grads((self_packet, d_self))
+    team_s.grads((encoder_packet, e_all))
+    team_w.step()
     team_e.grads((encoder_packet, e_all))
-    team_w.step()
     team_q.step()
-    team_s.grads((encoder_packet, e_all))
-    team_e.step()
+    team_r.step()
     team_w.step()
     team_s.step()
     team_q.step()
+    team_r.step()
     team_e.step()
+    team_q.step()
+    team_s.step()
+    (theirs,) = line.after(ended.sides_theirs)
+    theirs = pair_swap(theirs, "section", 1)
     team_w.step()
+    team_e.step()
+    team_q.end()
     team_s.step()
-    team_q.step()
+    team_r.step()
     team_e.step()
-    team_s.step()
+    team_w.end()
     mine, theirs = line.after(ended.sides_mine, theirs)
     results, gradients = (
         jnp.stack(
@@ -1031,13 +1092,12 @@
         for i in (0, 1)
     )
     line.mark(gradients)
-    team_w.end()
-    team_q.end()
     team_s.end()
+    team_r.end()
     team_e.end()
 
     done = {}
-    for team in (team_w, team_q, team_e, team_s):
+    for team in (team_w, team_q, team_r, team_e, team_s):
         done.update(team.done)
     deltas = SimpleNamespace(**done)
     shares = team_s.shares

time: 106 us -> 98.8 us (0.932)
  the two profiles are of different devices: /device:TPU:1 before, /device:TPU:0 now
where the time goes in v3:
time: 98.8 us; the launch traced here: 98.1 us
  Pallas kernels  38 us (38%)
  starting transfers between devices  37.5 us (38%)
  waiting for transfers between devices  19.4 us (20%)
  other arithmetic  1.49 us (2%)
    ppermute x20, starting transfers between devices, go(): self.came = lax.ppermute(self.sent, ('section', 'rows'), route)  32.3 us
    pallas_call x5, Pallas kernels, call(): pl.pallas_call(kernel, out_shape=shapes_out, in_specs=[HBM] * len(arrays)...  24.8 us
    ppermute x20, waiting for transfers between devices, go(): self.came = lax.ppermute(self.sent, ('section', 'rows'), route)  17.9 us
    pallas_call x5, Pallas kernels, weight_grads(): pl.pallas_call(kernel, out_shape=[half, half], in_specs=[VMEM] * len(arra...  5.91 us
    ppermute x6, starting transfers between devices, pair_swap(): return lax.ppermute(value, axis, [(i, i ^ apart) for i in range(count)])  5.22 us
    pallas_call x15, Pallas kernels, halve(): pl.pallas_call(kernel, out_shape=[half, half], in_specs=[VMEM] * 2, out_s...  3.79 us
    pallas_call x5, Pallas kernels, end(): pl.pallas_call(kernel, out_shape=outs, in_specs=[VMEM] * 2, out_specs=[VM...  3.42 us
  transfers between devices with their start and end apart: 26, of which 10 were waited for; matrix products, arithmetic and copies ran while one was open for 2% of the time, Pallas kernels for 29%

profile of v3, /device:TPU:0, one launch (start us, length us, event | category | flops | bytes accessed | tf_op | source)
XLA Modules:
  0.0 98.1 jit_solution(10602714225719393810)
XLA Ops:
  1.6 3.0 %collective-permute-start = (bf16[128,512]{1,0:T(8,128)(2,1)S(1)}, bf16[128,512]{1,0:T(8,128)(2,1)S(1)}, u32[]{:S(2)}, u32[]{:S(2)}) collective-permute-start(bf16[128,512]{1,0:T(8,128)(2,1)S(1)} %dynamic-slice_bitcast_fusion), channel_id=1, source_target_pairs={{0,16},{16,0},{1,17},{17,1},{2,18},{18,2},{3,19},{19,3},{4,20},{20... | collective-permute-start | bytes 393224 | tf_op jit(solution)/shard_map/ppermute | solution.py:640
  4.6 4.1 %shard_map.305 = (bf16[512,1536]{1,0:T(8,128)(2,1)S(1)}, bf16[512,512]{1,0:T(8,128)(2,1)S(1)}, f32[128,512]{1,0:T(8,128)}, bf16[128,1536]{1,0:T(8,128)(2,1)}, f3...) custom-call(s32[2,2,1,128]{3,2,1,0:T(1,128)} %refs_0_.4, ...), custom_call_target="tpu_custom_call" | custom-call | flops 32000000000 | bytes 1 | tf_op jit(solution)/shard_map/pallas_call | solution.py:290
  8.7 9.0 %shard_map.306 = (bf16[128,512]{1,0:T(8,128)(2,1)S(1)}, bf16[128,512]{1,0:T(8,128)(2,1)S(1)}, bf16[128,1536]{1,0:T(8,128)(2,1)S(1)}, f32[2,512,128]{2,1,0:T(8,12...) custom-call(s32[2,2,1,128]{3,2,1,0:T(1,128)} %refs_0_.4, ...), custom_call_target="tpu_custom_call" | custom-call | flops 88000004096 | bytes 1 | tf_op jit(solution)/shard_map/pallas_call | solution.py:290
  17.8 2.4 %shard_map.307 = (bf16[128,512]{1,0:T(8,128)(2,1)S(1)}, f32[128,512]{1,0:T(8,128)S(1)}, f32[4,512]{1,0:T(4,128)S(1)}, bf16[768,128]{1,0:T(8,128)(2,1)S(1)}, bf16[2816,128]{1,0:T(8,128)(2,1)S(1)}) custom-call(f32[128,512]{1,0:T(8,128)} %get-tuple-element.184.refs_0_, f32[128,128]{1,0:T(8,128)} %get-tuple-element.185.refs_1_, ...), custom_call_target="tpu_custom_call" | custom-call | flops 37600002048 | bytes 1 | tf_op jit(solution)/shard_map/pallas_call | solution.py:290
  20.8 2.1 %shard_map.308 = (bf16[8,256,256]{2,1,0:T(8,128)(2,1)S(1)}, bf16[8,256,256]{2,1,0:T(8,128)(2,1)}) custom-call(bf16[1280,128]{1,0:T(8,128)(2,1)S(1)} %get-tuple-element.214.refs_0_, bf16[3840,128]{1,0:T(8,128)(2,1)S(1)} %get-tuple-element.215.refs_1_, bf16[3840,128]{1,0:T(8,128)(2,1)S(1)} %collective-permute-done.2.refs_2_), custom_call_target="tpu_custom_call" | custom-call | flops 28000000000 | bytes 1 | tf_op jit(solution)/shard_map/pallas_call | solution.py:393
  22.9 1.5 %collective-permute-start.6 = (bf16[8,256,256]{2,1,0:T(8,128)(2,1)}, bf16[8,256,256]{2,1,0:T(8,128)(2,1)}, u32[]{:S(2)}, u32[]{:S(2)}) collective-permute-start(bf16[8,256,256]{2,1,0:T(8,128)(2,1)} %get-tuple-element.217), channel_id=1, source_target_pairs={{0,2},{1,5},{2,0},{3,7},{4,6},{5,1},{6,4},{7,3},{8,10},{9,13},{10,... | collective-permute-start | bytes 3145736 | tf_op jit(solution)/shard_map/ppermute | solution.py:689
  24.4 1.4 %shard_map.309 = (bf16[8,128,256]{2,1,0:T(8,128)(2,1)S(1)}, bf16[8,128,256]{2,1,0:T(8,128)(2,1)}) custom-call(bf16[768,128]{1,0:T(8,128)(2,1)S(1)} %get-tuple-element.218.refs_0_, bf16[2816,128]{1,0:T(8,128)(2,1)S(1)} %get-tuple-element.219.refs_1_, bf16[2816,128]{1,0:T(8,128)(2,1)S(1)} %collective-permute-done.1.refs_2_), custom_call_target="tpu_custom_call" | custom-call | flops 28000000000 | bytes 1 | tf_op jit(solution)/shard_map/pallas_call | solution.py:393
  26.9 4.0 %shard_map.310 = (bf16[128,512]{1,0:T(8,128)(2,1)S(1)}, bf16[512,128]{1,0:T(8,128)(2,1)S(1)}, bf16[2560,128]{1,0:T(8,128)(2,1)S(1)}) custom-call(bf16[512,512]{1,0:T(8,128)(2,1)} %refs_0_.5, bf16[128,1536]{1,0:T(8,128)(2,1)} %get-tuple-element.186.refs_1_.refs_2_, f32[2,512,128]{2,1,0:T(8,128)} %get-tuple-element.187.refs_2_.refs_3_, ...), custom_call_target="tpu_custom_call" | custom-call | flops 40000000000 | bytes 1 | tf_op jit(solution)/shard_map/pallas_call | solution.py:290
  30.9 5.4 %shard_map.311 = (bf16[2,128,512]{2,1,0:T(8,128)(2,1)S(1)}, bf16[2,128,512]{2,1,0:T(8,128)(2,1)S(1)}, bf16[1792,128]{1,0:T(8,128)(2,1)S(1)}, bf16[6464,128]{1,0:T(8,128)(2,1)S(1)}) custom-call(f32[128,512]{1,0:T(8,128)} %get-tuple-element.184.refs_0_, f32[128,128]{1,0:T(8,128)} %get-tuple-element.185.refs_1_, ...), custom_call_target="tpu_custom_call" | custom-call | flops 64000000000 | bytes 1 | tf_op jit(solution)/shard_map/pallas_call | solution.py:290
  38.5 1.5 %collective-permute-done.3.refs_2_ = bf16[6464,128]{1,0:T(8,128)(2,1)S(1)} collective-permute-done((bf16[6464,128]{1,0:T(8,128)(2,1)S(1)}, bf16[6464,128]{1,0:T(8,128)(2,1)S(1)}, u32[]{:S(2)}, u32[]{:S(2)}) %collective-permute-start.3) | collective-permute-done | bytes 1654816 | tf_op jit(solution)/shard_map/ppermute | solution.py:640
  41.6 1.5 %shard_map.314 = (bf16[4,256,256]{2,1,0:T(8,128)(2,1)S(1)}, bf16[4,256,256]{2,1,0:T(8,128)(2,1)S(1)}) custom-call(bf16[8,256,256]{2,1,0:T(8,128)(2,1)S(1)} %get-tuple-element.256.kept_ref, bf16[8,256,256]{2,1,0:T(8,128)(2,1)} %collective-permute-done.6.came_ref), custom_call_target="tpu_custom_call" | custom-call | flops 16000000000 | bytes 1 | tf_op jit(solution)/shard_map/pallas_call | solution.py:655
  47.7 1.6 %collective-permute-start.11 = (bf16[4,128,256]{2,1,0:T(8,128)(2,1)S(1)}, bf16[4,128,256]{2,1,0:T(8,128)(2,1)S(1)}, u32[]{:S(2)}, u32[]{:S(2)}) collective-permute-start(bf16[4,128,256]{2,1,0:T(8,128)(2,1)S(1)} %get-tuple-element.268), channel_id=1, source_target_pairs={{0,2},{1,3},{2,0},{3,1},{4,6},{5,7},{6,4},{7,5},{8,10},{9,11},{10,... | collective-permute-start | bytes 786440 | tf_op jit(solution)/shard_map/ppermute | solution.py:689
  49.7 1.6 %collective-permute-start.14 = (bf16[4,128,256]{2,1,0:T(8,128)(2,1)S(1)}, bf16[4,128,256]{2,1,0:T(8,128)(2,1)S(1)}, u32[]{:S(2)}, u32[]{:S(2)}) collective-permute-start(bf16[4,128,256]{2,1,0:T(8,128)(2,1)S(1)} %get-tuple-element.271), channel_id=1, source_target_pairs={{0,4},{1,5},{2,6},{3,7},{4,0},{5,1},{6,2},{7,3},{8,12},{9,13},{10,... | collective-permute-start | bytes 786440 | tf_op jit(solution)/shard_map/ppermute | solution.py:689
  51.4 9.2 %collective-permute-done.7.came_ref = bf16[4,256,256]{2,1,0:T(8,128)(2,1)S(1)} collective-permute-done((bf16[4,256,256]{2,1,0:T(8,128)(2,1)S(1)}, bf16[4,256,256]{2,1,0:T(8,128)(2,1)S(1)}, u32[]{:S(2)}, u32[]{:S(2)}) %collective-permute-start.7) | collective-permute-done | bytes 524320 | tf_op jit(solution)/shard_map/ppermute | solution.py:689
  60.7 1.5 %collective-permute-start.16 = (bf16[2,256,256]{2,1,0:T(8,128)(2,1)S(1)}, bf16[2,256,256]{2,1,0:T(8,128)(2,1)S(1)}, u32[]{:S(2)}, u32[]{:S(2)}) collective-permute-start(bf16[2,256,256]{2,1,0:T(8,128)(2,1)S(1)} %get-tuple-element.274), channel_id=1, source_target_pairs={{0,8},{1,17},{2,10},{3,19},{4,12},{5,21},{6,14},{7,23},{8,0},{9,25... | collective-permute-start | bytes 786440 | tf_op jit(solution)/shard_map/ppermute | solution.py:689
  63.4 2.5 %collective-permute-start.12 = (bf16[2,128,256]{2,1,0:T(8,128)(2,1)S(1)}, bf16[2,128,256]{2,1,0:T(8,128)(2,1)S(1)}, u32[]{:S(2)}, u32[]{:S(2)}) collective-permute-start(bf16[2,128,256]{2,1,0:T(8,128)(2,1)S(1)} %get-tuple-element.283), channel_id=1, source_target_pairs={{0,4},{1,5},{2,6},{3,7},{4,0},{5,1},{6,2},{7,3},{8,12},{9,13},{10,... | collective-permute-start | bytes 393224 | tf_op jit(solution)/shard_map/ppermute | solution.py:689
  68.6 2.1 %collective-permute-done.12.came_ref = bf16[2,128,256]{2,1,0:T(8,128)(2,1)S(1)} collective-permute-done((bf16[2,128,256]{2,1,0:T(8,128)(2,1)S(1)}, bf16[2,128,256]{2,1,0:T(8,128)(2,1)S(1)}, u32[]{:S(2)}, u32[]{:S(2)}) %collective-permute-start.12) | collective-permute-done | bytes 131104 | tf_op jit(solution)/shard_map/ppermute | solution.py:689
  70.8 1.9 %collective-permute-start.22 = (bf16[1,128,256]{2,1,0:T(8,128)(2,1)S(1)}, bf16[1,128,256]{2,1,0:T(8,128)(2,1)S(1)}, u32[]{:S(2)}, u32[]{:S(2)}) collective-permute-start(bf16[1,128,256]{2,1,0:T(8,128)(2,1)S(1)} %get-tuple-element.294), channel_id=1, source_target_pairs={{0,8},{1,9},{2,10},{3,11},{4,12},{5,13},{6,14},{7,15},{8,0},{9,1},... | collective-permute-start | bytes 196616 | tf_op jit(solution)/shard_map/ppermute | solution.py:689
  72.8 2.4 %collective-permute-start.21 = (bf16[2,144,256]{2,1,0:T(8,128)(2,1)S(1)}, bf16[2,144,256]{2,1,0:T(8,128)(2,1)S(1)}, u32[]{:S(2)}, u32[]{:S(2)}) collective-permute-start(bf16[2,144,256]{2,1,0:T(8,128)(2,1)S(1)} %get-tuple-element.297), channel_id=1, source_target_pairs={{0,4},{1,9},{2,6},{3,11},{4,0},{5,13},{6,2},{7,15},{8,12},{9,1},{1... | collective-permute-start | bytes 442376 | tf_op jit(solution)/shard_map/ppermute | solution.py:689
  78.4 1.6 %collective-permute-start.19 = (bf16[2,256,256]{2,1,0:T(8,128)(2,1)S(1)}, bf16[2,256,256]{2,1,0:T(8,128)(2,1)S(1)}, u32[]{:S(2)}, u32[]{:S(2)}) collective-permute-start(bf16[2,256,256]{2,1,0:T(8,128)(2,1)S(1)} %get-tuple-element.308), channel_id=1, source_target_pairs={{0,4},{1,5},{2,6},{3,7},{4,0},{5,1},{6,2},{7,3},{8,12},{9,13},{10,... | collective-permute-start | bytes 786440 | tf_op jit(solution)/shard_map/ppermute | solution.py:689
  80.7 1.9 %collective-permute-start.23 = (bf16[1,144,256]{2,1,0:T(8,128)(2,1)S(1)}, bf16[1,144,256]{2,1,0:T(8,128)(2,1)S(1)}, u32[]{:S(2)}, u32[]{:S(2)}) collective-permute-start(bf16[1,144,256]{2,1,0:T(8,128)(2,1)S(1)} %get-tuple-element.317), channel_id=1, source_target_pairs={{0,8},{1,3},{2,10},{3,1},{4,12},{5,7},{6,14},{7,5},{8,0},{9,11},{1... | collective-permute-start | bytes 221192 | tf_op jit(solution)/shard_map/ppermute | solution.py:689
  83.8 2.3 %collective-permute-done.19.came_ref = bf16[2,256,256]{2,1,0:T(8,128)(2,1)S(1)} collective-permute-done((bf16[2,256,256]{2,1,0:T(8,128)(2,1)S(1)}, bf16[2,256,256]{2,1,0:T(8,128)(2,1)S(1)}, u32[]{:S(2)}, u32[]{:S(2)}) %collective-permute-start.19) | collective-permute-done | bytes 262176 | tf_op jit(solution)/shard_map/ppermute | solution.py:689
  86.3 5.0 %collective-permute-start.24 = (bf16[1,256,256]{2,1,0:T(8,128)(2,1)S(1)}, bf16[1,256,256]{2,1,0:T(8,128)(2,1)S(1)}, u32[]{:S(2)}, u32[]{:S(2)}) collective-permute-start(bf16[1,256,256]{2,1,0:T(8,128)(2,1)S(1)} %get-tuple-element.323), channel_id=1, source_target_pairs={{0,8},{1,9},{2,10},{3,11},{4,12},{5,13},{6,14},{7,15},{8,0},{9,1},... | collective-permute-start | bytes 393224 | tf_op jit(solution)/shard_map/ppermute | solution.py:689
  94.8 2.6 %collective-permute-done.24.came_ref = bf16[1,256,256]{2,1,0:T(8,128)(2,1)S(1)} collective-permute-done((bf16[1,256,256]{2,1,0:T(8,128)(2,1)S(1)}, bf16[1,256,256]{2,1,0:T(8,128)(2,1)S(1)}, u32[]{:S(2)}, u32[]{:S(2)}) %collective-permute-start.24) | collective-permute-done | bytes 131104 | tf_op jit(solution)/shard_map/ppermute | solution.py:689
  (62 shorter events, 25.2 us)
Async XLA Ops:
  1.6 7.1 %collective-permute-start = (bf16[128,512]{1,0:T(8,128)(2,1)S(1)}, bf16[128,512]{1,0:T(8,128)(2,1)S(1)}, u32[]{:S(2)}, u32[]{:S(2)}) collective-permute-start(bf16[128,512]{1,0:T(8,128)(2,1)S(1)} %dynamic-slice_bitcast_fusion), channel_id=1, source_target_pairs={{0,16},{16,0},{1,17},{17,1},{2,18},{18,2},{3,19},{19,3},{4,20},{20... | collective-permute-start | bytes 393224 | tf_op jit(solution)/shard_map/ppermute | solution.py:640
  20.2 4.2 %collective-permute-start.1 = (bf16[2816,128]{1,0:T(8,128)(2,1)S(1)}, bf16[2816,128]{1,0:T(8,128)(2,1)S(1)}, u32[]{:S(2)}, u32[]{:S(2)}) collective-permute-start(bf16[2816,128]{1,0:T(8,128)(2,1)S(1)} %get-tuple-element.219.refs_1_), channel_id=1, source_target_pairs={{0,1},{1,0},{2,3},{3,2},{4,5},{5,4},{6,7},{7,6},{8,9},{9,8},{10,11... | collective-permute-start | bytes 2162696 | tf_op jit(solution)/shard_map/ppermute | solution.py:640
  22.9 18.7 %collective-permute-start.6 = (bf16[8,256,256]{2,1,0:T(8,128)(2,1)}, bf16[8,256,256]{2,1,0:T(8,128)(2,1)}, u32[]{:S(2)}, u32[]{:S(2)}) collective-permute-start(bf16[8,256,256]{2,1,0:T(8,128)(2,1)} %get-tuple-element.217), channel_id=1, source_target_pairs={{0,2},{1,5},{2,0},{3,7},{4,6},{5,1},{6,4},{7,3},{8,10},{9,13},{10,... | collective-permute-start | bytes 3145736 | tf_op jit(solution)/shard_map/ppermute | solution.py:689
  25.8 20.7 %collective-permute-start.9 = (bf16[8,128,256]{2,1,0:T(8,128)(2,1)}, bf16[8,128,256]{2,1,0:T(8,128)(2,1)}, u32[]{:S(2)}, u32[]{:S(2)}) collective-permute-start(bf16[8,128,256]{2,1,0:T(8,128)(2,1)} %get-tuple-element.221), channel_id=1, source_target_pairs={{0,16},{1,17},{2,18},{3,19},{4,20},{5,21},{6,22},{7,23},{8,24},{9,... | collective-permute-start | bytes 1572872 | tf_op jit(solution)/shard_map/ppermute | solution.py:689
  30.8 6.0 %collective-permute-start.4 = (bf16[2560,128]{1,0:T(8,128)(2,1)S(1)}, bf16[2560,128]{1,0:T(8,128)(2,1)S(1)}, u32[]{:S(2)}, u32[]{:S(2)}) collective-permute-start(bf16[2560,128]{1,0:T(8,128)(2,1)S(1)} %get-tuple-element.247.refs_1_), channel_id=1, source_target_pairs={{0,1},{1,0},{2,3},{3,2},{4,5},{5,4},{6,7},{7,6},{8,9},{9,8},{10,11... | collective-permute-start | bytes 1966088 | tf_op jit(solution)/shard_map/ppermute | solution.py:640
  37.4 12.2 %collective-permute-start.8 = (bf16[8,128,256]{2,1,0:T(8,128)(2,1)S(1)}, bf16[8,128,256]{2,1,0:T(8,128)(2,1)S(1)}, u32[]{:S(2)}, u32[]{:S(2)}) collective-permute-start(bf16[8,128,256]{2,1,0:T(8,128)(2,1)S(1)} %get-tuple-element.249), channel_id=1, source_target_pairs={{0,16},{1,3},{2,18},{3,1},{4,20},{5,7},{6,22},{7,5},{8,24},{9,11},... | collective-permute-start | bytes 1572872 | tf_op jit(solution)/shard_map/ppermute | solution.py:689
  40.6 21.6 %collective-permute-start.5 = (bf16[8,144,256]{2,1,0:T(8,128)(2,1)S(1)}, bf16[8,144,256]{2,1,0:T(8,128)(2,1)S(1)}, u32[]{:S(2)}, u32[]{:S(2)}) collective-permute-start(bf16[8,144,256]{2,1,0:T(8,128)(2,1)S(1)} %get-tuple-element.254), channel_id=1, source_target_pairs={{0,2},{1,17},{2,0},{3,19},{4,6},{5,21},{6,4},{7,23},{8,10},{9,25},... | collective-permute-start | bytes 1769480 | tf_op jit(solution)/shard_map/ppermute | solution.py:689
  43.0 17.6 %collective-permute-start.7 = (bf16[4,256,256]{2,1,0:T(8,128)(2,1)S(1)}, bf16[4,256,256]{2,1,0:T(8,128)(2,1)S(1)}, u32[]{:S(2)}, u32[]{:S(2)}) collective-permute-start(bf16[4,256,256]{2,1,0:T(8,128)(2,1)S(1)} %get-tuple-element.259), channel_id=1, source_target_pairs={{0,4},{1,9},{2,6},{3,11},{4,0},{5,13},{6,2},{7,15},{8,12},{9,1},{1... | collective-permute-start | bytes 1572872 | tf_op jit(solution)/shard_map/ppermute | solution.py:689
  45.4 21.6 %collective-permute-start.13 = (bf16[8,256,256]{2,1,0:T(8,128)(2,1)S(1)}, bf16[8,256,256]{2,1,0:T(8,128)(2,1)S(1)}, u32[]{:S(2)}, u32[]{:S(2)}) collective-permute-start(bf16[8,256,256]{2,1,0:T(8,128)(2,1)S(1)} %get-tuple-element.265), channel_id=1, source_target_pairs={{0,16},{1,3},{2,18},{3,1},{4,20},{5,7},{6,22},{7,5},{8,24},{9,11},... | collective-permute-start | bytes 3145736 | tf_op jit(solution)/shard_map/ppermute | solution.py:689
  47.7 15.7 %collective-permute-start.11 = (bf16[4,128,256]{2,1,0:T(8,128)(2,1)S(1)}, bf16[4,128,256]{2,1,0:T(8,128)(2,1)S(1)}, u32[]{:S(2)}, u32[]{:S(2)}) collective-permute-start(bf16[4,128,256]{2,1,0:T(8,128)(2,1)S(1)} %get-tuple-element.268), channel_id=1, source_target_pairs={{0,2},{1,3},{2,0},{3,1},{4,6},{5,7},{6,4},{7,5},{8,10},{9,11},{10,... | collective-permute-start | bytes 786440 | tf_op jit(solution)/shard_map/ppermute | solution.py:689
  49.7 16.3 %collective-permute-start.14 = (bf16[4,128,256]{2,1,0:T(8,128)(2,1)S(1)}, bf16[4,128,256]{2,1,0:T(8,128)(2,1)S(1)}, u32[]{:S(2)}, u32[]{:S(2)}) collective-permute-start(bf16[4,128,256]{2,1,0:T(8,128)(2,1)S(1)} %get-tuple-element.271), channel_id=1, source_target_pairs={{0,4},{1,5},{2,6},{3,7},{4,0},{5,1},{6,2},{7,3},{8,12},{9,13},{10,... | collective-permute-start | bytes 786440 | tf_op jit(solution)/shard_map/ppermute | solution.py:689
  60.7 14.4 %collective-permute-start.16 = (bf16[2,256,256]{2,1,0:T(8,128)(2,1)S(1)}, bf16[2,256,256]{2,1,0:T(8,128)(2,1)S(1)}, u32[]{:S(2)}, u32[]{:S(2)}) collective-permute-start(bf16[2,256,256]{2,1,0:T(8,128)(2,1)S(1)} %get-tuple-element.274), channel_id=1, source_target_pairs={{0,8},{1,17},{2,10},{3,19},{4,12},{5,21},{6,14},{7,23},{8,0},{9,25... | collective-permute-start | bytes 786440 | tf_op jit(solution)/shard_map/ppermute | solution.py:689
  62.3 10.4 %collective-permute-start.10 = (bf16[4,144,256]{2,1,0:T(8,128)(2,1)S(1)}, bf16[4,144,256]{2,1,0:T(8,128)(2,1)S(1)}, u32[]{:S(2)}, u32[]{:S(2)}) collective-permute-start(bf16[4,144,256]{2,1,0:T(8,128)(2,1)S(1)} %get-tuple-element.278), channel_id=1, source_target_pairs={{0,16},{1,5},{2,18},{3,7},{4,20},{5,1},{6,22},{7,3},{8,24},{9,13},... | collective-permute-start | bytes 884744 | tf_op jit(solution)/shard_map/ppermute | solution.py:689
  63.4 7.3 %collective-permute-start.12 = (bf16[2,128,256]{2,1,0:T(8,128)(2,1)S(1)}, bf16[2,128,256]{2,1,0:T(8,128)(2,1)S(1)}, u32[]{:S(2)}, u32[]{:S(2)}) collective-permute-start(bf16[2,128,256]{2,1,0:T(8,128)(2,1)S(1)} %get-tuple-element.283), channel_id=1, source_target_pairs={{0,4},{1,5},{2,6},{3,7},{4,0},{5,1},{6,2},{7,3},{8,12},{9,13},{10,... | collective-permute-start | bytes 393224 | tf_op jit(solution)/shard_map/ppermute | solution.py:689
  66.2 16.5 %collective-permute-start.20 = (bf16[2,128,256]{2,1,0:T(8,128)(2,1)S(1)}, bf16[2,128,256]{2,1,0:T(8,128)(2,1)S(1)}, u32[]{:S(2)}, u32[]{:S(2)}) collective-permute-start(bf16[2,128,256]{2,1,0:T(8,128)(2,1)S(1)} %get-tuple-element.288), channel_id=1, source_target_pairs={{0,8},{1,9},{2,10},{3,11},{4,12},{5,13},{6,14},{7,15},{8,0},{9,1},... | collective-permute-start | bytes 393224 | tf_op jit(solution)/shard_map/ppermute | solution.py:689
  67.3 9.2 %collective-permute-start.18 = (bf16[4,256,256]{2,1,0:T(8,128)(2,1)S(1)}, bf16[4,256,256]{2,1,0:T(8,128)(2,1)S(1)}, u32[]{:S(2)}, u32[]{:S(2)}) collective-permute-start(bf16[4,256,256]{2,1,0:T(8,128)(2,1)S(1)} %get-tuple-element.291), channel_id=1, source_target_pairs={{0,2},{1,17},{2,0},{3,19},{4,6},{5,21},{6,4},{7,23},{8,10},{9,25},... | collective-permute-start | bytes 1572872 | tf_op jit(solution)/shard_map/ppermute | solution.py:689
  70.8 7.6 %collective-permute-start.22 = (bf16[1,128,256]{2,1,0:T(8,128)(2,1)S(1)}, bf16[1,128,256]{2,1,0:T(8,128)(2,1)S(1)}, u32[]{:S(2)}, u32[]{:S(2)}) collective-permute-start(bf16[1,128,256]{2,1,0:T(8,128)(2,1)S(1)} %get-tuple-element.294), channel_id=1, source_target_pairs={{0,8},{1,9},{2,10},{3,11},{4,12},{5,13},{6,14},{7,15},{8,0},{9,1},... | collective-permute-start | bytes 196616 | tf_op jit(solution)/shard_map/ppermute | solution.py:689
  72.8 7.9 %collective-permute-start.21 = (bf16[2,144,256]{2,1,0:T(8,128)(2,1)S(1)}, bf16[2,144,256]{2,1,0:T(8,128)(2,1)S(1)}, u32[]{:S(2)}, u32[]{:S(2)}) collective-permute-start(bf16[2,144,256]{2,1,0:T(8,128)(2,1)S(1)} %get-tuple-element.297), channel_id=1, source_target_pairs={{0,4},{1,9},{2,6},{3,11},{4,0},{5,13},{6,2},{7,15},{8,12},{9,1},{1... | collective-permute-start | bytes 442376 | tf_op jit(solution)/shard_map/ppermute | solution.py:689
  75.2 16.1 %collective-permute-start.17 = (bf16[1,256,256]{2,1,0:T(8,128)(2,1)S(1)}, bf16[1,256,256]{2,1,0:T(8,128)(2,1)S(1)}, u32[]{:S(2)}, u32[]{:S(2)}) collective-permute-start(bf16[1,256,256]{2,1,0:T(8,128)(2,1)S(1)} %get-tuple-element.303), channel_id=1, source_target_pairs={{0,16},{1,3},{2,18},{3,1},{4,20},{5,7},{6,22},{7,5},{8,24},{9,11},... | collective-permute-start | bytes 393224 | tf_op jit(solution)/shard_map/ppermute | solution.py:689
  76.5 15.4 %collective-permute-start.15 = (bf16[2,128,512]{2,1,0:T(8,128)(2,1)S(1)}, bf16[2,128,512]{2,1,0:T(8,128)(2,1)S(1)}, u32[]{:S(2)}, u32[]{:S(2)}) collective-permute-start(bf16[2,128,512]{2,1,0:T(8,128)(2,1)S(1)} %get-tuple-element.298), channel_id=1, source_target_pairs={{0,16},{16,0},{1,17},{17,1},{2,18},{18,2},{3,19},{19,3},{4,20},{20... | collective-permute-start | bytes 786440 | tf_op jit(solution)/shard_map/ppermute | solution.py:640
  78.4 7.8 %collective-permute-start.19 = (bf16[2,256,256]{2,1,0:T(8,128)(2,1)S(1)}, bf16[2,256,256]{2,1,0:T(8,128)(2,1)S(1)}, u32[]{:S(2)}, u32[]{:S(2)}) collective-permute-start(bf16[2,256,256]{2,1,0:T(8,128)(2,1)S(1)} %get-tuple-element.308), channel_id=1, source_target_pairs={{0,4},{1,5},{2,6},{3,7},{4,0},{5,1},{6,2},{7,3},{8,12},{9,13},{10,... | collective-permute-start | bytes 786440 | tf_op jit(solution)/shard_map/ppermute | solution.py:689
  80.7 12.0 %collective-permute-start.23 = (bf16[1,144,256]{2,1,0:T(8,128)(2,1)S(1)}, bf16[1,144,256]{2,1,0:T(8,128)(2,1)S(1)}, u32[]{:S(2)}, u32[]{:S(2)}) collective-permute-start(bf16[1,144,256]{2,1,0:T(8,128)(2,1)S(1)} %get-tuple-element.317), channel_id=1, source_target_pairs={{0,8},{1,3},{2,10},{3,1},{4,12},{5,7},{6,14},{7,5},{8,0},{9,11},{1... | collective-permute-start | bytes 221192 | tf_op jit(solution)/shard_map/ppermute | solution.py:689
  82.7 10.8 %collective-permute-start.25 = (bf16[1,128,256]{2,1,0:T(8,128)(2,1)S(1)}, bf16[1,128,256]{2,1,0:T(8,128)(2,1)S(1)}, u32[]{:S(2)}, u32[]{:S(2)}) collective-permute-start(bf16[1,128,256]{2,1,0:T(8,128)(2,1)S(1)} %get-tuple-element.320), channel_id=1, source_target_pairs={{0,2},{1,17},{2,0},{3,19},{4,6},{5,21},{6,4},{7,23},{8,10},{9,25},... | collective-permute-start | bytes 196616 | tf_op jit(solution)/shard_map/ppermute | solution.py:689
  86.3 11.1 %collective-permute-start.24 = (bf16[1,256,256]{2,1,0:T(8,128)(2,1)S(1)}, bf16[1,256,256]{2,1,0:T(8,128)(2,1)S(1)}, u32[]{:S(2)}, u32[]{:S(2)}) collective-permute-start(bf16[1,256,256]{2,1,0:T(8,128)(2,1)S(1)} %get-tuple-element.323), channel_id=1, source_target_pairs={{0,8},{1,9},{2,10},{3,11},{4,12},{5,13},{6,14},{7,15},{8,0},{9,1},... | collective-permute-start | bytes 393224 | tf_op jit(solution)/shard_map/ppermute | solution.py:689
  (2 other events, 6.8 us)

commit v4 on v3

--- a/solution.py
+++ b/solution.py
@@ -17,11 +17,10 @@
 GROUPS = 16
 SLAB = 256
 LANES = 128
-PER_SLAB = SLAB // HEAD_DIM
 BF = jnp.bfloat16
 F32 = jnp.float32
 def lasting(span):
-    return pl.CostEstimate(flops=int(span * 8e9), bytes_accessed=1, transcendentals=0)
+    return pl.CostEstimate(flops=int(span * 5.5e9), bytes_accessed=1, transcendentals=0)
 
 
 FACTOR = 1.0 / math.sqrt(HEAD_DIM)
@@ -62,61 +61,64 @@
 def gelu_both(before):
     root = math.sqrt(2.0 / math.pi)
     square = before * before
-    bent = jnp.tanh(root * before * (1.0 + 0.044715 * square))
-    half = 0.5 * (1.0 + bent)
-    slope = half + 0.5 * before * (1.0 - bent * bent) * (root * (1.0 + 3 * 0.044715 * square))
-    return before * half, slope
-
-
-def head_marks(dtype):
-    lane = lax.broadcasted_iota(jnp.int32, (1, SLAB), 1) // HEAD_DIM
-    return [(lane == h).astype(F32).astype(dtype) for h in range(PER_SLAB)]
-
-
-def spread_heads(slab, marks):
-    return jnp.concatenate([slab * mark for mark in marks], 0)
-
-
-def gather_heads(stacked, rows):
-    lane = lax.broadcasted_iota(jnp.int32, (1, SLAB), 1) // HEAD_DIM
-    total = stacked[:rows]
-    for h in range(1, PER_SLAB):
-        total = jnp.where(lane == h, stacked[h * rows : (h + 1) * rows], total)
-    return total
+    half = 0.5 + 0.5 * jnp.tanh(before * (root + root * 0.044715 * square))
+    steep = 2 * root + 6 * root * 0.044715 * square
+    return before * half, half * (1.0 + before * (1.0 - half) * steep)
+
+
+def pair_marks():
+    lane = lax.broadcasted_iota(jnp.int32, (1, LANES), 1) // HEAD_DIM
+    return [(lane == h).astype(F32).astype(BF) for h in (0, 1)]
+
+
+def join_pairs(parts):
+    lane = lax.broadcasted_iota(jnp.int32, (1, LANES), 1) // HEAD_DIM
+    pairs = zip(parts[0::2], parts[1::2])
+    return jnp.concatenate([jnp.where(lane == 0, one, two) for one, two in pairs], 1)
 
 
 def attend(query, keys, values, allowed, chances_ref):
-    rows = query.shape[0]
-    marks = head_marks(BF)
-    wide = jnp.concatenate([allowed] * PER_SLAB, 0)
+    marks = pair_marks()
+    query_down, values_down = query.T, values.T
+    scores = []
+    for head in range(HEADS):
+        at = slice(head // 2 * LANES, (head // 2 + 1) * LANES)
+        scores.append(matmul(keys[:, at] * marks[head % 2], query_down[at]))
+    scores = [jnp.where(allowed, item * FACTOR, NEG) for item in scores]
+    weights = [jnp.exp(item - jnp.max(item, 0, keepdims=True)) for item in scores]
+    chances = [item * (1.0 / jnp.sum(item, 0, keepdims=True)) for item in weights]
     mixed = []
-    for slab in range(query.shape[1] // SLAB):
-        at = slice(slab * SLAB, (slab + 1) * SLAB)
-        scores = matmul_back(spread_heads(query[:, at], marks), keys[:, at]) * FACTOR
-        scores = jnp.where(wide, scores, NEG)
-        weights = jnp.exp(scores - jnp.max(scores, -1, keepdims=True))
-        chances = weights * (1.0 / jnp.sum(weights, -1, keepdims=True))
-        chances_ref[slab] = chances
-        mixed.append(gather_heads(matmul(chances.astype(BF), values[:, at]), rows).astype(BF))
-    return jnp.concatenate(mixed, 1)
+    for head, item in enumerate(chances):
+        chances_ref[head] = item
+        at = slice(head * HEAD_DIM, (head + 1) * HEAD_DIM)
+        mixed.append(matmul(values_down[at], item.astype(BF)).astype(BF))
+    return jnp.concatenate(mixed, 0).T
 
 
 def attend_back(query, keys, values, chances_ref, grad_mixed):
-    rows = query.shape[0]
-    marks = head_marks(BF)
-    grad_query, grad_keys, grad_values = [], [], []
-    for slab in range(query.shape[1] // SLAB):
-        at = slice(slab * SLAB, (slab + 1) * SLAB)
-        chances = chances_ref[slab]
-        spread_grad = spread_heads(grad_mixed[:, at], marks)
-        grad_chances = matmul_back(spread_grad, values[:, at])
-        grad_values.append(matmul_across(chances.astype(BF), spread_grad).astype(BF))
-        held = jnp.sum(chances * grad_chances, -1, keepdims=True)
-        grad_scores = (chances * (grad_chances - held)).astype(BF)
-        grad_query.append((gather_heads(matmul(grad_scores, keys[:, at]), rows) * FACTOR).astype(BF))
-        spread_query = spread_heads(query[:, at], marks)
-        grad_keys.append((matmul_across(grad_scores, spread_query) * FACTOR).astype(BF))
-    return [jnp.concatenate(item, 1) for item in (grad_query, grad_keys, grad_values)]
+    marks = pair_marks()
+    grad_down, keys_down = grad_mixed.T, keys.T
+    pairs = [slice(head // 2 * LANES, (head // 2 + 1) * LANES) for head in range(HEADS)]
+    chances = [chances_ref[head] for head in range(HEADS)]
+    grad_chances = [
+        matmul(values[:, at] * marks[head % 2], grad_down[at]) for head, at in enumerate(pairs)
+    ]
+    grad_values = [matmul(item.astype(BF), grad_mixed[:, at]) for item, at in zip(chances, pairs)]
+    held = [jnp.sum(one * two, 0, keepdims=True) for one, two in zip(chances, grad_chances)]
+    grad_scores = [
+        (one * (two - total)).astype(BF) for one, two, total in zip(chances, grad_chances, held)
+    ]
+    grad_keys = [matmul(item, query[:, at]) for item, at in zip(grad_scores, pairs)]
+    grad_query = [
+        matmul(keys_down[head * HEAD_DIM : (head + 1) * HEAD_DIM], item)
+        for head, item in enumerate(grad_scores)
+    ]
+    turned = (jnp.concatenate(grad_query, 0) * FACTOR).astype(BF).T
+    return [
+        turned,
+        (join_pairs(grad_keys) * FACTOR).astype(BF),
+        join_pairs(grad_values).astype(BF),
+    ]
 
 
 def tiles_of(array):
@@ -423,7 +425,7 @@
     rows = lax.broadcasted_iota(jnp.int32, (length, length), 0)
     columns = lax.broadcasted_iota(jnp.int32, (length, length), 1)
     reach = jnp.where(causal, 0, length)
-    allowed = equal_ids(ids, ids) & (rows + reach >= columns)
+    allowed = equal_ids(ids, ids) & (columns + reach >= rows)
     mixed = attend(*thirds(room.projected), allowed, room.chances)
     room.mixed[...] = mixed
     room.leave("chances", "mixed")
@@ -479,7 +481,7 @@
         query,
         room.c_paired[:, :width],
         room.c_paired[:, width:],
-        equal_ids(target_ids, source_ids),
+        equal_ids(source_ids, target_ids),
         room.c_chances,
     )
     room.c_mixed[...] = mixed
@@ -804,7 +806,7 @@
         return jax.ShapeDtypeStruct(shape, F32)
 
     slabs, units, scales = low(length, width), full(length, width), full(length, LANES)
-    chances = full(width // SLAB, PER_SLAB * length, length)
+    chances = full(HEADS, length, length)
     attended = dict(
         projected=low(length, 3 * width), chances=chances, mixed=slabs, unit=units, scale=scales
     )
@@ -1021,14 +1023,14 @@
 
     team_w = Team(
         line,
-        (YZX, ZXY),
+        (XYZ, YZX),
         False,
         decoder_narrow=decoder_narrow,
         decoder_widen=decoder_widen,
     )
     team_q = Team(
         line,
-        (XYZ, XYZ),
+        (ZYX, ZYX),
         False,
         decoder_cross_query=decoder_cross_query,
         decoder_cross_memory=decoder_cross_memory,
@@ -1046,11 +1048,16 @@
         (XYZ, YXZ),
         False,
         encoder_narrow=encoder_narrow,
+    )
+    team_f = Team(
+        line,
+        (XZY, XYZ),
+        False,
         encoder_widen=encoder_widen,
     )
     team_s = Team(
         line,
-        (YXZ, XZY),
+        (XYZ, YXZ),
         True,
         encoder_inward=encoder_inward,
         encoder_outward=encoder_outward,
@@ -1060,27 +1067,31 @@
     self_packet, turned, d_self = d_self_run()
     encoder_packet, ended, e_all = encoder_run(turned.d_inputs)
     team_r.grads((self_packet, d_self))
-    team_s.grads((encoder_packet, e_all))
     team_w.step()
     team_e.grads((encoder_packet, e_all))
     team_q.step()
     team_r.step()
+    team_f.grads((encoder_packet, e_all))
     team_w.step()
+    team_s.grads((encoder_packet, e_all))
+    team_q.step()
+    team_e.step()
+    team_r.step()
+    team_f.step()
+    team_q.step()
+    team_w.step()
+    team_e.step()
+    team_r.step()
     team_s.step()
-    team_q.step()
-    team_r.step()
-    team_e.step()
-    team_q.step()
-    team_s.step()
+    team_f.step()
+    team_w.end()
     (theirs,) = line.after(ended.sides_theirs)
     theirs = pair_swap(theirs, "section", 1)
-    team_w.step()
+    team_r.end()
+    team_s.step()
     team_e.step()
-    team_q.end()
+    team_f.step()
     team_s.step()
-    team_r.step()
-    team_e.step()
-    team_w.end()
     mine, theirs = line.after(ended.sides_mine, theirs)
     results, gradients = (
         jnp.stack(
@@ -1092,12 +1103,13 @@
         for i in (0, 1)
     )
     line.mark(gradients)
+    team_q.end()
+    team_f.end()
+    team_e.end()
     team_s.end()
-    team_r.end()
-    team_e.end()
 
     done = {}
-    for team in (team_w, team_q, team_r, team_e, team_s):
+    for team in (team_w, team_q, team_r, team_e, team_f, team_s):
         done.update(team.done)
     deltas = SimpleNamespace(**done)
     shares = team_s.shares

time: 98.8 us -> 93.1 us (0.942)
  Pallas kernels: 38 us -> 32.9 us
  starting transfers between devices: 37.5 us -> 35.4 us
  waiting for transfers between devices: 19.4 us -> 21.3 us
    ppermute x20 -> x24, waiting for transfers between devices: 17.9 us -> 21.3 us  [go(): self.came = lax.ppermute(self.sent, ('section', 'rows'), route)]
    ppermute x20 -> x24, starting transfers between devices: 32.3 us -> 30 us  [go(): self.came = lax.ppermute(self.sent, ('section', 'rows'), route)]
    pallas_call x15 -> x18, Pallas kernels: 3.79 us -> 1.56 us  [halve(): pl.pallas_call(kernel, out_shape=[half, half], in_specs=[VMEM] * 2, out_s...]
    pallas_call x5 -> x6, Pallas kernels: 5.91 us -> 4.12 us  [weight_grads(): pl.pallas_call(kernel, out_shape=[half, half], in_specs=[VMEM] * len(arra...]
    pallas_call x5, Pallas kernels: 24.8 us -> 23.2 us  [call(): pl.pallas_call(kernel, out_shape=shapes_out, in_specs=[HBM] * len(arrays)...]
    ppermute x6, waiting for transfers between devices: 1.5 us -> 0.02 us  [pair_swap(): return lax.ppermute(value, axis, [(i, i ^ apart) for i in range(count)])]
    pallas_call x5 -> x6, Pallas kernels: 3.42 us -> 4.04 us  [end(): pl.pallas_call(kernel, out_shape=outs, in_specs=[VMEM] * 2, out_specs=[VM...]
  transfers between devices with their start and end apart: 26 -> 30, of which waited for: 10 -> 13; matrix products, arithmetic and copies ran while one was open for 2% -> 2% of each run, Pallas kernels for 29% -> 26%
where the time goes in v4:
time: 93.1 us; the launch traced here: 92.9 us
  starting transfers between devices  35.4 us (38%)
  Pallas kernels  32.9 us (35%)
  waiting for transfers between devices  21.3 us (23%)
  other arithmetic  1.49 us (2%)
    ppermute x24, starting transfers between devices, go(): self.came = lax.ppermute(self.sent, ('section', 'rows'), route)  30 us
    pallas_call x5, Pallas kernels, call(): pl.pallas_call(kernel, out_shape=shapes_out, in_specs=[HBM] * len(arrays)...  23.2 us
    ppermute x24, waiting for transfers between devices, go(): self.came = lax.ppermute(self.sent, ('section', 'rows'), route)  21.3 us
    ppermute x6, starting transfers between devices, pair_swap(): return lax.ppermute(value, axis, [(i, i ^ apart) for i in range(count)])  5.36 us
    pallas_call x6, Pallas kernels, weight_grads(): pl.pallas_call(kernel, out_shape=[half, half], in_specs=[VMEM] * len(arra...  4.12 us
    pallas_call x6, Pallas kernels, end(): pl.pallas_call(kernel, out_shape=outs, in_specs=[VMEM] * 2, out_specs=[VM...  4.04 us
  transfers between devices with their start and end apart: 30, of which 13 were waited for; matrix products, arithmetic and copies ran while one was open for 2% of the time, Pallas kernels for 26%

profile of v4, /device:TPU:0, one launch (start us, length us, event | category | flops | bytes accessed | tf_op | source)
XLA Modules:
  0.0 92.9 jit_solution(1935708797051491356)
XLA Ops:
  1.6 3.0 %collective-permute-start = (bf16[128,512]{1,0:T(8,128)(2,1)S(1)}, bf16[128,512]{1,0:T(8,128)(2,1)S(1)}, u32[]{:S(2)}, u32[]{:S(2)}) collective-permute-start(bf16[128,512]{1,0:T(8,128)(2,1)S(1)} %dynamic-slice_bitcast_fusion), channel_id=1, source_target_pairs={{0,16},{16,0},{1,17},{17,1},{2,18},{18,2},{3,19},{19,3},{4,20},{20... | collective-permute-start | bytes 393224 | tf_op jit(solution)/shard_map/ppermute | solution.py:642
  4.6 3.8 %shard_map.305 = (bf16[512,1536]{1,0:T(8,128)(2,1)S(1)}, bf16[512,512]{1,0:T(8,128)(2,1)S(1)}, f32[128,512]{1,0:T(8,128)}, bf16[128,1536]{1,0:T(8,128)(2,1)}, f3...) custom-call(s32[2,2,1,128]{3,2,1,0:T(1,128)} %refs_0_.4, ...), custom_call_target="tpu_custom_call" | custom-call | flops 22000001024 | bytes 1 | tf_op jit(solution)/shard_map/pallas_call | solution.py:292
  8.4 8.2 %shard_map.306 = (bf16[128,512]{1,0:T(8,128)(2,1)S(1)}, bf16[128,512]{1,0:T(8,128)(2,1)S(1)}, bf16[128,1536]{1,0:T(8,128)(2,1)S(1)}, f32[8,128,128]{2,1,0:T(8,12...) custom-call(s32[2,2,1,128]{3,2,1,0:T(1,128)} %refs_0_.4, ...), custom_call_target="tpu_custom_call" | custom-call | flops 60500000768 | bytes 1 | tf_op jit(solution)/shard_map/pallas_call | solution.py:292
  16.6 2.5 %shard_map.307 = (bf16[128,512]{1,0:T(8,128)(2,1)S(1)}, f32[128,512]{1,0:T(8,128)S(1)}, f32[4,512]{1,0:T(4,128)S(1)}, bf16[768,128]{1,0:T(8,128)(2,1)S(1)}, bf16[2816,128]{1,0:T(8,128)(2,1)S(1)}) custom-call(f32[128,512]{1,0:T(8,128)} %get-tuple-element.201.refs_0_, f32[128,128]{1,0:T(8,128)} %get-tuple-element.202.refs_1_, ...), custom_call_target="tpu_custom_call" | custom-call | flops 25849999360 | bytes 1 | tf_op jit(solution)/shard_map/pallas_call | solution.py:292
  20.8 1.4 %collective-permute-start.3 = (bf16[8,256,256]{2,1,0:T(8,128)(2,1)S(1)}, bf16[8,256,256]{2,1,0:T(8,128)(2,1)S(1)}, u32[]{:S(2)}, u32[]{:S(2)}) collective-permute-start(bf16[8,256,256]{2,1,0:T(8,128)(2,1)S(1)} %get-tuple-element.234), channel_id=1, source_target_pairs={{0,16},{1,3},{2,18},{3,1},{4,20},{5,7},{6,22},{7,5},{8,24},{9,11},... | collective-permute-start | bytes 3145736 | tf_op jit(solution)/shard_map/ppermute | solution.py:691
  22.8 1.6 %collective-permute-start.8 = (bf16[8,128,256]{2,1,0:T(8,128)(2,1)S(1)}, bf16[8,128,256]{2,1,0:T(8,128)(2,1)S(1)}, u32[]{:S(2)}, u32[]{:S(2)}) collective-permute-start(bf16[8,128,256]{2,1,0:T(8,128)(2,1)S(1)} %get-tuple-element.238), channel_id=1, source_target_pairs={{0,4},{1,5},{2,6},{3,7},{4,0},{5,1},{6,2},{7,3},{8,12},{9,13},{10,... | collective-permute-start | bytes 1572872 | tf_op jit(solution)/shard_map/ppermute | solution.py:691
  24.4 3.5 %shard_map.310 = (bf16[128,512]{1,0:T(8,128)(2,1)S(1)}, bf16[512,128]{1,0:T(8,128)(2,1)S(1)}, bf16[2560,128]{1,0:T(8,128)(2,1)S(1)}) custom-call(bf16[512,512]{1,0:T(8,128)(2,1)} %refs_0_.5, bf16[128,1536]{1,0:T(8,128)(2,1)} %get-tuple-element.203.refs_1_.refs_2_, f32[8,128,128]{2,1,0:T(8,128)} %get-tuple-element.204.refs_2_.refs_3_, ...), custom_call_target="tpu_custom_call" | custom-call | flops 27499999232 | bytes 1 | tf_op jit(solution)/shard_map/pallas_call | solution.py:292
  28.0 5.3 %shard_map.311 = (bf16[2,128,512]{2,1,0:T(8,128)(2,1)S(1)}, bf16[2,128,512]{2,1,0:T(8,128)(2,1)S(1)}, bf16[1792,128]{1,0:T(8,128)(2,1)S(1)}, bf16[6464,128]{1,0:T(8,128)(2,1)S(1)}) custom-call(f32[128,512]{1,0:T(8,128)} %get-tuple-element.201.refs_0_, f32[128,128]{1,0:T(8,128)} %get-tuple-element.202.refs_1_, ...), custom_call_target="tpu_custom_call" | custom-call | flops 44000002048 | bytes 1 | tf_op jit(solution)/shard_map/pallas_call | solution.py:292
  35.9 1.6 %collective-permute-start.5 = (bf16[4,256,256]{2,1,0:T(8,128)(2,1)S(1)}, bf16[4,256,256]{2,1,0:T(8,128)(2,1)S(1)}, u32[]{:S(2)}, u32[]{:S(2)}) collective-permute-start(bf16[4,256,256]{2,1,0:T(8,128)(2,1)S(1)} %get-tuple-element.269), channel_id=1, source_target_pairs={{0,2},{1,5},{2,0},{3,7},{4,6},{5,1},{6,4},{7,3},{8,10},{9,13},{10,... | collective-permute-start | bytes 1572872 | tf_op jit(solution)/shard_map/ppermute | solution.py:691
  38.1 1.4 %collective-permute-start.14 = (bf16[8,128,256]{2,1,0:T(8,128)(2,1)S(1)}, bf16[8,128,256]{2,1,0:T(8,128)(2,1)S(1)}, u32[]{:S(2)}, u32[]{:S(2)}) collective-permute-start(bf16[8,128,256]{2,1,0:T(8,128)(2,1)S(1)} %get-tuple-element.277), channel_id=1, source_target_pairs={{0,16},{1,3},{2,18},{3,1},{4,20},{5,7},{6,22},{7,5},{8,24},{9,11},... | collective-permute-start | bytes 1572872 | tf_op jit(solution)/shard_map/ppermute | solution.py:691
  39.6 2.7 %collective-permute-start.10 = (bf16[4,128,256]{2,1,0:T(8,128)(2,1)S(1)}, bf16[4,128,256]{2,1,0:T(8,128)(2,1)S(1)}, u32[]{:S(2)}, u32[]{:S(2)}) collective-permute-start(bf16[4,128,256]{2,1,0:T(8,128)(2,1)S(1)} %get-tuple-element.280), channel_id=1, source_target_pairs={{0,8},{1,9},{2,10},{3,11},{4,12},{5,13},{6,14},{7,15},{8,0},{9,1},... | collective-permute-start | bytes 786440 | tf_op jit(solution)/shard_map/ppermute | solution.py:691
  42.3 1.4 %collective-permute-done.7.came_ref = bf16[8,128,256]{2,1,0:T(8,128)(2,1)S(1)} collective-permute-done((bf16[8,128,256]{2,1,0:T(8,128)(2,1)S(1)}, bf16[8,128,256]{2,1,0:T(8,128)(2,1)S(1)}, u32[]{:S(2)}, u32[]{:S(2)}) %collective-permute-start.7) | collective-permute-done | bytes 524320 | tf_op jit(solution)/shard_map/ppermute | solution.py:691
  45.6 5.2 %collective-permute-done.5.came_ref = bf16[4,256,256]{2,1,0:T(8,128)(2,1)S(1)} collective-permute-done((bf16[4,256,256]{2,1,0:T(8,128)(2,1)S(1)}, bf16[4,256,256]{2,1,0:T(8,128)(2,1)S(1)}, u32[]{:S(2)}, u32[]{:S(2)}) %collective-permute-start.5) | collective-permute-done | bytes 524320 | tf_op jit(solution)/shard_map/ppermute | solution.py:691
  51.0 1.6 %collective-permute-start.9 = (bf16[2,256,256]{2,1,0:T(8,128)(2,1)S(1)}, bf16[2,256,256]{2,1,0:T(8,128)(2,1)S(1)}, u32[]{:S(2)}, u32[]{:S(2)}) collective-permute-start(bf16[2,256,256]{2,1,0:T(8,128)(2,1)S(1)} %get-tuple-element.291), channel_id=1, source_target_pairs={{0,4},{1,9},{2,6},{3,11},{4,0},{5,13},{6,2},{7,15},{8,12},{9,1},{1... | collective-permute-start | bytes 786440 | tf_op jit(solution)/shard_map/ppermute | solution.py:691
  53.3 2.2 %collective-permute-done.10.came_ref = bf16[4,128,256]{2,1,0:T(8,128)(2,1)S(1)} collective-permute-done((bf16[4,128,256]{2,1,0:T(8,128)(2,1)S(1)}, bf16[4,128,256]{2,1,0:T(8,128)(2,1)S(1)}, u32[]{:S(2)}, u32[]{:S(2)}) %collective-permute-start.10) | collective-permute-done | bytes 262176 | tf_op jit(solution)/shard_map/ppermute | solution.py:691
  58.6 1.7 %collective-permute-done.12.came_ref = bf16[8,128,256]{2,1,0:T(8,128)(2,1)S(1)} collective-permute-done((bf16[8,128,256]{2,1,0:T(8,128)(2,1)S(1)}, bf16[8,128,256]{2,1,0:T(8,128)(2,1)S(1)}, u32[]{:S(2)}, u32[]{:S(2)}) %collective-permute-start.12) | collective-permute-done | bytes 524320 | tf_op jit(solution)/shard_map/ppermute | solution.py:691
  60.3 2.6 %collective-permute-start.18 = (bf16[2,128,256]{2,1,0:T(8,128)(2,1)S(1)}, bf16[2,128,256]{2,1,0:T(8,128)(2,1)S(1)}, u32[]{:S(2)}, u32[]{:S(2)}) collective-permute-start(bf16[2,128,256]{2,1,0:T(8,128)(2,1)S(1)} %get-tuple-element.309), channel_id=1, source_target_pairs={{0,8},{1,9},{2,10},{3,11},{4,12},{5,13},{6,14},{7,15},{8,0},{9,1},... | collective-permute-start | bytes 393224 | tf_op jit(solution)/shard_map/ppermute | solution.py:691
  63.2 1.5 %collective-permute-start.29 = (bf16[1,128,256]{2,1,0:T(8,128)(2,1)S(1)}, bf16[1,128,256]{2,1,0:T(8,128)(2,1)S(1)}, u32[]{:S(2)}, u32[]{:S(2)}) collective-permute-start(bf16[1,128,256]{2,1,0:T(8,128)(2,1)S(1)} %get-tuple-element.315), channel_id=1, source_target_pairs={{0,16},{1,17},{2,18},{3,19},{4,20},{5,21},{6,22},{7,23},{8,24},{9,... | collective-permute-start | bytes 196616 | tf_op jit(solution)/shard_map/ppermute | solution.py:691
  64.8 3.0 %collective-permute-done.19.came_ref = bf16[4,128,256]{2,1,0:T(8,128)(2,1)S(1)} collective-permute-done((bf16[4,128,256]{2,1,0:T(8,128)(2,1)S(1)}, bf16[4,128,256]{2,1,0:T(8,128)(2,1)S(1)}, u32[]{:S(2)}, u32[]{:S(2)}) %collective-permute-start.19) | collective-permute-done | bytes 262176 | tf_op jit(solution)/shard_map/ppermute | solution.py:691
  72.2 1.6 %collective-permute-start.21 = (bf16[4,144,256]{2,1,0:T(8,128)(2,1)S(1)}, bf16[4,144,256]{2,1,0:T(8,128)(2,1)S(1)}, u32[]{:S(2)}, u32[]{:S(2)}) collective-permute-start(bf16[4,144,256]{2,1,0:T(8,128)(2,1)S(1)} %get-tuple-element.332), channel_id=1, source_target_pairs={{0,2},{1,17},{2,0},{3,19},{4,6},{5,21},{6,4},{7,23},{8,10},{9,25},... | collective-permute-start | bytes 884744 | tf_op jit(solution)/shard_map/ppermute | solution.py:691
  79.0 1.6 %collective-permute-start.23 = (bf16[2,144,256]{2,1,0:T(8,128)(2,1)S(1)}, bf16[2,144,256]{2,1,0:T(8,128)(2,1)S(1)}, u32[]{:S(2)}, u32[]{:S(2)}) collective-permute-start(bf16[2,144,256]{2,1,0:T(8,128)(2,1)S(1)} %get-tuple-element.348), channel_id=1, source_target_pairs={{0,4},{1,5},{2,6},{3,7},{4,0},{5,1},{6,2},{7,3},{8,12},{9,13},{10,... | collective-permute-start | bytes 442376 | tf_op jit(solution)/shard_map/ppermute | solution.py:691
  80.6 1.9 %collective-permute-start.27 = (bf16[1,128,256]{2,1,0:T(8,128)(2,1)S(1)}, bf16[1,128,256]{2,1,0:T(8,128)(2,1)S(1)}, u32[]{:S(2)}, u32[]{:S(2)}) collective-permute-start(bf16[1,128,256]{2,1,0:T(8,128)(2,1)S(1)} %get-tuple-element.353), channel_id=1, source_target_pairs={{0,8},{1,9},{2,10},{3,11},{4,12},{5,13},{6,14},{7,15},{8,0},{9,1},... | collective-permute-start | bytes 196616 | tf_op jit(solution)/shard_map/ppermute | solution.py:691
  83.2 3.0 %collective-permute-done.23.came_ref = bf16[2,144,256]{2,1,0:T(8,128)(2,1)S(1)} collective-permute-done((bf16[2,144,256]{2,1,0:T(8,128)(2,1)S(1)}, bf16[2,144,256]{2,1,0:T(8,128)(2,1)S(1)}, u32[]{:S(2)}, u32[]{:S(2)}) %collective-permute-start.23) | collective-permute-done | bytes 147488 | tf_op jit(solution)/shard_map/ppermute | solution.py:691
  86.2 2.4 %collective-permute-start.26 = (bf16[1,144,256]{2,1,0:T(8,128)(2,1)S(1)}, bf16[1,144,256]{2,1,0:T(8,128)(2,1)S(1)}, u32[]{:S(2)}, u32[]{:S(2)}) collective-permute-start(bf16[1,144,256]{2,1,0:T(8,128)(2,1)S(1)} %get-tuple-element.359), channel_id=1, source_target_pairs={{0,8},{1,9},{2,10},{3,11},{4,12},{5,13},{6,14},{7,15},{8,0},{9,1},... | collective-permute-start | bytes 221192 | tf_op jit(solution)/shard_map/ppermute | solution.py:691
  (75 shorter events, 27.2 us)
Async XLA Ops:
  1.6 6.8 %collective-permute-start = (bf16[128,512]{1,0:T(8,128)(2,1)S(1)}, bf16[128,512]{1,0:T(8,128)(2,1)S(1)}, u32[]{:S(2)}, u32[]{:S(2)}) collective-permute-start(bf16[128,512]{1,0:T(8,128)(2,1)S(1)} %dynamic-slice_bitcast_fusion), channel_id=1, source_target_pairs={{0,16},{16,0},{1,17},{17,1},{2,18},{18,2},{3,19},{19,3},{4,20},{20... | collective-permute-start | bytes 393224 | tf_op jit(solution)/shard_map/ppermute | solution.py:642
  20.8 14.9 %collective-permute-start.3 = (bf16[8,256,256]{2,1,0:T(8,128)(2,1)S(1)}, bf16[8,256,256]{2,1,0:T(8,128)(2,1)S(1)}, u32[]{:S(2)}, u32[]{:S(2)}) collective-permute-start(bf16[8,256,256]{2,1,0:T(8,128)(2,1)S(1)} %get-tuple-element.234), channel_id=1, source_target_pairs={{0,16},{1,3},{2,18},{3,1},{4,20},{5,7},{6,22},{7,5},{8,24},{9,11},... | collective-permute-start | bytes 3145736 | tf_op jit(solution)/shard_map/ppermute | solution.py:691
  22.8 16.7 %collective-permute-start.8 = (bf16[8,128,256]{2,1,0:T(8,128)(2,1)S(1)}, bf16[8,128,256]{2,1,0:T(8,128)(2,1)S(1)}, u32[]{:S(2)}, u32[]{:S(2)}) collective-permute-start(bf16[8,128,256]{2,1,0:T(8,128)(2,1)S(1)} %get-tuple-element.238), channel_id=1, source_target_pairs={{0,4},{1,5},{2,6},{3,7},{4,0},{5,1},{6,2},{7,3},{8,12},{9,13},{10,... | collective-permute-start | bytes 1572872 | tf_op jit(solution)/shard_map/ppermute | solution.py:691
  34.5 9.2 %collective-permute-start.7 = (bf16[8,128,256]{2,1,0:T(8,128)(2,1)S(1)}, bf16[8,128,256]{2,1,0:T(8,128)(2,1)S(1)}, u32[]{:S(2)}, u32[]{:S(2)}) collective-permute-start(bf16[8,128,256]{2,1,0:T(8,128)(2,1)S(1)} %get-tuple-element.265), channel_id=1, source_target_pairs={{0,16},{1,3},{2,18},{3,1},{4,20},{5,7},{6,22},{7,5},{8,24},{9,11},... | collective-permute-start | bytes 1572872 | tf_op jit(solution)/shard_map/ppermute | solution.py:691
  35.9 14.9 %collective-permute-start.5 = (bf16[4,256,256]{2,1,0:T(8,128)(2,1)S(1)}, bf16[4,256,256]{2,1,0:T(8,128)(2,1)S(1)}, u32[]{:S(2)}, u32[]{:S(2)}) collective-permute-start(bf16[4,256,256]{2,1,0:T(8,128)(2,1)S(1)} %get-tuple-element.269), channel_id=1, source_target_pairs={{0,2},{1,5},{2,0},{3,7},{4,6},{5,1},{6,4},{7,3},{8,10},{9,13},{10,... | collective-permute-start | bytes 1572872 | tf_op jit(solution)/shard_map/ppermute | solution.py:691
  38.1 18.2 %collective-permute-start.14 = (bf16[8,128,256]{2,1,0:T(8,128)(2,1)S(1)}, bf16[8,128,256]{2,1,0:T(8,128)(2,1)S(1)}, u32[]{:S(2)}, u32[]{:S(2)}) collective-permute-start(bf16[8,128,256]{2,1,0:T(8,128)(2,1)S(1)} %get-tuple-element.277), channel_id=1, source_target_pairs={{0,16},{1,3},{2,18},{3,1},{4,20},{5,7},{6,22},{7,5},{8,24},{9,11},... | collective-permute-start | bytes 1572872 | tf_op jit(solution)/shard_map/ppermute | solution.py:691
  39.6 15.9 %collective-permute-start.10 = (bf16[4,128,256]{2,1,0:T(8,128)(2,1)S(1)}, bf16[4,128,256]{2,1,0:T(8,128)(2,1)S(1)}, u32[]{:S(2)}, u32[]{:S(2)}) collective-permute-start(bf16[4,128,256]{2,1,0:T(8,128)(2,1)S(1)} %get-tuple-element.280), channel_id=1, source_target_pairs={{0,8},{1,9},{2,10},{3,11},{4,12},{5,13},{6,14},{7,15},{8,0},{9,1},... | collective-permute-start | bytes 786440 | tf_op jit(solution)/shard_map/ppermute | solution.py:691
  43.8 13.3 %collective-permute-start.13 = (bf16[4,128,256]{2,1,0:T(8,128)(2,1)S(1)}, bf16[4,128,256]{2,1,0:T(8,128)(2,1)S(1)}, u32[]{:S(2)}, u32[]{:S(2)}) collective-permute-start(bf16[4,128,256]{2,1,0:T(8,128)(2,1)S(1)} %get-tuple-element.283), channel_id=1, source_target_pairs={{0,4},{1,5},{2,6},{3,7},{4,0},{5,1},{6,2},{7,3},{8,12},{9,13},{10,... | collective-permute-start | bytes 786440 | tf_op jit(solution)/shard_map/ppermute | solution.py:691
  44.9 15.4 %collective-permute-start.12 = (bf16[8,128,256]{2,1,0:T(8,128)(2,1)S(1)}, bf16[8,128,256]{2,1,0:T(8,128)(2,1)S(1)}, u32[]{:S(2)}, u32[]{:S(2)}) collective-permute-start(bf16[8,128,256]{2,1,0:T(8,128)(2,1)S(1)} %get-tuple-element.287), channel_id=1, source_target_pairs={{0,16},{1,17},{2,18},{3,19},{4,20},{5,21},{6,22},{7,23},{8,24},{9,... | collective-permute-start | bytes 1572872 | tf_op jit(solution)/shard_map/ppermute | solution.py:691
  51.0 12.2 %collective-permute-start.9 = (bf16[2,256,256]{2,1,0:T(8,128)(2,1)S(1)}, bf16[2,256,256]{2,1,0:T(8,128)(2,1)S(1)}, u32[]{:S(2)}, u32[]{:S(2)}) collective-permute-start(bf16[2,256,256]{2,1,0:T(8,128)(2,1)S(1)} %get-tuple-element.291), channel_id=1, source_target_pairs={{0,4},{1,9},{2,6},{3,11},{4,0},{5,13},{6,2},{7,15},{8,12},{9,1},{1... | collective-permute-start | bytes 786440 | tf_op jit(solution)/shard_map/ppermute | solution.py:691
  55.5 15.3 %collective-permute-start.17 = (bf16[8,144,256]{2,1,0:T(8,128)(2,1)S(1)}, bf16[8,144,256]{2,1,0:T(8,128)(2,1)S(1)}, u32[]{:S(2)}, u32[]{:S(2)}) collective-permute-start(bf16[8,144,256]{2,1,0:T(8,128)(2,1)S(1)} %get-tuple-element.296), channel_id=1, source_target_pairs={{0,16},{1,3},{2,18},{3,1},{4,20},{5,7},{6,22},{7,5},{8,24},{9,11},... | collective-permute-start | bytes 1769480 | tf_op jit(solution)/shard_map/ppermute | solution.py:691
  56.3 6.8 %collective-permute-start.11 = (bf16[2,128,256]{2,1,0:T(8,128)(2,1)S(1)}, bf16[2,128,256]{2,1,0:T(8,128)(2,1)S(1)}, u32[]{:S(2)}, u32[]{:S(2)}) collective-permute-start(bf16[2,128,256]{2,1,0:T(8,128)(2,1)S(1)} %get-tuple-element.300), channel_id=1, source_target_pairs={{0,2},{1,3},{2,0},{3,1},{4,6},{5,7},{6,4},{7,5},{8,10},{9,11},{10,... | collective-permute-start | bytes 393224 | tf_op jit(solution)/shard_map/ppermute | solution.py:691
  57.2 10.6 %collective-permute-start.19 = (bf16[4,128,256]{2,1,0:T(8,128)(2,1)S(1)}, bf16[4,128,256]{2,1,0:T(8,128)(2,1)S(1)}, u32[]{:S(2)}, u32[]{:S(2)}) collective-permute-start(bf16[4,128,256]{2,1,0:T(8,128)(2,1)S(1)} %get-tuple-element.306), channel_id=1, source_target_pairs={{0,2},{1,17},{2,0},{3,19},{4,6},{5,21},{6,4},{7,23},{8,10},{9,25},... | collective-permute-start | bytes 786440 | tf_op jit(solution)/shard_map/ppermute | solution.py:691
  60.3 9.5 %collective-permute-start.18 = (bf16[2,128,256]{2,1,0:T(8,128)(2,1)S(1)}, bf16[2,128,256]{2,1,0:T(8,128)(2,1)S(1)}, u32[]{:S(2)}, u32[]{:S(2)}) collective-permute-start(bf16[2,128,256]{2,1,0:T(8,128)(2,1)S(1)} %get-tuple-element.309), channel_id=1, source_target_pairs={{0,8},{1,9},{2,10},{3,11},{4,12},{5,13},{6,14},{7,15},{8,0},{9,1},... | collective-permute-start | bytes 393224 | tf_op jit(solution)/shard_map/ppermute | solution.py:691
  63.1 9.1 %collective-permute-start.16 = (bf16[4,128,256]{2,1,0:T(8,128)(2,1)S(1)}, bf16[4,128,256]{2,1,0:T(8,128)(2,1)S(1)}, u32[]{:S(2)}, u32[]{:S(2)}) collective-permute-start(bf16[4,128,256]{2,1,0:T(8,128)(2,1)S(1)} %get-tuple-element.312), channel_id=1, source_target_pairs={{0,4},{1,3},{2,6},{3,1},{4,0},{5,7},{6,2},{7,5},{8,12},{9,11},{10,... | collective-permute-start | bytes 786440 | tf_op jit(solution)/shard_map/ppermute | solution.py:691
  63.2 26.2 %collective-permute-start.29 = (bf16[1,128,256]{2,1,0:T(8,128)(2,1)S(1)}, bf16[1,128,256]{2,1,0:T(8,128)(2,1)S(1)}, u32[]{:S(2)}, u32[]{:S(2)}) collective-permute-start(bf16[1,128,256]{2,1,0:T(8,128)(2,1)S(1)} %get-tuple-element.315), channel_id=1, source_target_pairs={{0,16},{1,17},{2,18},{3,19},{4,20},{5,21},{6,22},{7,23},{8,24},{9,... | collective-permute-start | bytes 196616 | tf_op jit(solution)/shard_map/ppermute | solution.py:691
  67.8 7.1 %collective-permute-start.15 = (bf16[1,256,256]{2,1,0:T(8,128)(2,1)S(1)}, bf16[1,256,256]{2,1,0:T(8,128)(2,1)S(1)}, u32[]{:S(2)}, u32[]{:S(2)}) collective-permute-start(bf16[1,256,256]{2,1,0:T(8,128)(2,1)S(1)} %get-tuple-element.319), channel_id=1, source_target_pairs={{0,8},{1,17},{2,10},{3,19},{4,12},{5,21},{6,14},{7,23},{8,0},{9,25... | collective-permute-start | bytes 393224 | tf_op jit(solution)/shard_map/ppermute | solution.py:691
  69.9 10.7 %collective-permute-start.25 = (bf16[2,128,256]{2,1,0:T(8,128)(2,1)S(1)}, bf16[2,128,256]{2,1,0:T(8,128)(2,1)S(1)}, u32[]{:S(2)}, u32[]{:S(2)}) collective-permute-start(bf16[2,128,256]{2,1,0:T(8,128)(2,1)S(1)} %get-tuple-element.326), channel_id=1, source_target_pairs={{0,4},{1,5},{2,6},{3,7},{4,0},{5,1},{6,2},{7,3},{8,12},{9,13},{10,... | collective-permute-start | bytes 393224 | tf_op jit(solution)/shard_map/ppermute | solution.py:691
  72.2 6.7 %collective-permute-start.21 = (bf16[4,144,256]{2,1,0:T(8,128)(2,1)S(1)}, bf16[4,144,256]{2,1,0:T(8,128)(2,1)S(1)}, u32[]{:S(2)}, u32[]{:S(2)}) collective-permute-start(bf16[4,144,256]{2,1,0:T(8,128)(2,1)S(1)} %get-tuple-element.332), channel_id=1, source_target_pairs={{0,2},{1,17},{2,0},{3,19},{4,6},{5,21},{6,4},{7,23},{8,10},{9,25},... | collective-permute-start | bytes 884744 | tf_op jit(solution)/shard_map/ppermute | solution.py:691
  74.8 7.7 %collective-permute-start.24 = (bf16[2,128,256]{2,1,0:T(8,128)(2,1)S(1)}, bf16[2,128,256]{2,1,0:T(8,128)(2,1)S(1)}, u32[]{:S(2)}, u32[]{:S(2)}) collective-permute-start(bf16[2,128,256]{2,1,0:T(8,128)(2,1)S(1)} %get-tuple-element.335), channel_id=1, source_target_pairs={{0,8},{1,5},{2,10},{3,7},{4,12},{5,1},{6,14},{7,3},{8,0},{9,13},{1... | collective-permute-start | bytes 393224 | tf_op jit(solution)/shard_map/ppermute | solution.py:691
  76.5 12.1 %collective-permute-start.20 = (bf16[2,128,512]{2,1,0:T(8,128)(2,1)S(1)}, bf16[2,128,512]{2,1,0:T(8,128)(2,1)S(1)}, u32[]{:S(2)}, u32[]{:S(2)}) collective-permute-start(bf16[2,128,512]{2,1,0:T(8,128)(2,1)S(1)} %get-tuple-element.339), channel_id=1, source_target_pairs={{0,16},{16,0},{1,17},{17,1},{2,18},{18,2},{3,19},{19,3},{4,20},{20... | collective-permute-start | bytes 786440 | tf_op jit(solution)/shard_map/ppermute | solution.py:642
  79.0 7.2 %collective-permute-start.23 = (bf16[2,144,256]{2,1,0:T(8,128)(2,1)S(1)}, bf16[2,144,256]{2,1,0:T(8,128)(2,1)S(1)}, u32[]{:S(2)}, u32[]{:S(2)}) collective-permute-start(bf16[2,144,256]{2,1,0:T(8,128)(2,1)S(1)} %get-tuple-element.348), channel_id=1, source_target_pairs={{0,4},{1,5},{2,6},{3,7},{4,0},{5,1},{6,2},{7,3},{8,12},{9,13},{10,... | collective-permute-start | bytes 442376 | tf_op jit(solution)/shard_map/ppermute | solution.py:691
  80.6 10.0 %collective-permute-start.27 = (bf16[1,128,256]{2,1,0:T(8,128)(2,1)S(1)}, bf16[1,128,256]{2,1,0:T(8,128)(2,1)S(1)}, u32[]{:S(2)}, u32[]{:S(2)}) collective-permute-start(bf16[1,128,256]{2,1,0:T(8,128)(2,1)S(1)} %get-tuple-element.353), channel_id=1, source_target_pairs={{0,8},{1,9},{2,10},{3,11},{4,12},{5,13},{6,14},{7,15},{8,0},{9,1},... | collective-permute-start | bytes 196616 | tf_op jit(solution)/shard_map/ppermute | solution.py:691
  82.6 7.4 %collective-permute-start.28 = (bf16[1,128,256]{2,1,0:T(8,128)(2,1)S(1)}, bf16[1,128,256]{2,1,0:T(8,128)(2,1)S(1)}, u32[]{:S(2)}, u32[]{:S(2)}) collective-permute-start(bf16[1,128,256]{2,1,0:T(8,128)(2,1)S(1)} %get-tuple-element.356), channel_id=1, source_target_pairs={{0,2},{1,9},{2,0},{3,11},{4,6},{5,13},{6,4},{7,15},{8,10},{9,1},{1... | collective-permute-start | bytes 196616 | tf_op jit(solution)/shard_map/ppermute | solution.py:691
  (6 other events, 27.9 us)

commit v5 on v4

--- a/solution.py
+++ b/solution.py
@@ -505,7 +505,8 @@
     packet.stash(
         decoder_narrow=(room.d_hidden[...], grad_low), decoder_widen=(low, grad_before)
     )
-    room.d_grad[...] = grad_sum + matmul_back(grad_before, room.decoder_widen[...])
+    room.d_sum[...] = grad_sum
+    room.d_before[...] = grad_before
     room.d_small2[...] = jnp.concatenate([grad_gain, grad_shift], 0)
 
 
@@ -527,9 +528,9 @@
 
 
 def cross_back_body(room, packet):
-    gain = room.decoder_gain
+    grad_normed = room.d_sum[...] + matmul_back(room.d_before[...], room.decoder_widen[...])
     grad_sum, gain1, shift1 = norm_back(
-        room.d_grad[...], room.d_unit1[...], room.d_scale1[:, :1], gain[1:2]
+        grad_normed, room.d_unit1[...], room.d_scale1[:, :1], room.decoder_gain[1:2]
     )
     grad_low = grad_sum.astype(BF)
     grad_mixed = matmul_back(grad_low, room.decoder_cross_outward[...]).astype(BF)
@@ -545,16 +546,10 @@
         decoder_cross_memory=(room.memory[...], grad_paired),
         decoder_cross_outward=(room.c_mixed[...], grad_low),
     )
-    room.grad_memory[...] = matmul_back(grad_paired, room.decoder_cross_memory[...]).astype(BF)
-    grad_normed = grad_sum + matmul_back(grad_query, room.decoder_cross_query[...])
-    grad_sum, gain0, shift0 = norm_back(
-        grad_normed,
-        room.either(room.far_unit, room.near_unit),
-        room.either(room.far_scale, room.near_scale)[:, :1],
-        gain[0:1],
-    )
-    room.d_grad0[...] = grad_sum
-    room.d_small01[...] = jnp.concatenate([gain0, gain1, shift0, shift1], 0)
+    room.d_sum1[...] = grad_sum
+    room.c_grad_query[...] = grad_query
+    room.c_grad_paired[...] = grad_paired
+    room.d_small1[...] = jnp.concatenate([gain1, shift1], 0)
 
 
 def self_back(grad_sum, inward, outward, tokens, projected, chances, mixed):
@@ -567,8 +562,18 @@
 
 def decoder_self_body(room, packet):
     either = room.either
+    grad_query, grad_paired = room.c_grad_query[...], room.c_grad_paired[...]
+    room.grad_memory[...] = matmul_back(grad_paired, room.decoder_cross_memory[...]).astype(BF)
+    grad_normed = room.d_sum1[...] + matmul_back(grad_query, room.decoder_cross_query[...])
+    grad_sum, gain0, shift0 = norm_back(
+        grad_normed,
+        either(room.far_unit, room.near_unit),
+        either(room.far_scale, room.near_scale)[:, :1],
+        room.decoder_gain[0:1],
+    )
+    room.d_small0[...] = jnp.concatenate([gain0, shift0], 0)
     (inward, outward), grad_inputs = self_back(
-        room.d_grad0[...],
+        grad_sum,
         room.decoder_inward,
         room.decoder_outward,
         either(room.far_tokens, room.near_tokens),
@@ -598,10 +603,12 @@
         either(room.near_scale, room.far_scale)[:, :1],
         gain[0:1],
     )
-    inner, outer = room.d_small01[...], room.d_small2[...]
+    smalls = [room.d_small0[...], room.d_small1[...], room.d_small2[...]]
     small = jnp.concatenate(
-        [gain0, gain1, shift0, shift1, inner[0:2], outer[0:1], inner[2:4], outer[1:2]]
-        + [jnp.zeros((6, inner.shape[1]), F32)],
+        [gain0, gain1, shift0, shift1]
+        + [item[0:1] for item in smalls]
+        + [item[1:2] for item in smalls]
+        + [jnp.zeros((6, gain0.shape[1]), F32)],
         0,
     )
     for place, tile in enumerate(tiles_of(small.astype(BF))):
@@ -890,7 +897,8 @@
             c_mixed=slabs,
             d_unit1=units,
             d_scale1=scales,
-            d_grad=units,
+            d_sum=units,
+            d_before=low(length, wide),
             d_small2=full(2, width),
         ),
         dict(
@@ -901,16 +909,13 @@
             decoder_cross_query=decoder_cross_query,
             decoder_cross_memory=decoder_cross_memory,
             decoder_cross_outward=decoder_cross_outward,
+            decoder_widen=decoder_widen,
         ),
         11,
         14,
         wide_packet,
         dict(d_hidden=low(length, wide), d_slope=full(length, wide)),
-        late=dict(
-            decoder_widen=decoder_widen,
-            decoder_narrow=decoder_narrow,
-            cotangent=Entry(cotangent),
-        ),
+        late=dict(decoder_narrow=decoder_narrow, cotangent=Entry(cotangent)),
     )
 
     cross_packet = Packet(
@@ -920,9 +925,11 @@
     )
     crossed, d_cross = run(
         cross_back_body,
-        dict(near_unit=near.unit, near_scale=near.scale),
+        {},
         dict(
-            d_grad=far.d_grad,
+            d_sum=far.d_sum,
+            d_before=far.d_before,
+            decoder_widen=far.decoder_widen,
             decoder_gain=far.decoder_gain,
             d_unit1=far.d_unit1,
             d_scale1=far.d_scale1,
@@ -933,12 +940,13 @@
             memory=far.memory,
             c_mixed=far.c_mixed,
             decoder_cross_outward=far.decoder_cross_outward,
-            decoder_cross_memory=far.decoder_cross_memory,
-            decoder_cross_query=far.decoder_cross_query,
-            far_unit=far.unit,
-            far_scale=far.scale,
         ),
-        dict(grad_memory=slabs, d_grad0=units, d_small01=full(4, width)),
+        dict(
+            d_sum1=units,
+            c_grad_query=slabs,
+            c_grad_paired=low(length, 2 * width),
+            d_small1=full(2, width),
+        ),
         {},
         4.7,
         5,
@@ -950,6 +958,8 @@
         return packet, *run(
             decoder_self_body,
             dict(
+                near_unit=near.unit,
+                near_scale=near.scale,
                 decoder_outward=decoder_outward,
                 near_projected=near.projected,
                 near_chances=near.chances,
@@ -959,19 +969,26 @@
             ),
             dict(
                 far_tokens=other,
-                d_grad0=crossed.d_grad0,
+                c_grad_query=crossed.c_grad_query,
+                c_grad_paired=crossed.c_grad_paired,
+                d_sum1=crossed.d_sum1,
+                decoder_cross_memory=far.decoder_cross_memory,
+                decoder_cross_query=far.decoder_cross_query,
+                decoder_gain=far.decoder_gain,
+                far_unit=far.unit,
+                far_scale=far.scale,
                 far_projected=far.projected,
                 far_chances=far.chances,
                 far_mixed=far.mixed,
             ),
-            dict(d_inputs=slabs),
+            dict(d_inputs=slabs, grad_memory=slabs, d_small0=full(2, width)),
             {},
             5,
             5,
             packet,
         )
 
-    def encoder_run(d_inputs):
+    def encoder_run(turned):
         packet = Packet(
             64,
             encoder_narrow=encoder_narrow,
@@ -995,7 +1012,7 @@
             dict(
                 far_tokens=other,
                 encoder_gain=far.encoder_gain,
-                grad_memory=crossed.grad_memory,
+                grad_memory=turned.grad_memory,
                 e_unit1=far.e_unit1,
                 e_scale1=far.e_scale1,
                 encoder_narrow=far.encoder_narrow,
@@ -1003,14 +1020,15 @@
                 e_hidden=far.e_hidden,
                 e_low=far.e_low,
                 encoder_widen=far.encoder_widen,
-                d_small01=crossed.d_small01,
+                d_small0=turned.d_small0,
+                d_small1=crossed.d_small1,
                 d_small2=far.d_small2,
                 far_unit=far.unit,
                 far_scale=far.scale,
                 far_projected=far.projected,
                 far_chances=far.chances,
                 far_mixed=far.mixed,
-                d_inputs=d_inputs,
+                d_inputs=turned.d_inputs,
                 memory=far.memory,
                 output=far.output,
             ),
@@ -1045,7 +1063,7 @@
     )
     team_e = Team(
         line,
-        (XYZ, YXZ),
+        (YZX, XYZ),
         False,
         encoder_narrow=encoder_narrow,
     )
@@ -1065,13 +1083,13 @@
     team_w.grads((wide_packet, d_wide))
     team_q.grads((cross_packet, d_cross))
     self_packet, turned, d_self = d_self_run()
-    encoder_packet, ended, e_all = encoder_run(turned.d_inputs)
+    encoder_packet, ended, e_all = encoder_run(turned)
     team_r.grads((self_packet, d_self))
     team_w.step()
+    team_q.step()
     team_e.grads((encoder_packet, e_all))
-    team_q.step()
+    team_f.grads((encoder_packet, e_all))
     team_r.step()
-    team_f.grads((encoder_packet, e_all))
     team_w.step()
     team_s.grads((encoder_packet, e_all))
     team_q.step()

time: 93.1 us -> 91.1 us (0.979)
  waiting for transfers between devices: 21.3 us -> 14.2 us
  starting transfers between devices: 35.4 us -> 41.3 us
    ppermute x24, waiting for transfers between devices: 21.3 us -> 13.9 us  [go(): self.came = lax.ppermute(self.sent, ('section', 'rows'), route)]
    ppermute x24, starting transfers between devices: 30 us -> 36.3 us  [go(): self.came = lax.ppermute(self.sent, ('section', 'rows'), route)]
  transfers between devices with their start and end apart: 30 -> 30, of which waited for: 13 -> 8; matrix products, arithmetic and copies ran while one was open for 2% -> 2% of each run, Pallas kernels for 26% -> 26%
where the time goes in v5:
time: 91.1 us; the launch traced here: 90.9 us
  starting transfers between devices  41.3 us (45%)
  Pallas kernels  32.1 us (35%)
  waiting for transfers between devices  14.2 us (16%)
  other arithmetic  1.49 us (2%)
  between operations  0.93 us (1%)
  local copies, waits for them, and re-layouts  0.92 us (1%)
    ppermute x24, starting transfers between devices, go(): self.came = lax.ppermute(self.sent, ('section', 'rows'), route)  36.3 us
    pallas_call x5, Pallas kernels, call(): pl.pallas_call(kernel, out_shape=shapes_out, in_specs=[HBM] * len(arrays)...  22.4 us
    ppermute x24, waiting for transfers between devices, go(): self.came = lax.ppermute(self.sent, ('section', 'rows'), route)  13.9 us
    ppermute x6, starting transfers between devices, pair_swap(): return lax.ppermute(value, axis, [(i, i ^ apart) for i in range(count)])  5.05 us
    pallas_call x6, Pallas kernels, weight_grads(): pl.pallas_call(kernel, out_shape=[half, half], in_specs=[VMEM] * len(arra...  4.11 us
    pallas_call x6, Pallas kernels, end(): pl.pallas_call(kernel, out_shape=outs, in_specs=[VMEM] * 2, out_specs=[VM...  4.04 us
  transfers between devices with their start and end apart: 30, of which 8 were waited for; matrix products, arithmetic and copies ran while one was open for 2% of the time, Pallas kernels for 26%

profile of v5, /device:TPU:0, one launch (start us, length us, event | category | flops | bytes accessed | tf_op | source)
XLA Modules:
  0.0 90.9 jit_solution(6848959264713999640)
XLA Ops:
  1.6 3.0 %collective-permute-start = (bf16[128,512]{1,0:T(8,128)(2,1)S(1)}, bf16[128,512]{1,0:T(8,128)(2,1)S(1)}, u32[]{:S(2)}, u32[]{:S(2)}) collective-permute-start(bf16[128,512]{1,0:T(8,128)(2,1)S(1)} %dynamic-slice_bitcast_fusion), channel_id=1, source_target_pairs={{0,16},{16,0},{1,17},{17,1},{2,18},{18,2},{3,19},{19,3},{4,20},{20... | collective-permute-start | bytes 393224 | tf_op jit(solution)/shard_map/ppermute | solution.py:649
  4.6 3.8 %shard_map.305 = (bf16[512,1536]{1,0:T(8,128)(2,1)S(1)}, bf16[512,512]{1,0:T(8,128)(2,1)S(1)}, f32[128,512]{1,0:T(8,128)}, bf16[128,1536]{1,0:T(8,128)(2,1)}, f3...) custom-call(s32[2,2,1,128]{3,2,1,0:T(1,128)} %refs_0_.3, ...), custom_call_target="tpu_custom_call" | custom-call | flops 22000001024 | bytes 1 | tf_op jit(solution)/shard_map/pallas_call | solution.py:292
  8.4 7.5 %shard_map.306 = (bf16[128,512]{1,0:T(8,128)(2,1)S(1)}, bf16[128,512]{1,0:T(8,128)(2,1)S(1)}, bf16[128,1536]{1,0:T(8,128)(2,1)S(1)}, f32[8,128,128]{2,1,0:T(8,12...) custom-call(s32[2,2,1,128]{3,2,1,0:T(1,128)} %refs_0_.3, ...), custom_call_target="tpu_custom_call" | custom-call | flops 60500000768 | bytes 1 | tf_op jit(solution)/shard_map/pallas_call | solution.py:292
  16.0 1.7 %shard_map.307 = (f32[128,512]{1,0:T(8,128)S(1)}, bf16[128,512]{1,0:T(8,128)(2,1)S(1)}, bf16[128,1024]{1,0:T(8,128)(2,1)S(1)}, f32[2,512]{1,0:T(2,128)S(1)}, bf1...) custom-call(f32[128,512]{1,0:T(8,128)S(1)} %get-tuple-element.217.refs_0_, ...), custom_call_target="tpu_custom_call" | custom-call | flops 25849999360 | bytes 1 | tf_op jit(solution)/shard_map/pallas_call | solution.py:292
  19.7 1.4 %collective-permute-start.3 = (bf16[8,256,256]{2,1,0:T(8,128)(2,1)S(1)}, bf16[8,256,256]{2,1,0:T(8,128)(2,1)S(1)}, u32[]{:S(2)}, u32[]{:S(2)}) collective-permute-start(bf16[8,256,256]{2,1,0:T(8,128)(2,1)S(1)} %get-tuple-element.237), channel_id=1, source_target_pairs={{0,16},{1,3},{2,18},{3,1},{4,20},{5,7},{6,22},{7,5},{8,24},{9,11},... | collective-permute-start | bytes 3145736 | tf_op jit(solution)/shard_map/ppermute | solution.py:698
  21.7 1.6 %collective-permute-start.8 = (bf16[8,128,256]{2,1,0:T(8,128)(2,1)S(1)}, bf16[8,128,256]{2,1,0:T(8,128)(2,1)S(1)}, u32[]{:S(2)}, u32[]{:S(2)}) collective-permute-start(bf16[8,128,256]{2,1,0:T(8,128)(2,1)S(1)} %get-tuple-element.241), channel_id=1, source_target_pairs={{0,4},{1,5},{2,6},{3,7},{4,0},{5,1},{6,2},{7,3},{8,12},{9,13},{10,... | collective-permute-start | bytes 1572872 | tf_op jit(solution)/shard_map/ppermute | solution.py:698
  23.3 4.1 %shard_map.310 = (bf16[128,512]{1,0:T(8,128)(2,1)S(1)}, bf16[128,512]{1,0:T(8,128)(2,1)S(1)}, f32[2,512]{1,0:T(2,128)S(1)}, bf16[512,128]{1,0:T(8,128)(2,1)S(1)}, bf16[2560,128]{1,0:T(8,128)(2,1)S(1)}) custom-call(f32[128,512]{1,0:T(8,128)} %get-tuple-element.206.refs_0_, f32[128,128]{1,0:T(8,128)} %get-tuple-element.207.refs_1_, bf16[512,512]{1,0:T(8,128)(2,1)} %refs_2_.5, ...), custom_call_target="tpu_custom_call" | custom-call | flops 27499999232 | bytes 1 | tf_op jit(solution)/shard_map/pallas_call | solution.py:292
  27.5 5.3 %shard_map.311 = (bf16[2,128,512]{2,1,0:T(8,128)(2,1)S(1)}, bf16[2,128,512]{2,1,0:T(8,128)(2,1)S(1)}, bf16[1792,128]{1,0:T(8,128)(2,1)S(1)}, bf16[6464,128]{1,0:T(8,128)(2,1)S(1)}) custom-call(f32[128,512]{1,0:T(8,128)} %get-tuple-element.206.refs_0_, f32[128,128]{1,0:T(8,128)} %get-tuple-element.207.refs_1_, ...), custom_call_target="tpu_custom_call" | custom-call | flops 44000002048 | bytes 1 | tf_op jit(solution)/shard_map/pallas_call | solution.py:292
  34.9 1.6 %collective-permute-start.5 = (bf16[4,256,256]{2,1,0:T(8,128)(2,1)S(1)}, bf16[4,256,256]{2,1,0:T(8,128)(2,1)S(1)}, u32[]{:S(2)}, u32[]{:S(2)}) collective-permute-start(bf16[4,256,256]{2,1,0:T(8,128)(2,1)S(1)} %get-tuple-element.279), channel_id=1, source_target_pairs={{0,2},{1,5},{2,0},{3,7},{4,6},{5,1},{6,4},{7,3},{8,10},{9,13},{10,... | collective-permute-start | bytes 1572872 | tf_op jit(solution)/shard_map/ppermute | solution.py:698
  36.6 2.6 %collective-permute-start.10 = (bf16[4,128,256]{2,1,0:T(8,128)(2,1)S(1)}, bf16[4,128,256]{2,1,0:T(8,128)(2,1)S(1)}, u32[]{:S(2)}, u32[]{:S(2)}) collective-permute-start(bf16[4,128,256]{2,1,0:T(8,128)(2,1)S(1)} %get-tuple-element.286), channel_id=1, source_target_pairs={{0,8},{1,9},{2,10},{3,11},{4,12},{5,13},{6,14},{7,15},{8,0},{9,1},... | collective-permute-start | bytes 786440 | tf_op jit(solution)/shard_map/ppermute | solution.py:698
  41.0 1.4 %collective-permute-start.12 = (bf16[8,128,256]{2,1,0:T(8,128)(2,1)S(1)}, bf16[8,128,256]{2,1,0:T(8,128)(2,1)S(1)}, u32[]{:S(2)}, u32[]{:S(2)}) collective-permute-start(bf16[8,128,256]{2,1,0:T(8,128)(2,1)S(1)} %get-tuple-element.294), channel_id=1, source_target_pairs={{0,16},{1,17},{2,18},{3,19},{4,20},{5,21},{6,22},{7,23},{8,24},{9,... | collective-permute-start | bytes 1572872 | tf_op jit(solution)/shard_map/ppermute | solution.py:698
  42.4 2.4 %collective-permute-done.6.came_ref = bf16[8,128,256]{2,1,0:T(8,128)(2,1)S(1)} collective-permute-done((bf16[8,128,256]{2,1,0:T(8,128)(2,1)S(1)}, bf16[8,128,256]{2,1,0:T(8,128)(2,1)S(1)}, u32[]{:S(2)}, u32[]{:S(2)}) %collective-permute-start.6) | collective-permute-done | bytes 524320 | tf_op jit(solution)/shard_map/ppermute | solution.py:698
  44.9 2.9 %collective-permute-done.5.came_ref = bf16[4,256,256]{2,1,0:T(8,128)(2,1)S(1)} collective-permute-done((bf16[4,256,256]{2,1,0:T(8,128)(2,1)S(1)}, bf16[4,256,256]{2,1,0:T(8,128)(2,1)S(1)}, u32[]{:S(2)}, u32[]{:S(2)}) %collective-permute-start.5) | collective-permute-done | bytes 524320 | tf_op jit(solution)/shard_map/ppermute | solution.py:698
  50.3 3.1 %collective-permute-done.14.came_ref = bf16[8,128,256]{2,1,0:T(8,128)(2,1)S(1)} collective-permute-done((bf16[8,128,256]{2,1,0:T(8,128)(2,1)S(1)}, bf16[8,128,256]{2,1,0:T(8,128)(2,1)S(1)}, u32[]{:S(2)}, u32[]{:S(2)}) %collective-permute-start.14) | collective-permute-done | bytes 524320 | tf_op jit(solution)/shard_map/ppermute | solution.py:698
  53.4 2.3 %collective-permute-start.11 = (bf16[2,128,256]{2,1,0:T(8,128)(2,1)S(1)}, bf16[2,128,256]{2,1,0:T(8,128)(2,1)S(1)}, u32[]{:S(2)}, u32[]{:S(2)}) collective-permute-start(bf16[2,128,256]{2,1,0:T(8,128)(2,1)S(1)} %get-tuple-element.310), channel_id=1, source_target_pairs={{0,2},{1,3},{2,0},{3,1},{4,6},{5,7},{6,4},{7,5},{8,10},{9,11},{10,... | collective-permute-start | bytes 393224 | tf_op jit(solution)/shard_map/ppermute | solution.py:698
  56.8 5.6 %collective-permute-start.18 = (bf16[2,128,256]{2,1,0:T(8,128)(2,1)S(1)}, bf16[2,128,256]{2,1,0:T(8,128)(2,1)S(1)}, u32[]{:S(2)}, u32[]{:S(2)}) collective-permute-start(bf16[2,128,256]{2,1,0:T(8,128)(2,1)S(1)} %get-tuple-element.319), channel_id=1, source_target_pairs={{0,8},{1,9},{2,10},{3,11},{4,12},{5,13},{6,14},{7,15},{8,0},{9,1},... | collective-permute-start | bytes 393224 | tf_op jit(solution)/shard_map/ppermute | solution.py:698
  63.9 4.4 %collective-permute-start.15 = (bf16[1,256,256]{2,1,0:T(8,128)(2,1)S(1)}, bf16[1,256,256]{2,1,0:T(8,128)(2,1)S(1)}, u32[]{:S(2)}, u32[]{:S(2)}) collective-permute-start(bf16[1,256,256]{2,1,0:T(8,128)(2,1)S(1)} %get-tuple-element.329), channel_id=1, source_target_pairs={{0,8},{1,17},{2,10},{3,19},{4,12},{5,21},{6,14},{7,23},{8,0},{9,25... | collective-permute-start | bytes 393224 | tf_op jit(solution)/shard_map/ppermute | solution.py:698
  68.5 1.5 %collective-permute-start.22 = (bf16[1,128,256]{2,1,0:T(8,128)(2,1)S(1)}, bf16[1,128,256]{2,1,0:T(8,128)(2,1)S(1)}, u32[]{:S(2)}, u32[]{:S(2)}) collective-permute-start(bf16[1,128,256]{2,1,0:T(8,128)(2,1)S(1)} %get-tuple-element.339), channel_id=1, source_target_pairs={{0,2},{1,17},{2,0},{3,19},{4,6},{5,21},{6,4},{7,23},{8,10},{9,25},... | collective-permute-start | bytes 196616 | tf_op jit(solution)/shard_map/ppermute | solution.py:698
  70.2 1.7 %collective-permute-done.16.came_ref = bf16[4,128,256]{2,1,0:T(8,128)(2,1)S(1)} collective-permute-done((bf16[4,128,256]{2,1,0:T(8,128)(2,1)S(1)}, bf16[4,128,256]{2,1,0:T(8,128)(2,1)S(1)}, u32[]{:S(2)}, u32[]{:S(2)}) %collective-permute-start.16) | collective-permute-done | bytes 262176 | tf_op jit(solution)/shard_map/ppermute | solution.py:698
  76.4 2.1 %collective-permute-done.21.came_ref = bf16[4,144,256]{2,1,0:T(8,128)(2,1)S(1)} collective-permute-done((bf16[4,144,256]{2,1,0:T(8,128)(2,1)S(1)}, bf16[4,144,256]{2,1,0:T(8,128)(2,1)S(1)}, u32[]{:S(2)}, u32[]{:S(2)}) %collective-permute-start.21) | collective-permute-done | bytes 294944 | tf_op jit(solution)/shard_map/ppermute | solution.py:698
  78.6 2.3 %collective-permute-start.23 = (bf16[2,144,256]{2,1,0:T(8,128)(2,1)S(1)}, bf16[2,144,256]{2,1,0:T(8,128)(2,1)S(1)}, u32[]{:S(2)}, u32[]{:S(2)}) collective-permute-start(bf16[2,144,256]{2,1,0:T(8,128)(2,1)S(1)} %get-tuple-element.358), channel_id=1, source_target_pairs={{0,4},{1,5},{2,6},{3,7},{4,0},{5,1},{6,2},{7,3},{8,12},{9,13},{10,... | collective-permute-start | bytes 442376 | tf_op jit(solution)/shard_map/ppermute | solution.py:698
  80.9 1.3 %collective-permute-start.27 = (bf16[1,128,256]{2,1,0:T(8,128)(2,1)S(1)}, bf16[1,128,256]{2,1,0:T(8,128)(2,1)S(1)}, u32[]{:S(2)}, u32[]{:S(2)}) collective-permute-start(bf16[1,128,256]{2,1,0:T(8,128)(2,1)S(1)} %get-tuple-element.363), channel_id=1, source_target_pairs={{0,16},{1,9},{2,18},{3,11},{4,20},{5,13},{6,22},{7,15},{8,24},{9,1... | collective-permute-start | bytes 196616 | tf_op jit(solution)/shard_map/ppermute | solution.py:698
  82.3 1.7 %collective-permute-start.28 = (bf16[1,128,256]{2,1,0:T(8,128)(2,1)S(1)}, bf16[1,128,256]{2,1,0:T(8,128)(2,1)S(1)}, u32[]{:S(2)}, u32[]{:S(2)}) collective-permute-start(bf16[1,128,256]{2,1,0:T(8,128)(2,1)S(1)} %get-tuple-element.366), channel_id=1, source_target_pairs={{0,2},{1,9},{2,0},{3,11},{4,6},{5,13},{6,4},{7,15},{8,10},{9,1},{1... | collective-permute-start | bytes 196616 | tf_op jit(solution)/shard_map/ppermute | solution.py:698
  84.8 1.9 %collective-permute-start.26 = (bf16[1,144,256]{2,1,0:T(8,128)(2,1)S(1)}, bf16[1,144,256]{2,1,0:T(8,128)(2,1)S(1)}, u32[]{:S(2)}, u32[]{:S(2)}) collective-permute-start(bf16[1,144,256]{2,1,0:T(8,128)(2,1)S(1)} %get-tuple-element.369), channel_id=1, source_target_pairs={{0,8},{1,9},{2,10},{3,11},{4,12},{5,13},{6,14},{7,15},{8,0},{9,1},... | collective-permute-start | bytes 221192 | tf_op jit(solution)/shard_map/ppermute | solution.py:698
  (75 shorter events, 22.8 us)
Async XLA Ops:
  1.6 6.8 %collective-permute-start = (bf16[128,512]{1,0:T(8,128)(2,1)S(1)}, bf16[128,512]{1,0:T(8,128)(2,1)S(1)}, u32[]{:S(2)}, u32[]{:S(2)}) collective-permute-start(bf16[128,512]{1,0:T(8,128)(2,1)S(1)} %dynamic-slice_bitcast_fusion), channel_id=1, source_target_pairs={{0,16},{16,0},{1,17},{17,1},{2,18},{18,2},{3,19},{19,3},{4,20},{20... | collective-permute-start | bytes 393224 | tf_op jit(solution)/shard_map/ppermute | solution.py:649
  19.7 15.0 %collective-permute-start.3 = (bf16[8,256,256]{2,1,0:T(8,128)(2,1)S(1)}, bf16[8,256,256]{2,1,0:T(8,128)(2,1)S(1)}, u32[]{:S(2)}, u32[]{:S(2)}) collective-permute-start(bf16[8,256,256]{2,1,0:T(8,128)(2,1)S(1)} %get-tuple-element.237), channel_id=1, source_target_pairs={{0,16},{1,3},{2,18},{3,1},{4,20},{5,7},{6,22},{7,5},{8,24},{9,11},... | collective-permute-start | bytes 3145736 | tf_op jit(solution)/shard_map/ppermute | solution.py:698
  21.7 14.8 %collective-permute-start.8 = (bf16[8,128,256]{2,1,0:T(8,128)(2,1)S(1)}, bf16[8,128,256]{2,1,0:T(8,128)(2,1)S(1)}, u32[]{:S(2)}, u32[]{:S(2)}) collective-permute-start(bf16[8,128,256]{2,1,0:T(8,128)(2,1)S(1)} %get-tuple-element.241), channel_id=1, source_target_pairs={{0,4},{1,5},{2,6},{3,7},{4,0},{5,1},{6,2},{7,3},{8,12},{9,13},{10,... | collective-permute-start | bytes 1572872 | tf_op jit(solution)/shard_map/ppermute | solution.py:698
  32.8 6.5 %collective-permute-start.7 = (bf16[6464,128]{1,0:T(8,128)(2,1)S(1)}, bf16[6464,128]{1,0:T(8,128)(2,1)S(1)}, u32[]{:S(2)}, u32[]{:S(2)}) collective-permute-start(bf16[6464,128]{1,0:T(8,128)(2,1)S(1)} %get-tuple-element.304.refs_1_), channel_id=1, source_target_pairs={{0,1},{1,0},{2,3},{3,2},{4,5},{5,4},{6,7},{7,6},{8,9},{9,8},{10,11... | collective-permute-start | bytes 4964360 | tf_op jit(solution)/shard_map/ppermute | solution.py:649
  33.9 10.8 %collective-permute-start.6 = (bf16[8,128,256]{2,1,0:T(8,128)(2,1)S(1)}, bf16[8,128,256]{2,1,0:T(8,128)(2,1)S(1)}, u32[]{:S(2)}, u32[]{:S(2)}) collective-permute-start(bf16[8,128,256]{2,1,0:T(8,128)(2,1)S(1)} %get-tuple-element.275), channel_id=1, source_target_pairs={{0,16},{1,3},{2,18},{3,1},{4,20},{5,7},{6,22},{7,5},{8,24},{9,11},... | collective-permute-start | bytes 1572872 | tf_op jit(solution)/shard_map/ppermute | solution.py:698
  34.9 13.0 %collective-permute-start.5 = (bf16[4,256,256]{2,1,0:T(8,128)(2,1)S(1)}, bf16[4,256,256]{2,1,0:T(8,128)(2,1)S(1)}, u32[]{:S(2)}, u32[]{:S(2)}) collective-permute-start(bf16[4,256,256]{2,1,0:T(8,128)(2,1)S(1)} %get-tuple-element.279), channel_id=1, source_target_pairs={{0,2},{1,5},{2,0},{3,7},{4,6},{5,1},{6,4},{7,3},{8,10},{9,13},{10,... | collective-permute-start | bytes 1572872 | tf_op jit(solution)/shard_map/ppermute | solution.py:698
  36.6 12.6 %collective-permute-start.10 = (bf16[4,128,256]{2,1,0:T(8,128)(2,1)S(1)}, bf16[4,128,256]{2,1,0:T(8,128)(2,1)S(1)}, u32[]{:S(2)}, u32[]{:S(2)}) collective-permute-start(bf16[4,128,256]{2,1,0:T(8,128)(2,1)S(1)} %get-tuple-element.286), channel_id=1, source_target_pairs={{0,8},{1,9},{2,10},{3,11},{4,12},{5,13},{6,14},{7,15},{8,0},{9,1},... | collective-permute-start | bytes 786440 | tf_op jit(solution)/shard_map/ppermute | solution.py:698
  39.8 13.6 %collective-permute-start.14 = (bf16[8,128,256]{2,1,0:T(8,128)(2,1)S(1)}, bf16[8,128,256]{2,1,0:T(8,128)(2,1)S(1)}, u32[]{:S(2)}, u32[]{:S(2)}) collective-permute-start(bf16[8,128,256]{2,1,0:T(8,128)(2,1)S(1)} %get-tuple-element.290), channel_id=1, source_target_pairs={{0,2},{1,17},{2,0},{3,19},{4,6},{5,21},{6,4},{7,23},{8,10},{9,25},... | collective-permute-start | bytes 1572872 | tf_op jit(solution)/shard_map/ppermute | solution.py:698
  41.0 15.8 %collective-permute-start.12 = (bf16[8,128,256]{2,1,0:T(8,128)(2,1)S(1)}, bf16[8,128,256]{2,1,0:T(8,128)(2,1)S(1)}, u32[]{:S(2)}, u32[]{:S(2)}) collective-permute-start(bf16[8,128,256]{2,1,0:T(8,128)(2,1)S(1)} %get-tuple-element.294), channel_id=1, source_target_pairs={{0,16},{1,17},{2,18},{3,19},{4,20},{5,21},{6,22},{7,23},{8,24},{9,... | collective-permute-start | bytes 1572872 | tf_op jit(solution)/shard_map/ppermute | solution.py:698
  44.9 11.9 %collective-permute-start.13 = (bf16[4,128,256]{2,1,0:T(8,128)(2,1)S(1)}, bf16[4,128,256]{2,1,0:T(8,128)(2,1)S(1)}, u32[]{:S(2)}, u32[]{:S(2)}) collective-permute-start(bf16[4,128,256]{2,1,0:T(8,128)(2,1)S(1)} %get-tuple-element.297), channel_id=1, source_target_pairs={{0,4},{1,5},{2,6},{3,7},{4,0},{5,1},{6,2},{7,3},{8,12},{9,13},{10,... | collective-permute-start | bytes 786440 | tf_op jit(solution)/shard_map/ppermute | solution.py:698
  48.0 14.7 %collective-permute-start.9 = (bf16[2,256,256]{2,1,0:T(8,128)(2,1)S(1)}, bf16[2,256,256]{2,1,0:T(8,128)(2,1)S(1)}, u32[]{:S(2)}, u32[]{:S(2)}) collective-permute-start(bf16[2,256,256]{2,1,0:T(8,128)(2,1)S(1)} %get-tuple-element.301), channel_id=1, source_target_pairs={{0,4},{1,9},{2,6},{3,11},{4,0},{5,13},{6,2},{7,15},{8,12},{9,1},{1... | collective-permute-start | bytes 786440 | tf_op jit(solution)/shard_map/ppermute | solution.py:698
  49.1 19.4 %collective-permute-start.17 = (bf16[8,144,256]{2,1,0:T(8,128)(2,1)S(1)}, bf16[8,144,256]{2,1,0:T(8,128)(2,1)S(1)}, u32[]{:S(2)}, u32[]{:S(2)}) collective-permute-start(bf16[8,144,256]{2,1,0:T(8,128)(2,1)S(1)} %get-tuple-element.306), channel_id=1, source_target_pairs={{0,16},{1,3},{2,18},{3,1},{4,20},{5,7},{6,22},{7,5},{8,24},{9,11},... | collective-permute-start | bytes 1769480 | tf_op jit(solution)/shard_map/ppermute | solution.py:698
  53.4 9.1 %collective-permute-start.11 = (bf16[2,128,256]{2,1,0:T(8,128)(2,1)S(1)}, bf16[2,128,256]{2,1,0:T(8,128)(2,1)S(1)}, u32[]{:S(2)}, u32[]{:S(2)}) collective-permute-start(bf16[2,128,256]{2,1,0:T(8,128)(2,1)S(1)} %get-tuple-element.310), channel_id=1, source_target_pairs={{0,2},{1,3},{2,0},{3,1},{4,6},{5,7},{6,4},{7,5},{8,10},{9,11},{10,... | collective-permute-start | bytes 393224 | tf_op jit(solution)/shard_map/ppermute | solution.py:698
  56.7 7.2 %collective-permute-start.19 = (bf16[4,128,256]{2,1,0:T(8,128)(2,1)S(1)}, bf16[4,128,256]{2,1,0:T(8,128)(2,1)S(1)}, u32[]{:S(2)}, u32[]{:S(2)}) collective-permute-start(bf16[4,128,256]{2,1,0:T(8,128)(2,1)S(1)} %get-tuple-element.316), channel_id=1, source_target_pairs={{0,4},{1,3},{2,6},{3,1},{4,0},{5,7},{6,2},{7,5},{8,12},{9,11},{10,... | collective-permute-start | bytes 786440 | tf_op jit(solution)/shard_map/ppermute | solution.py:698
  56.8 11.6 %collective-permute-start.18 = (bf16[2,128,256]{2,1,0:T(8,128)(2,1)S(1)}, bf16[2,128,256]{2,1,0:T(8,128)(2,1)S(1)}, u32[]{:S(2)}, u32[]{:S(2)}) collective-permute-start(bf16[2,128,256]{2,1,0:T(8,128)(2,1)S(1)} %get-tuple-element.319), channel_id=1, source_target_pairs={{0,8},{1,9},{2,10},{3,11},{4,12},{5,13},{6,14},{7,15},{8,0},{9,1},... | collective-permute-start | bytes 393224 | tf_op jit(solution)/shard_map/ppermute | solution.py:698
  62.6 9.2 %collective-permute-start.16 = (bf16[4,128,256]{2,1,0:T(8,128)(2,1)S(1)}, bf16[4,128,256]{2,1,0:T(8,128)(2,1)S(1)}, u32[]{:S(2)}, u32[]{:S(2)}) collective-permute-start(bf16[4,128,256]{2,1,0:T(8,128)(2,1)S(1)} %get-tuple-element.322), channel_id=1, source_target_pairs={{0,4},{1,3},{2,6},{3,1},{4,0},{5,7},{6,2},{7,5},{8,12},{9,11},{10,... | collective-permute-start | bytes 786440 | tf_op jit(solution)/shard_map/ppermute | solution.py:698
  62.7 24.8 %collective-permute-start.29 = (bf16[1,128,256]{2,1,0:T(8,128)(2,1)S(1)}, bf16[1,128,256]{2,1,0:T(8,128)(2,1)S(1)}, u32[]{:S(2)}, u32[]{:S(2)}) collective-permute-start(bf16[1,128,256]{2,1,0:T(8,128)(2,1)S(1)} %get-tuple-element.325), channel_id=1, source_target_pairs={{0,16},{1,17},{2,18},{3,19},{4,20},{5,21},{6,22},{7,23},{8,24},{9,... | collective-permute-start | bytes 196616 | tf_op jit(solution)/shard_map/ppermute | solution.py:698
  63.9 9.0 %collective-permute-start.15 = (bf16[1,256,256]{2,1,0:T(8,128)(2,1)S(1)}, bf16[1,256,256]{2,1,0:T(8,128)(2,1)S(1)}, u32[]{:S(2)}, u32[]{:S(2)}) collective-permute-start(bf16[1,256,256]{2,1,0:T(8,128)(2,1)S(1)} %get-tuple-element.329), channel_id=1, source_target_pairs={{0,8},{1,17},{2,10},{3,19},{4,12},{5,21},{6,14},{7,23},{8,0},{9,25... | collective-permute-start | bytes 393224 | tf_op jit(solution)/shard_map/ppermute | solution.py:698
  68.4 12.5 %collective-permute-start.25 = (bf16[2,128,256]{2,1,0:T(8,128)(2,1)S(1)}, bf16[2,128,256]{2,1,0:T(8,128)(2,1)S(1)}, u32[]{:S(2)}, u32[]{:S(2)}) collective-permute-start(bf16[2,128,256]{2,1,0:T(8,128)(2,1)S(1)} %get-tuple-element.336), channel_id=1, source_target_pairs={{0,8},{1,5},{2,10},{3,7},{4,12},{5,1},{6,14},{7,3},{8,0},{9,13},{1... | collective-permute-start | bytes 393224 | tf_op jit(solution)/shard_map/ppermute | solution.py:698
  68.5 6.4 %collective-permute-start.22 = (bf16[1,128,256]{2,1,0:T(8,128)(2,1)S(1)}, bf16[1,128,256]{2,1,0:T(8,128)(2,1)S(1)}, u32[]{:S(2)}, u32[]{:S(2)}) collective-permute-start(bf16[1,128,256]{2,1,0:T(8,128)(2,1)S(1)} %get-tuple-element.339), channel_id=1, source_target_pairs={{0,2},{1,17},{2,0},{3,19},{4,6},{5,21},{6,4},{7,23},{8,10},{9,25},... | collective-permute-start | bytes 196616 | tf_op jit(solution)/shard_map/ppermute | solution.py:698
  71.8 6.7 %collective-permute-start.21 = (bf16[4,144,256]{2,1,0:T(8,128)(2,1)S(1)}, bf16[4,144,256]{2,1,0:T(8,128)(2,1)S(1)}, u32[]{:S(2)}, u32[]{:S(2)}) collective-permute-start(bf16[4,144,256]{2,1,0:T(8,128)(2,1)S(1)} %get-tuple-element.342), channel_id=1, source_target_pairs={{0,2},{1,17},{2,0},{3,19},{4,6},{5,21},{6,4},{7,23},{8,10},{9,25},... | collective-permute-start | bytes 884744 | tf_op jit(solution)/shard_map/ppermute | solution.py:698
  72.9 9.3 %collective-permute-start.24 = (bf16[2,128,256]{2,1,0:T(8,128)(2,1)S(1)}, bf16[2,128,256]{2,1,0:T(8,128)(2,1)S(1)}, u32[]{:S(2)}, u32[]{:S(2)}) collective-permute-start(bf16[2,128,256]{2,1,0:T(8,128)(2,1)S(1)} %get-tuple-element.345), channel_id=1, source_target_pairs={{0,8},{1,5},{2,10},{3,7},{4,12},{5,1},{6,14},{7,3},{8,0},{9,13},{1... | collective-permute-start | bytes 393224 | tf_op jit(solution)/shard_map/ppermute | solution.py:698
  74.9 11.8 %collective-permute-start.20 = (bf16[2,128,512]{2,1,0:T(8,128)(2,1)S(1)}, bf16[2,128,512]{2,1,0:T(8,128)(2,1)S(1)}, u32[]{:S(2)}, u32[]{:S(2)}) collective-permute-start(bf16[2,128,512]{2,1,0:T(8,128)(2,1)S(1)} %get-tuple-element.349), channel_id=1, source_target_pairs={{0,16},{16,0},{1,17},{17,1},{2,18},{18,2},{3,19},{19,3},{4,20},{20... | collective-permute-start | bytes 786440 | tf_op jit(solution)/shard_map/ppermute | solution.py:649
  80.9 8.0 %collective-permute-start.27 = (bf16[1,128,256]{2,1,0:T(8,128)(2,1)S(1)}, bf16[1,128,256]{2,1,0:T(8,128)(2,1)S(1)}, u32[]{:S(2)}, u32[]{:S(2)}) collective-permute-start(bf16[1,128,256]{2,1,0:T(8,128)(2,1)S(1)} %get-tuple-element.363), channel_id=1, source_target_pairs={{0,16},{1,9},{2,18},{3,11},{4,20},{5,13},{6,22},{7,15},{8,24},{9,1... | collective-permute-start | bytes 196616 | tf_op jit(solution)/shard_map/ppermute | solution.py:698
  (6 other events, 29.5 us)

commit v6 on v5

--- a/solution.py
+++ b/solution.py
@@ -673,9 +673,10 @@
 
 class Team:
     def __init__(self, line, orders, small=False, **weights):
-        self.line, self.orders, self.small = line, orders, small
+        self.line, self.small = line, small
         self.shapes = {name: array.shape for name, array in weights.items()}
         self.even = lax.axis_size("rows") == GROUPS
+        self.orders = orders if self.even else (XYZ, XYZ)
         self.turn = 0
         self.done = {}
 

time: 91.1 us -> 91.1 us (level)
  no operation moved by 1% of the time
where the time goes in v6:
time: 91.1 us; the launch traced here: 90.9 us
  starting transfers between devices  41.3 us (45%)
  Pallas kernels  32.1 us (35%)
  waiting for transfers between devices  14.2 us (16%)
  other arithmetic  1.49 us (2%)
  between operations  0.93 us (1%)
  local copies, waits for them, and re-layouts  0.92 us (1%)
    ppermute x24, starting transfers between devices, go(): self.came = lax.ppermute(self.sent, ('section', 'rows'), route)  36.3 us
    pallas_call x5, Pallas kernels, call(): pl.pallas_call(kernel, out_shape=shapes_out, in_specs=[HBM] * len(arrays)...  22.4 us
    ppermute x24, waiting for transfers between devices, go(): self.came = lax.ppermute(self.sent, ('section', 'rows'), route)  13.9 us
    ppermute x6, starting transfers between devices, pair_swap(): return lax.ppermute(value, axis, [(i, i ^ apart) for i in range(count)])  5.05 us
    pallas_call x6, Pallas kernels, weight_grads(): pl.pallas_call(kernel, out_shape=[half, half], in_specs=[VMEM] * len(arra...  4.11 us
    pallas_call x6, Pallas kernels, end(): pl.pallas_call(kernel, out_shape=outs, in_specs=[VMEM] * 2, out_specs=[VM...  4.04 us
  transfers between devices with their start and end apart: 30, of which 8 were waited for; matrix products, arithmetic and copies ran while one was open for 2% of the time, Pallas kernels for 26%

profile of v6, /device:TPU:0, one launch (start us, length us, event | category | flops | bytes accessed | tf_op | source)
XLA Modules:
  0.0 90.9 jit_solution(6848959264713999640)
XLA Ops:
  1.6 3.0 %collective-permute-start = (bf16[128,512]{1,0:T(8,128)(2,1)S(1)}, bf16[128,512]{1,0:T(8,128)(2,1)S(1)}, u32[]{:S(2)}, u32[]{:S(2)}) collective-permute-start(bf16[128,512]{1,0:T(8,128)(2,1)S(1)} %dynamic-slice_bitcast_fusion), channel_id=1, source_target_pairs={{0,16},{16,0},{1,17},{17,1},{2,18},{18,2},{3,19},{19,3},{4,20},{20... | collective-permute-start | bytes 393224 | tf_op jit(solution)/shard_map/ppermute | solution.py:649
  4.6 3.8 %shard_map.305 = (bf16[512,1536]{1,0:T(8,128)(2,1)S(1)}, bf16[512,512]{1,0:T(8,128)(2,1)S(1)}, f32[128,512]{1,0:T(8,128)}, bf16[128,1536]{1,0:T(8,128)(2,1)}, f3...) custom-call(s32[2,2,1,128]{3,2,1,0:T(1,128)} %refs_0_.3, ...), custom_call_target="tpu_custom_call" | custom-call | flops 22000001024 | bytes 1 | tf_op jit(solution)/shard_map/pallas_call | solution.py:292
  8.4 7.5 %shard_map.306 = (bf16[128,512]{1,0:T(8,128)(2,1)S(1)}, bf16[128,512]{1,0:T(8,128)(2,1)S(1)}, bf16[128,1536]{1,0:T(8,128)(2,1)S(1)}, f32[8,128,128]{2,1,0:T(8,12...) custom-call(s32[2,2,1,128]{3,2,1,0:T(1,128)} %refs_0_.3, ...), custom_call_target="tpu_custom_call" | custom-call | flops 60500000768 | bytes 1 | tf_op jit(solution)/shard_map/pallas_call | solution.py:292
  16.0 1.7 %shard_map.307 = (f32[128,512]{1,0:T(8,128)S(1)}, bf16[128,512]{1,0:T(8,128)(2,1)S(1)}, bf16[128,1024]{1,0:T(8,128)(2,1)S(1)}, f32[2,512]{1,0:T(2,128)S(1)}, bf1...) custom-call(f32[128,512]{1,0:T(8,128)S(1)} %get-tuple-element.217.refs_0_, ...), custom_call_target="tpu_custom_call" | custom-call | flops 25849999360 | bytes 1 | tf_op jit(solution)/shard_map/pallas_call | solution.py:292
  19.7 1.4 %collective-permute-start.3 = (bf16[8,256,256]{2,1,0:T(8,128)(2,1)S(1)}, bf16[8,256,256]{2,1,0:T(8,128)(2,1)S(1)}, u32[]{:S(2)}, u32[]{:S(2)}) collective-permute-start(bf16[8,256,256]{2,1,0:T(8,128)(2,1)S(1)} %get-tuple-element.237), channel_id=1, source_target_pairs={{0,16},{1,3},{2,18},{3,1},{4,20},{5,7},{6,22},{7,5},{8,24},{9,11},... | collective-permute-start | bytes 3145736 | tf_op jit(solution)/shard_map/ppermute | solution.py:699
  21.7 1.6 %collective-permute-start.8 = (bf16[8,128,256]{2,1,0:T(8,128)(2,1)S(1)}, bf16[8,128,256]{2,1,0:T(8,128)(2,1)S(1)}, u32[]{:S(2)}, u32[]{:S(2)}) collective-permute-start(bf16[8,128,256]{2,1,0:T(8,128)(2,1)S(1)} %get-tuple-element.241), channel_id=1, source_target_pairs={{0,4},{1,5},{2,6},{3,7},{4,0},{5,1},{6,2},{7,3},{8,12},{9,13},{10,... | collective-permute-start | bytes 1572872 | tf_op jit(solution)/shard_map/ppermute | solution.py:699
  23.3 4.1 %shard_map.310 = (bf16[128,512]{1,0:T(8,128)(2,1)S(1)}, bf16[128,512]{1,0:T(8,128)(2,1)S(1)}, f32[2,512]{1,0:T(2,128)S(1)}, bf16[512,128]{1,0:T(8,128)(2,1)S(1)}, bf16[2560,128]{1,0:T(8,128)(2,1)S(1)}) custom-call(f32[128,512]{1,0:T(8,128)} %get-tuple-element.206.refs_0_, f32[128,128]{1,0:T(8,128)} %get-tuple-element.207.refs_1_, bf16[512,512]{1,0:T(8,128)(2,1)} %refs_2_.5, ...), custom_call_target="tpu_custom_call" | custom-call | flops 27499999232 | bytes 1 | tf_op jit(solution)/shard_map/pallas_call | solution.py:292
  27.5 5.3 %shard_map.311 = (bf16[2,128,512]{2,1,0:T(8,128)(2,1)S(1)}, bf16[2,128,512]{2,1,0:T(8,128)(2,1)S(1)}, bf16[1792,128]{1,0:T(8,128)(2,1)S(1)}, bf16[6464,128]{1,0:T(8,128)(2,1)S(1)}) custom-call(f32[128,512]{1,0:T(8,128)} %get-tuple-element.206.refs_0_, f32[128,128]{1,0:T(8,128)} %get-tuple-element.207.refs_1_, ...), custom_call_target="tpu_custom_call" | custom-call | flops 44000002048 | bytes 1 | tf_op jit(solution)/shard_map/pallas_call | solution.py:292
  34.9 1.6 %collective-permute-start.5 = (bf16[4,256,256]{2,1,0:T(8,128)(2,1)S(1)}, bf16[4,256,256]{2,1,0:T(8,128)(2,1)S(1)}, u32[]{:S(2)}, u32[]{:S(2)}) collective-permute-start(bf16[4,256,256]{2,1,0:T(8,128)(2,1)S(1)} %get-tuple-element.279), channel_id=1, source_target_pairs={{0,2},{1,5},{2,0},{3,7},{4,6},{5,1},{6,4},{7,3},{8,10},{9,13},{10,... | collective-permute-start | bytes 1572872 | tf_op jit(solution)/shard_map/ppermute | solution.py:699
  36.6 2.6 %collective-permute-start.10 = (bf16[4,128,256]{2,1,0:T(8,128)(2,1)S(1)}, bf16[4,128,256]{2,1,0:T(8,128)(2,1)S(1)}, u32[]{:S(2)}, u32[]{:S(2)}) collective-permute-start(bf16[4,128,256]{2,1,0:T(8,128)(2,1)S(1)} %get-tuple-element.286), channel_id=1, source_target_pairs={{0,8},{1,9},{2,10},{3,11},{4,12},{5,13},{6,14},{7,15},{8,0},{9,1},... | collective-permute-start | bytes 786440 | tf_op jit(solution)/shard_map/ppermute | solution.py:699
  41.0 1.4 %collective-permute-start.12 = (bf16[8,128,256]{2,1,0:T(8,128)(2,1)S(1)}, bf16[8,128,256]{2,1,0:T(8,128)(2,1)S(1)}, u32[]{:S(2)}, u32[]{:S(2)}) collective-permute-start(bf16[8,128,256]{2,1,0:T(8,128)(2,1)S(1)} %get-tuple-element.294), channel_id=1, source_target_pairs={{0,16},{1,17},{2,18},{3,19},{4,20},{5,21},{6,22},{7,23},{8,24},{9,... | collective-permute-start | bytes 1572872 | tf_op jit(solution)/shard_map/ppermute | solution.py:699
  42.4 2.4 %collective-permute-done.6.came_ref = bf16[8,128,256]{2,1,0:T(8,128)(2,1)S(1)} collective-permute-done((bf16[8,128,256]{2,1,0:T(8,128)(2,1)S(1)}, bf16[8,128,256]{2,1,0:T(8,128)(2,1)S(1)}, u32[]{:S(2)}, u32[]{:S(2)}) %collective-permute-start.6) | collective-permute-done | bytes 524320 | tf_op jit(solution)/shard_map/ppermute | solution.py:699
  44.9 2.9 %collective-permute-done.5.came_ref = bf16[4,256,256]{2,1,0:T(8,128)(2,1)S(1)} collective-permute-done((bf16[4,256,256]{2,1,0:T(8,128)(2,1)S(1)}, bf16[4,256,256]{2,1,0:T(8,128)(2,1)S(1)}, u32[]{:S(2)}, u32[]{:S(2)}) %collective-permute-start.5) | collective-permute-done | bytes 524320 | tf_op jit(solution)/shard_map/ppermute | solution.py:699
  50.3 3.1 %collective-permute-done.14.came_ref = bf16[8,128,256]{2,1,0:T(8,128)(2,1)S(1)} collective-permute-done((bf16[8,128,256]{2,1,0:T(8,128)(2,1)S(1)}, bf16[8,128,256]{2,1,0:T(8,128)(2,1)S(1)}, u32[]{:S(2)}, u32[]{:S(2)}) %collective-permute-start.14) | collective-permute-done | bytes 524320 | tf_op jit(solution)/shard_map/ppermute | solution.py:699
  53.4 2.3 %collective-permute-start.11 = (bf16[2,128,256]{2,1,0:T(8,128)(2,1)S(1)}, bf16[2,128,256]{2,1,0:T(8,128)(2,1)S(1)}, u32[]{:S(2)}, u32[]{:S(2)}) collective-permute-start(bf16[2,128,256]{2,1,0:T(8,128)(2,1)S(1)} %get-tuple-element.310), channel_id=1, source_target_pairs={{0,2},{1,3},{2,0},{3,1},{4,6},{5,7},{6,4},{7,5},{8,10},{9,11},{10,... | collective-permute-start | bytes 393224 | tf_op jit(solution)/shard_map/ppermute | solution.py:699
  56.8 5.6 %collective-permute-start.18 = (bf16[2,128,256]{2,1,0:T(8,128)(2,1)S(1)}, bf16[2,128,256]{2,1,0:T(8,128)(2,1)S(1)}, u32[]{:S(2)}, u32[]{:S(2)}) collective-permute-start(bf16[2,128,256]{2,1,0:T(8,128)(2,1)S(1)} %get-tuple-element.319), channel_id=1, source_target_pairs={{0,8},{1,9},{2,10},{3,11},{4,12},{5,13},{6,14},{7,15},{8,0},{9,1},... | collective-permute-start | bytes 393224 | tf_op jit(solution)/shard_map/ppermute | solution.py:699
  63.9 4.4 %collective-permute-start.15 = (bf16[1,256,256]{2,1,0:T(8,128)(2,1)S(1)}, bf16[1,256,256]{2,1,0:T(8,128)(2,1)S(1)}, u32[]{:S(2)}, u32[]{:S(2)}) collective-permute-start(bf16[1,256,256]{2,1,0:T(8,128)(2,1)S(1)} %get-tuple-element.329), channel_id=1, source_target_pairs={{0,8},{1,17},{2,10},{3,19},{4,12},{5,21},{6,14},{7,23},{8,0},{9,25... | collective-permute-start | bytes 393224 | tf_op jit(solution)/shard_map/ppermute | solution.py:699
  68.5 1.5 %collective-permute-start.22 = (bf16[1,128,256]{2,1,0:T(8,128)(2,1)S(1)}, bf16[1,128,256]{2,1,0:T(8,128)(2,1)S(1)}, u32[]{:S(2)}, u32[]{:S(2)}) collective-permute-start(bf16[1,128,256]{2,1,0:T(8,128)(2,1)S(1)} %get-tuple-element.339), channel_id=1, source_target_pairs={{0,2},{1,17},{2,0},{3,19},{4,6},{5,21},{6,4},{7,23},{8,10},{9,25},... | collective-permute-start | bytes 196616 | tf_op jit(solution)/shard_map/ppermute | solution.py:699
  70.2 1.7 %collective-permute-done.16.came_ref = bf16[4,128,256]{2,1,0:T(8,128)(2,1)S(1)} collective-permute-done((bf16[4,128,256]{2,1,0:T(8,128)(2,1)S(1)}, bf16[4,128,256]{2,1,0:T(8,128)(2,1)S(1)}, u32[]{:S(2)}, u32[]{:S(2)}) %collective-permute-start.16) | collective-permute-done | bytes 262176 | tf_op jit(solution)/shard_map/ppermute | solution.py:699
  76.4 2.1 %collective-permute-done.21.came_ref = bf16[4,144,256]{2,1,0:T(8,128)(2,1)S(1)} collective-permute-done((bf16[4,144,256]{2,1,0:T(8,128)(2,1)S(1)}, bf16[4,144,256]{2,1,0:T(8,128)(2,1)S(1)}, u32[]{:S(2)}, u32[]{:S(2)}) %collective-permute-start.21) | collective-permute-done | bytes 294944 | tf_op jit(solution)/shard_map/ppermute | solution.py:699
  78.6 2.3 %collective-permute-start.23 = (bf16[2,144,256]{2,1,0:T(8,128)(2,1)S(1)}, bf16[2,144,256]{2,1,0:T(8,128)(2,1)S(1)}, u32[]{:S(2)}, u32[]{:S(2)}) collective-permute-start(bf16[2,144,256]{2,1,0:T(8,128)(2,1)S(1)} %get-tuple-element.358), channel_id=1, source_target_pairs={{0,4},{1,5},{2,6},{3,7},{4,0},{5,1},{6,2},{7,3},{8,12},{9,13},{10,... | collective-permute-start | bytes 442376 | tf_op jit(solution)/shard_map/ppermute | solution.py:699
  80.9 1.3 %collective-permute-start.27 = (bf16[1,128,256]{2,1,0:T(8,128)(2,1)S(1)}, bf16[1,128,256]{2,1,0:T(8,128)(2,1)S(1)}, u32[]{:S(2)}, u32[]{:S(2)}) collective-permute-start(bf16[1,128,256]{2,1,0:T(8,128)(2,1)S(1)} %get-tuple-element.363), channel_id=1, source_target_pairs={{0,16},{1,9},{2,18},{3,11},{4,20},{5,13},{6,22},{7,15},{8,24},{9,1... | collective-permute-start | bytes 196616 | tf_op jit(solution)/shard_map/ppermute | solution.py:699
  82.3 1.7 %collective-permute-start.28 = (bf16[1,128,256]{2,1,0:T(8,128)(2,1)S(1)}, bf16[1,128,256]{2,1,0:T(8,128)(2,1)S(1)}, u32[]{:S(2)}, u32[]{:S(2)}) collective-permute-start(bf16[1,128,256]{2,1,0:T(8,128)(2,1)S(1)} %get-tuple-element.366), channel_id=1, source_target_pairs={{0,2},{1,9},{2,0},{3,11},{4,6},{5,13},{6,4},{7,15},{8,10},{9,1},{1... | collective-permute-start | bytes 196616 | tf_op jit(solution)/shard_map/ppermute | solution.py:699
  84.8 1.9 %collective-permute-start.26 = (bf16[1,144,256]{2,1,0:T(8,128)(2,1)S(1)}, bf16[1,144,256]{2,1,0:T(8,128)(2,1)S(1)}, u32[]{:S(2)}, u32[]{:S(2)}) collective-permute-start(bf16[1,144,256]{2,1,0:T(8,128)(2,1)S(1)} %get-tuple-element.369), channel_id=1, source_target_pairs={{0,8},{1,9},{2,10},{3,11},{4,12},{5,13},{6,14},{7,15},{8,0},{9,1},... | collective-permute-start | bytes 221192 | tf_op jit(solution)/shard_map/ppermute | solution.py:699
  (75 shorter events, 22.8 us)
Async XLA Ops:
  1.6 6.8 %collective-permute-start = (bf16[128,512]{1,0:T(8,128)(2,1)S(1)}, bf16[128,512]{1,0:T(8,128)(2,1)S(1)}, u32[]{:S(2)}, u32[]{:S(2)}) collective-permute-start(bf16[128,512]{1,0:T(8,128)(2,1)S(1)} %dynamic-slice_bitcast_fusion), channel_id=1, source_target_pairs={{0,16},{16,0},{1,17},{17,1},{2,18},{18,2},{3,19},{19,3},{4,20},{20... | collective-permute-start | bytes 393224 | tf_op jit(solution)/shard_map/ppermute | solution.py:649
  19.7 15.0 %collective-permute-start.3 = (bf16[8,256,256]{2,1,0:T(8,128)(2,1)S(1)}, bf16[8,256,256]{2,1,0:T(8,128)(2,1)S(1)}, u32[]{:S(2)}, u32[]{:S(2)}) collective-permute-start(bf16[8,256,256]{2,1,0:T(8,128)(2,1)S(1)} %get-tuple-element.237), channel_id=1, source_target_pairs={{0,16},{1,3},{2,18},{3,1},{4,20},{5,7},{6,22},{7,5},{8,24},{9,11},... | collective-permute-start | bytes 3145736 | tf_op jit(solution)/shard_map/ppermute | solution.py:699
  21.7 14.8 %collective-permute-start.8 = (bf16[8,128,256]{2,1,0:T(8,128)(2,1)S(1)}, bf16[8,128,256]{2,1,0:T(8,128)(2,1)S(1)}, u32[]{:S(2)}, u32[]{:S(2)}) collective-permute-start(bf16[8,128,256]{2,1,0:T(8,128)(2,1)S(1)} %get-tuple-element.241), channel_id=1, source_target_pairs={{0,4},{1,5},{2,6},{3,7},{4,0},{5,1},{6,2},{7,3},{8,12},{9,13},{10,... | collective-permute-start | bytes 1572872 | tf_op jit(solution)/shard_map/ppermute | solution.py:699
  32.8 6.5 %collective-permute-start.7 = (bf16[6464,128]{1,0:T(8,128)(2,1)S(1)}, bf16[6464,128]{1,0:T(8,128)(2,1)S(1)}, u32[]{:S(2)}, u32[]{:S(2)}) collective-permute-start(bf16[6464,128]{1,0:T(8,128)(2,1)S(1)} %get-tuple-element.304.refs_1_), channel_id=1, source_target_pairs={{0,1},{1,0},{2,3},{3,2},{4,5},{5,4},{6,7},{7,6},{8,9},{9,8},{10,11... | collective-permute-start | bytes 4964360 | tf_op jit(solution)/shard_map/ppermute | solution.py:649
  33.9 10.8 %collective-permute-start.6 = (bf16[8,128,256]{2,1,0:T(8,128)(2,1)S(1)}, bf16[8,128,256]{2,1,0:T(8,128)(2,1)S(1)}, u32[]{:S(2)}, u32[]{:S(2)}) collective-permute-start(bf16[8,128,256]{2,1,0:T(8,128)(2,1)S(1)} %get-tuple-element.275), channel_id=1, source_target_pairs={{0,16},{1,3},{2,18},{3,1},{4,20},{5,7},{6,22},{7,5},{8,24},{9,11},... | collective-permute-start | bytes 1572872 | tf_op jit(solution)/shard_map/ppermute | solution.py:699
  34.9 13.0 %collective-permute-start.5 = (bf16[4,256,256]{2,1,0:T(8,128)(2,1)S(1)}, bf16[4,256,256]{2,1,0:T(8,128)(2,1)S(1)}, u32[]{:S(2)}, u32[]{:S(2)}) collective-permute-start(bf16[4,256,256]{2,1,0:T(8,128)(2,1)S(1)} %get-tuple-element.279), channel_id=1, source_target_pairs={{0,2},{1,5},{2,0},{3,7},{4,6},{5,1},{6,4},{7,3},{8,10},{9,13},{10,... | collective-permute-start | bytes 1572872 | tf_op jit(solution)/shard_map/ppermute | solution.py:699
  36.6 12.6 %collective-permute-start.10 = (bf16[4,128,256]{2,1,0:T(8,128)(2,1)S(1)}, bf16[4,128,256]{2,1,0:T(8,128)(2,1)S(1)}, u32[]{:S(2)}, u32[]{:S(2)}) collective-permute-start(bf16[4,128,256]{2,1,0:T(8,128)(2,1)S(1)} %get-tuple-element.286), channel_id=1, source_target_pairs={{0,8},{1,9},{2,10},{3,11},{4,12},{5,13},{6,14},{7,15},{8,0},{9,1},... | collective-permute-start | bytes 786440 | tf_op jit(solution)/shard_map/ppermute | solution.py:699
  39.8 13.6 %collective-permute-start.14 = (bf16[8,128,256]{2,1,0:T(8,128)(2,1)S(1)}, bf16[8,128,256]{2,1,0:T(8,128)(2,1)S(1)}, u32[]{:S(2)}, u32[]{:S(2)}) collective-permute-start(bf16[8,128,256]{2,1,0:T(8,128)(2,1)S(1)} %get-tuple-element.290), channel_id=1, source_target_pairs={{0,2},{1,17},{2,0},{3,19},{4,6},{5,21},{6,4},{7,23},{8,10},{9,25},... | collective-permute-start | bytes 1572872 | tf_op jit(solution)/shard_map/ppermute | solution.py:699
  41.0 15.8 %collective-permute-start.12 = (bf16[8,128,256]{2,1,0:T(8,128)(2,1)S(1)}, bf16[8,128,256]{2,1,0:T(8,128)(2,1)S(1)}, u32[]{:S(2)}, u32[]{:S(2)}) collective-permute-start(bf16[8,128,256]{2,1,0:T(8,128)(2,1)S(1)} %get-tuple-element.294), channel_id=1, source_target_pairs={{0,16},{1,17},{2,18},{3,19},{4,20},{5,21},{6,22},{7,23},{8,24},{9,... | collective-permute-start | bytes 1572872 | tf_op jit(solution)/shard_map/ppermute | solution.py:699
  44.9 11.9 %collective-permute-start.13 = (bf16[4,128,256]{2,1,0:T(8,128)(2,1)S(1)}, bf16[4,128,256]{2,1,0:T(8,128)(2,1)S(1)}, u32[]{:S(2)}, u32[]{:S(2)}) collective-permute-start(bf16[4,128,256]{2,1,0:T(8,128)(2,1)S(1)} %get-tuple-element.297), channel_id=1, source_target_pairs={{0,4},{1,5},{2,6},{3,7},{4,0},{5,1},{6,2},{7,3},{8,12},{9,13},{10,... | collective-permute-start | bytes 786440 | tf_op jit(solution)/shard_map/ppermute | solution.py:699
  48.0 14.7 %collective-permute-start.9 = (bf16[2,256,256]{2,1,0:T(8,128)(2,1)S(1)}, bf16[2,256,256]{2,1,0:T(8,128)(2,1)S(1)}, u32[]{:S(2)}, u32[]{:S(2)}) collective-permute-start(bf16[2,256,256]{2,1,0:T(8,128)(2,1)S(1)} %get-tuple-element.301), channel_id=1, source_target_pairs={{0,4},{1,9},{2,6},{3,11},{4,0},{5,13},{6,2},{7,15},{8,12},{9,1},{1... | collective-permute-start | bytes 786440 | tf_op jit(solution)/shard_map/ppermute | solution.py:699
  49.1 19.4 %collective-permute-start.17 = (bf16[8,144,256]{2,1,0:T(8,128)(2,1)S(1)}, bf16[8,144,256]{2,1,0:T(8,128)(2,1)S(1)}, u32[]{:S(2)}, u32[]{:S(2)}) collective-permute-start(bf16[8,144,256]{2,1,0:T(8,128)(2,1)S(1)} %get-tuple-element.306), channel_id=1, source_target_pairs={{0,16},{1,3},{2,18},{3,1},{4,20},{5,7},{6,22},{7,5},{8,24},{9,11},... | collective-permute-start | bytes 1769480 | tf_op jit(solution)/shard_map/ppermute | solution.py:699
  53.4 9.1 %collective-permute-start.11 = (bf16[2,128,256]{2,1,0:T(8,128)(2,1)S(1)}, bf16[2,128,256]{2,1,0:T(8,128)(2,1)S(1)}, u32[]{:S(2)}, u32[]{:S(2)}) collective-permute-start(bf16[2,128,256]{2,1,0:T(8,128)(2,1)S(1)} %get-tuple-element.310), channel_id=1, source_target_pairs={{0,2},{1,3},{2,0},{3,1},{4,6},{5,7},{6,4},{7,5},{8,10},{9,11},{10,... | collective-permute-start | bytes 393224 | tf_op jit(solution)/shard_map/ppermute | solution.py:699
  56.7 7.2 %collective-permute-start.19 = (bf16[4,128,256]{2,1,0:T(8,128)(2,1)S(1)}, bf16[4,128,256]{2,1,0:T(8,128)(2,1)S(1)}, u32[]{:S(2)}, u32[]{:S(2)}) collective-permute-start(bf16[4,128,256]{2,1,0:T(8,128)(2,1)S(1)} %get-tuple-element.316), channel_id=1, source_target_pairs={{0,4},{1,3},{2,6},{3,1},{4,0},{5,7},{6,2},{7,5},{8,12},{9,11},{10,... | collective-permute-start | bytes 786440 | tf_op jit(solution)/shard_map/ppermute | solution.py:699
  56.8 11.6 %collective-permute-start.18 = (bf16[2,128,256]{2,1,0:T(8,128)(2,1)S(1)}, bf16[2,128,256]{2,1,0:T(8,128)(2,1)S(1)}, u32[]{:S(2)}, u32[]{:S(2)}) collective-permute-start(bf16[2,128,256]{2,1,0:T(8,128)(2,1)S(1)} %get-tuple-element.319), channel_id=1, source_target_pairs={{0,8},{1,9},{2,10},{3,11},{4,12},{5,13},{6,14},{7,15},{8,0},{9,1},... | collective-permute-start | bytes 393224 | tf_op jit(solution)/shard_map/ppermute | solution.py:699
  62.6 9.2 %collective-permute-start.16 = (bf16[4,128,256]{2,1,0:T(8,128)(2,1)S(1)}, bf16[4,128,256]{2,1,0:T(8,128)(2,1)S(1)}, u32[]{:S(2)}, u32[]{:S(2)}) collective-permute-start(bf16[4,128,256]{2,1,0:T(8,128)(2,1)S(1)} %get-tuple-element.322), channel_id=1, source_target_pairs={{0,4},{1,3},{2,6},{3,1},{4,0},{5,7},{6,2},{7,5},{8,12},{9,11},{10,... | collective-permute-start | bytes 786440 | tf_op jit(solution)/shard_map/ppermute | solution.py:699
  62.7 24.8 %collective-permute-start.29 = (bf16[1,128,256]{2,1,0:T(8,128)(2,1)S(1)}, bf16[1,128,256]{2,1,0:T(8,128)(2,1)S(1)}, u32[]{:S(2)}, u32[]{:S(2)}) collective-permute-start(bf16[1,128,256]{2,1,0:T(8,128)(2,1)S(1)} %get-tuple-element.325), channel_id=1, source_target_pairs={{0,16},{1,17},{2,18},{3,19},{4,20},{5,21},{6,22},{7,23},{8,24},{9,... | collective-permute-start | bytes 196616 | tf_op jit(solution)/shard_map/ppermute | solution.py:699
  63.9 9.0 %collective-permute-start.15 = (bf16[1,256,256]{2,1,0:T(8,128)(2,1)S(1)}, bf16[1,256,256]{2,1,0:T(8,128)(2,1)S(1)}, u32[]{:S(2)}, u32[]{:S(2)}) collective-permute-start(bf16[1,256,256]{2,1,0:T(8,128)(2,1)S(1)} %get-tuple-element.329), channel_id=1, source_target_pairs={{0,8},{1,17},{2,10},{3,19},{4,12},{5,21},{6,14},{7,23},{8,0},{9,25... | collective-permute-start | bytes 393224 | tf_op jit(solution)/shard_map/ppermute | solution.py:699
  68.4 12.5 %collective-permute-start.25 = (bf16[2,128,256]{2,1,0:T(8,128)(2,1)S(1)}, bf16[2,128,256]{2,1,0:T(8,128)(2,1)S(1)}, u32[]{:S(2)}, u32[]{:S(2)}) collective-permute-start(bf16[2,128,256]{2,1,0:T(8,128)(2,1)S(1)} %get-tuple-element.336), channel_id=1, source_target_pairs={{0,8},{1,5},{2,10},{3,7},{4,12},{5,1},{6,14},{7,3},{8,0},{9,13},{1... | collective-permute-start | bytes 393224 | tf_op jit(solution)/shard_map/ppermute | solution.py:699
  68.5 6.4 %collective-permute-start.22 = (bf16[1,128,256]{2,1,0:T(8,128)(2,1)S(1)}, bf16[1,128,256]{2,1,0:T(8,128)(2,1)S(1)}, u32[]{:S(2)}, u32[]{:S(2)}) collective-permute-start(bf16[1,128,256]{2,1,0:T(8,128)(2,1)S(1)} %get-tuple-element.339), channel_id=1, source_target_pairs={{0,2},{1,17},{2,0},{3,19},{4,6},{5,21},{6,4},{7,23},{8,10},{9,25},... | collective-permute-start | bytes 196616 | tf_op jit(solution)/shard_map/ppermute | solution.py:699
  71.8 6.7 %collective-permute-start.21 = (bf16[4,144,256]{2,1,0:T(8,128)(2,1)S(1)}, bf16[4,144,256]{2,1,0:T(8,128)(2,1)S(1)}, u32[]{:S(2)}, u32[]{:S(2)}) collective-permute-start(bf16[4,144,256]{2,1,0:T(8,128)(2,1)S(1)} %get-tuple-element.342), channel_id=1, source_target_pairs={{0,2},{1,17},{2,0},{3,19},{4,6},{5,21},{6,4},{7,23},{8,10},{9,25},... | collective-permute-start | bytes 884744 | tf_op jit(solution)/shard_map/ppermute | solution.py:699
  72.9 9.3 %collective-permute-start.24 = (bf16[2,128,256]{2,1,0:T(8,128)(2,1)S(1)}, bf16[2,128,256]{2,1,0:T(8,128)(2,1)S(1)}, u32[]{:S(2)}, u32[]{:S(2)}) collective-permute-start(bf16[2,128,256]{2,1,0:T(8,128)(2,1)S(1)} %get-tuple-element.345), channel_id=1, source_target_pairs={{0,8},{1,5},{2,10},{3,7},{4,12},{5,1},{6,14},{7,3},{8,0},{9,13},{1... | collective-permute-start | bytes 393224 | tf_op jit(solution)/shard_map/ppermute | solution.py:699
  74.9 11.8 %collective-permute-start.20 = (bf16[2,128,512]{2,1,0:T(8,128)(2,1)S(1)}, bf16[2,128,512]{2,1,0:T(8,128)(2,1)S(1)}, u32[]{:S(2)}, u32[]{:S(2)}) collective-permute-start(bf16[2,128,512]{2,1,0:T(8,128)(2,1)S(1)} %get-tuple-element.349), channel_id=1, source_target_pairs={{0,16},{16,0},{1,17},{17,1},{2,18},{18,2},{3,19},{19,3},{4,20},{20... | collective-permute-start | bytes 786440 | tf_op jit(solution)/shard_map/ppermute | solution.py:649
  80.9 8.0 %collective-permute-start.27 = (bf16[1,128,256]{2,1,0:T(8,128)(2,1)S(1)}, bf16[1,128,256]{2,1,0:T(8,128)(2,1)S(1)}, u32[]{:S(2)}, u32[]{:S(2)}) collective-permute-start(bf16[1,128,256]{2,1,0:T(8,128)(2,1)S(1)} %get-tuple-element.363), channel_id=1, source_target_pairs={{0,16},{1,9},{2,18},{3,11},{4,20},{5,13},{6,22},{7,15},{8,24},{9,1... | collective-permute-start | bytes 196616 | tf_op jit(solution)/shard_map/ppermute | solution.py:699
  (6 other events, 29.5 us)
